TPU v7x, 512 devices: a whole 4x8x8 slice. The times are simulated.
512 devices in a mesh: replica: 64 (over x, z, y_hi), tensor: 8 (over y_lo, core).
Axes of the slice: x: 4, y: 8 (y_hi: 2, y_lo: 4; y = y_hi * 4 + y_lo), z: 8, core: 2. Of those that a mesh axis runs over, the one named last changes fastest.
Arguments:
- x_one: bfloat16 [32768, 5120], P('replica', 'tensor'), may hold values from -6 to 6
- x_two: bfloat16 [32768, 5120], P('replica', 'tensor'), may hold values from -6 to 6
- norm_one: float32 [5120], replicated, may hold values from 0.1 to 1.9
- norm_two: float32 [5120], replicated, may hold values from 0.1 to 1.9
- key_gain_one: float32 [128], replicated, may hold values from 0.1 to 1.9
- key_gain_two: float32 [128], replicated, may hold values from 0.1 to 1.9
- wk_one: bfloat16 [5120, 1024], P('replica', 'tensor'), may hold values from -0.078125 to 0.078125
- wv_one: bfloat16 [5120, 1024], P('replica', 'tensor'), may hold values from -0.078125 to 0.078125
- wk_two: bfloat16 [5120, 1024], P('replica', 'tensor'), may hold values from -0.078125 to 0.078125
- wv_two: bfloat16 [5120, 1024], P('replica', 'tensor'), may hold values from -0.078125 to 0.078125
- lengths: int32 [64], P('replica'), may hold values from 1 to 512, 24576 in all
- new_flag: int32 [64], P('replica'), may hold values from 0 to 1, as said below
- partner: int32 [64], P('replica'), may hold values from 0 to 63, as said below
Outputs:
- keys_one: bfloat16 [32768, 1024], P('replica', 'tensor')
- values_one: bfloat16 [32768, 1024], P('replica', 'tensor')
- keys_two: bfloat16 [65536, 1024], P('replica', 'tensor')
- values_two: bfloat16 [65536, 1024], P('replica', 'tensor')
Inputs may be any that keep to these rules, and one draw needn't show every extreme that they name: For every slot s exactly one of new_flag[s] and new_flag[partner[s]] is 1; the first and the last slot of every aligned block of 8 slots have new_flag 0. partner[s] = s XOR 2**b, where b is 0, 1 or 2 and is the same for all slots of an aligned block of 8 slots; partner[partner[s]] = s.
All inputs are finite; a program needn't handle non-finite values. No bound on the sum of `lengths` on one device may be relied on, other than what follows from the above.
Results may differ from a plain program's by a relative error of at most 0.0049.
Values may be sent and summed in bfloat16 or wider, within the bound.
No kernel may reach another device: no remote copies, remote signals or barrier semaphores. Data moves between devices by JAX's collectives and lax.ppermute only.
A program may use at most 64 MiB of HBM per device.

v0:
```python
import jax
import jax.numpy as jnp
from jax import lax
from jax.sharding import PartitionSpec as P

HD = 128


def swapped(value, axis, apart):
    mask = 2**apart
    pairs = [(source, source ^ mask) for source in range(lax.axis_size(axis))]
    return lax.ppermute(value, axis, pairs)


def normalize(full, gain):
    values = full.astype(jnp.float32)
    scale = lax.rsqrt(jnp.mean(values * values, axis=-1, keepdims=True) + 1e-06)
    return (values * scale * gain).astype(jnp.bfloat16)


def project_layer(normed, w_key, w_value, key_gain):
    raw_key = jnp.dot(
        normed,
        lax.all_gather(w_key, "replica", axis=0, tiled=True),
        preferred_element_type=jnp.float32,
    )
    value = jnp.dot(
        normed,
        lax.all_gather(w_value, "replica", axis=0, tiled=True),
        preferred_element_type=jnp.float32,
    )
    heads = raw_key.reshape(raw_key.shape[0], -1, HD)
    heads = heads * lax.rsqrt(jnp.mean(heads * heads, axis=-1, keepdims=True) + 1e-06) * key_gain
    return (heads.reshape(raw_key.shape).astype(jnp.bfloat16), value.astype(jnp.bfloat16))


def on_device(
    x_one,
    x_two,
    norm_one,
    norm_two,
    key_gain_one,
    key_gain_two,
    wk_one,
    wv_one,
    wk_two,
    wv_two,
    lengths,
    new_flag,
    partner,
):
    rows = x_one.shape[0]
    live_mask = (jnp.arange(rows, dtype=jnp.int32) < lengths[0])[:, None]
    live_one = jnp.where(live_mask, x_one, jnp.zeros_like(x_one))
    live_two = jnp.where(live_mask, x_two, jnp.zeros_like(x_two))
    pair_bit = jnp.bitwise_xor(partner[0], lax.axis_index("replica"))
    is_old = new_flag[0] == 0
    full_one = lax.all_gather(live_one, "tensor", axis=1, tiled=True)
    keys_one, values_one = project_layer(
        normalize(full_one, norm_one), wk_one, wv_one, key_gain_one
    )
    received = jnp.zeros_like(live_two)
    for bit in range(3):
        arrived = swapped(live_two, "replica", bit)
        received = jnp.where(pair_bit == 1 << bit, arrived, received)
    full_own, full_other = (
        lax.all_gather(live_two, "tensor", axis=1, tiled=True),
        lax.all_gather(received, "tensor", axis=1, tiled=True),
    )
    stacked = jnp.concatenate([full_own, full_other], axis=0)
    key_both, value_both = project_layer(normalize(stacked, norm_two), wk_two, wv_two, key_gain_two)
    keys_two = jnp.where(is_old, key_both, jnp.zeros_like(key_both))
    values_two = jnp.where(is_old, value_both, jnp.zeros_like(value_both))
    return (keys_one, values_one, keys_two, values_two)


def solution(mesh):
    in_specs = (
        P("replica", "tensor"),
        P("replica", "tensor"),
        P(),
        P(),
        P(),
        P(),
        P("replica", "tensor"),
        P("replica", "tensor"),
        P("replica", "tensor"),
        P("replica", "tensor"),
        P("replica"),
        P("replica"),
        P("replica"),
    )
    out_specs = (
        P("replica", "tensor"),
        P("replica", "tensor"),
        P("replica", "tensor"),
        P("replica", "tensor"),
    )
    return jax.shard_map(
        on_device, mesh=mesh, in_specs=in_specs, out_specs=out_specs, check_vma=False
    )
```

profile of v0, /device:TPU:1, one launch (start us, length us, event | category | flops | bytes accessed | tf_op | source)
XLA Modules:
  0.0 769.8 jit_solution(2615674043355329367)
XLA Ops:
  7.9 2.6 broadcast_select_fusion
  10.5 0.0 all-gather.10.cloned.1.call-start
  10.6 0.7 all-gather.10.cloned.1.call-update
  11.3 0.7 all-gather.12.cloned.1.call-update
  12.0 0.5 all-gather.14.cloned.1.call-update
  12.6 6.6 collective-permute-start
  19.3 4.0 collective-permute-start.1
  23.3 7.5 collective-permute-start.2
  31.4 15.6 %collective-permute-done = bf16[512,640]{1,0:T(8,128)(2,1)S(1)} collective-permute-done((bf16[512,640]{1,0:T(8,128)(2,1)}, bf16[512,640]{1,0:T(8,128)(2,1)S(1)}, u32[]{:S(2)}, u32[]{:S(2)}) %collective-permute-start) | collective-permute-done | bytes 655392 | tf_op jit(solution)/shard_map/ppermute | solution.py:12
  47.0 23.9 %collective-permute-done.2 = bf16[512,640]{1,0:T(8,128)(2,1)S(1)} collective-permute-done((bf16[512,640]{1,0:T(8,128)(2,1)}, bf16[512,640]{1,0:T(8,128)(2,1)S(1)}, u32[]{:S(2)}, u32[]{:S(2)}) %collective-permute-start.2) | collective-permute-done | bytes 655392 | tf_op jit(solution)/shard_map/ppermute | solution.py:12
  70.8 0.9 select_select_fusion
  71.9 0.5 all-gather.18.cloned.1.call-update
  72.5 0.7 all-gather.20.cloned.1.call-update
  73.8 36.3 %all-gather.8.cloned.1.call-done = bf16[512,5120]{1,0:T(8,128)(2,1)} async-done(((bf16[512,640]{1,0:T(8,128)(2,1)}), bf16[512,5120]{1,0:T(8,128)(2,1)}) %all-gather.8.cloned.1.call-update) | async-done | bytes 5242896 | tf_op jit(solution)/shard_map/all_gather | solution.py:58
  110.1 3.6 fusion.3
  113.7 123.5 %all-gather.10.cloned.1.call-done = bf16[5120,128]{1,0:T(8,128)(2,1)} async-done(((bf16[80,128]{1,0:T(8,128)(2,1)}), bf16[5120,128]{1,0:T(8,128)(2,1)}) %all-gather.10.cloned.1.call-update) | async-done | bytes 1310736 | tf_op jit(solution)/shard_map/all_gather | solution.py:24
  237.2 4.8 multiply_reduce_fusion.1
  242.1 0.1 multiply_convert_fusion.1
  242.2 0.8 copy.18
  242.9 121.5 %all-gather.12.cloned.1.call-done = bf16[5120,128]{1,0:T(8,128)(2,1)} async-done(((bf16[80,128]{1,0:T(8,128)(2,1)}), bf16[5120,128]{1,0:T(8,128)(2,1)}) %all-gather.12.cloned.1.call-update) | async-done | bytes 1310736 | tf_op jit(solution)/shard_map/all_gather | solution.py:29
  364.5 5.1 fusion.10
  369.6 61.1 %all-gather.14.cloned.1.call-done = bf16[512,5120]{1,0:T(8,128)(2,1)} async-done(((bf16[512,640]{1,0:T(8,128)(2,1)}), bf16[512,5120]{1,0:T(8,128)(2,1)}) %all-gather.14.cloned.1.call-update) | async-done | bytes 5242896 | tf_op jit(solution)/shard_map/all_gather | solution.py:67
  430.7 67.7 %all-gather.16.cloned.1.call-done = bf16[512,5120]{1,0:T(8,128)(2,1)} async-done(((bf16[512,640]{1,0:T(8,128)(2,1)}), bf16[512,5120]{1,0:T(8,128)(2,1)}) %all-gather.16.cloned.1.call-update) | async-done | bytes 5242896 | tf_op jit(solution)/shard_map/all_gather | solution.py:68
  498.4 7.7 fusion
  506.1 6.0 fusion.2
  512.1 114.9 %all-gather.18.cloned.1.call-done = bf16[5120,128]{1,0:T(8,128)(2,1)} async-done(((bf16[80,128]{1,0:T(8,128)(2,1)}), bf16[5120,128]{1,0:T(8,128)(2,1)}) %all-gather.18.cloned.1.call-update) | async-done | bytes 1310736 | tf_op jit(solution)/shard_map/all_gather | solution.py:24
  627.0 7.9 %multiply_reduce_fusion = (f32[1024]{0:T(1024)S(1)}, f32[1024,128]{0,1:T(8,128)S(1)}) fusion(bf16[1024,5120]{1,0:T(8,128)(2,1)} %fusion.2, bf16[5120,128]{1,0:T(8,128)(2,1)} %all-gather.18.cloned.1.call-done), kind=kOutput, calls=%fused_computation.20 | convolution fusion | flops 1342438400 | bytes 12324864 | tf_op jit(solution)/shard_map/dot_general | solution.py:22
  634.9 0.1 fusion.14
  635.0 0.8 copy.19
  635.9 118.3 %all-gather.20.cloned.1.call-done = bf16[5120,128]{1,0:T(8,128)(2,1)} async-done(((bf16[80,128]{1,0:T(8,128)(2,1)}), bf16[5120,128]{1,0:T(8,128)(2,1)}) %all-gather.20.cloned.1.call-update) | async-done | bytes 1310736 | tf_op jit(solution)/shard_map/all_gather | solution.py:29
  754.2 7.9 %fusion.13 = bf16[1024,128]{0,1:T(8,128)(2,1)S(1)} fusion(bf16[1024,5120]{1,0:T(8,128)(2,1)} %fusion.2, bf16[5120,128]{1,0:T(8,128)(2,1)} %all-gather.20.cloned.1.call-done, pred[]{:T(512)} %bitcast.1), kind=kOutput, calls=%fused_computation.15 | convolution fusion | flops 1342439424 | bytes 12058625 | tf_op jit(solution)/shard_map/dot_general | solution.py:27
  762.1 0.8 copy.20
  (26 shorter events, 0.3 us)
Async XLA Ops:
  7.2 230.0 %copy-start.5 = (f32[5120]{0:T(1024)S(1)}, f32[5120]{0:T(1024)}, u32[]{:S(2)}) copy-start(f32[5120]{0:T(1024)} %param.15) | copy-start | bytes 61444
  7.2 103.0 %all-gather.8.cloned.1.call-start = ((), (), s32[]{:S(2)}) async-start(), calls=%async_computation | async-start | bytes 5898240 | tf_op jit(solution)/shard_map/all_gather | solution.py:58
  10.5 226.7 %all-gather.10.cloned.1.call-start = ((), (), s32[]{:S(2)}) async-start(), calls=%async_computation.1 | async-start | bytes 1331200 | tf_op jit(solution)/shard_map/all_gather | solution.py:24
  11.3 353.2 %all-gather.12.cloned.1.call-start = ((), (), s32[]{:S(2)}) async-start(), calls=%async_computation.2 | async-start | bytes 1331200 | tf_op jit(solution)/shard_map/all_gather | solution.py:29
  12.0 418.7 %all-gather.14.cloned.1.call-start = ((), (), s32[]{:S(2)}) async-start(), calls=%async_computation.3 | async-start | bytes 5898240 | tf_op jit(solution)/shard_map/all_gather | solution.py:67
  12.6 485.8 %all-gather.16.cloned.1.call-start = ((), (), s32[]{:S(2)}) async-start(), calls=%async_computation.4 | async-start | bytes 5898240 | tf_op jit(solution)/shard_map/all_gather | solution.py:68
  12.6 34.4 %collective-permute-start = (bf16[512,640]{1,0:T(8,128)(2,1)}, bf16[512,640]{1,0:T(8,128)(2,1)S(1)}, u32[]{:S(2)}, u32[]{:S(2)}) collective-permute-start(bf16[512,640]{1,0:T(8,128)(2,1)} %get-tuple-element.8), channel_id=1, source_target_pairs={{0,32},{8,40},{16,48},{24,56},{32,0},{40,8},{48,16},{56,24},{64,96... | collective-permute-start | bytes 1966088 | tf_op jit(solution)/shard_map/ppermute | solution.py:12
  19.3 27.7 %collective-permute-start.1 = (bf16[512,640]{1,0:T(8,128)(2,1)}, bf16[512,640]{1,0:T(8,128)(2,1)S(1)}, u32[]{:S(2)}, u32[]{:S(2)}) collective-permute-start(bf16[512,640]{1,0:T(8,128)(2,1)} %get-tuple-element.8), channel_id=1, source_target_pairs={{0,16},{8,24},{16,0},{24,8},{32,48},{40,56},{48,32},{56,40},{64,80... | collective-permute-start | bytes 1966088 | tf_op jit(solution)/shard_map/ppermute | solution.py:12
  23.3 47.6 %collective-permute-start.2 = (bf16[512,640]{1,0:T(8,128)(2,1)}, bf16[512,640]{1,0:T(8,128)(2,1)S(1)}, u32[]{:S(2)}, u32[]{:S(2)}) collective-permute-start(bf16[512,640]{1,0:T(8,128)(2,1)} %get-tuple-element.8), channel_id=1, source_target_pairs={{0,8},{8,0},{16,24},{24,16},{32,40},{40,32},{48,56},{56,48},{64,72... | collective-permute-start | bytes 1966088 | tf_op jit(solution)/shard_map/ppermute | solution.py:12
  71.8 170.3 %copy-start.3 = (f32[128]{0:T(128)S(1)}, f32[128]{0:T(128)}, u32[]{:S(2)}) copy-start(f32[128]{0:T(128)} %param.17) | copy-start | bytes 1540
  71.8 555.2 %all-gather.18.cloned.1.call-start = ((), (), s32[]{:S(2)}) async-start(), calls=%async_computation.5 | async-start | bytes 1331200 | tf_op jit(solution)/shard_map/all_gather | solution.py:24
  72.4 681.8 %all-gather.20.cloned.1.call-start = ((), (), s32[]{:S(2)}) async-start(), calls=%async_computation.6 | async-start | bytes 1331200 | tf_op jit(solution)/shard_map/all_gather | solution.py:29
  242.9 263.1 %copy-start.2 = (f32[5120]{0:T(1024)S(1)}, f32[5120]{0:T(1024)}, u32[]{:S(2)}) copy-start(f32[5120]{0:T(1024)} %param.16) | copy-start | bytes 61444
  498.4 7.7 copy-start
  498.4 7.7 copy-start.1
  512.1 122.9 %copy-start.4 = (f32[128]{0:T(128)S(1)}, f32[128]{0:T(128)}, u32[]{:S(2)}) copy-start(f32[128]{0:T(128)} %param.18) | copy-start | bytes 1540
Sparse Core Ops, SparseCore 0:
  10.6 99.4 all-gather.7
  114.5 122.6 all-gather.9
  241.6 122.8 all-gather.11
  366.4 64.2 all-gather.13
  432.6 65.7 all-gather.15
  502.6 124.3 all-gather.17
  631.3 122.8 all-gather.19
where the time goes:
time: 774 us; the launch traced here: 770 us
  waiting for transfers between devices  686 us (89%)
  matrix products  25.7 us (3%)
  other arithmetic  21 us (3%)
  starting transfers between devices  18.4 us (2%)
  between operations  16.2 us (2%)
    all_gather x2, waiting for transfers between devices, project_layer(): lax.all_gather(w_value, 'replica', axis=0, tiled=True)  240 us
    all_gather x2, waiting for transfers between devices, project_layer(): lax.all_gather(w_key, 'replica', axis=0, tiled=True)  238 us
    all_gather x1, waiting for transfers between devices, on_device(): lax.all_gather(received, 'tensor', axis=1, tiled=True)  67.7 us
    all_gather x1, waiting for transfers between devices, on_device(): lax.all_gather(live_two, 'tensor', axis=1, tiled=True)  61.1 us
    ppermute x3, waiting for transfers between devices, swapped(): return lax.ppermute(value, axis, pairs)  39.5 us
    all_gather x1, waiting for transfers between devices, on_device(): full_one = lax.all_gather(live_one, 'tensor', axis=1, tiled=True)  36.3 us
    ppermute x3, starting transfers between devices, swapped(): return lax.ppermute(value, axis, pairs)  18.1 us
  transfers between devices with their start and end apart: 10, of which 9 were waited for; matrix products, arithmetic and copies ran while one was open for 5% of the time, Pallas kernels for 0%

commit v1 on v0

v1 whole, which is shorter than its diff:
```python
import functools

import jax
import jax.numpy as jnp
from jax import lax
from jax.experimental import pallas as pl
from jax.experimental.pallas import tpu as pltpu
from jax.sharding import Mesh
from jax.sharding import PartitionSpec as P

HD = 128
EPS = 1e-06
TILE = 128
AXES = ("x", "z", "h", "l", "c")
SIZES = (4, 8, 2, 4, 2)


def move(value, axes, place):
    sizes = [SIZES[AXES.index(axis)] for axis in axes]
    total = 1
    for size in sizes:
        total *= size

    def coordinates(index):
        found = []
        for size in reversed(sizes):
            found.append(index % size)
            index //= size
        return found[::-1]

    def flat(at):
        index = 0
        for size, one in zip(sizes, at):
            index = index * size + one
        return index

    pairs = [(index, flat(place(*coordinates(index)))) for index in range(total)]
    return lax.ppermute(value, axes, pairs)


def head_norm(raw_key, key_gain):
    mean = jnp.mean(raw_key * raw_key, axis=-1, keepdims=True)
    return raw_key * lax.rsqrt(mean + EPS) * key_gain


def live_scale(squares, width, length, first):
    rows = first + lax.broadcasted_iota(jnp.int32, squares.shape, 0)
    scale = lax.rsqrt(squares / width + EPS)
    return jnp.where(rows < length, scale, 0.0)


def block_of(w_ref, row, core):
    w = w_ref[pl.ds(core * 4, 4), row, 0]
    return w.reshape(w.shape[0] * w.shape[1], w.shape[2])


def two_kernel(place, *refs):
    x_refs, (w_ref, gain_ref, out_ref) = refs[:8], refs[8:]
    l, c, length = place[0], place[1], place[2]
    raw = jnp.zeros((TILE, 2 * HD), jnp.float32)
    squares = jnp.zeros((TILE, 1), jnp.float32)
    for i, x_ref in enumerate(x_refs):
        x = x_ref[...]
        w = block_of(w_ref, l ^ (i % 4), c ^ (i // 4))
        raw += jnp.dot(x, w, preferred_element_type=jnp.float32)
        wide = x.astype(jnp.float32)
        squares += jnp.sum(wide * wide, axis=-1, keepdims=True)
    raw *= live_scale(squares, 8 * x_refs[0].shape[1], length, pl.program_id(0) * TILE)
    out_ref[:, :HD] = head_norm(raw[:, :HD], gain_ref[...]).astype(out_ref.dtype)
    out_ref[:, HD:] = raw[:, HD:].astype(out_ref.dtype)


def one_kernel(place, *refs):
    x_refs, (w_ref, own_ref, other_ref, squares_ref) = refs[:4], refs[4:]
    l, c = place[0], place[1]
    mine = jnp.zeros((TILE, 2 * HD), jnp.float32)
    theirs = jnp.zeros((TILE, 2 * HD), jnp.float32)
    squares = jnp.zeros((TILE, 1), jnp.float32)
    for i, x_ref in enumerate(x_refs):
        x = x_ref[...]
        own = block_of(w_ref, l ^ (i % 2), c ^ (i // 2))
        other = block_of(w_ref, l ^ (2 + i % 2), c ^ (i // 2))
        mine += jnp.dot(x, own, preferred_element_type=jnp.float32)
        theirs += jnp.dot(x, other, preferred_element_type=jnp.float32)
        wide = x.astype(jnp.float32)
        squares += jnp.sum(wide * wide, axis=-1, keepdims=True)
    own_ref[...] = mine
    other_ref[...] = theirs.astype(other_ref.dtype)
    squares_ref[...] = jnp.broadcast_to(squares, (TILE, HD))


def finish_kernel(width, place, own_ref, other_ref, mine_ref, theirs_ref, gain_ref, key_ref, value_ref):
    raw = own_ref[...] + other_ref[...].astype(jnp.float32)
    squares = mine_ref[:, :1] + theirs_ref[:, :1]
    raw *= live_scale(squares, width, place[2], 0)
    key_ref[...] = head_norm(raw[:, :HD], gain_ref[...]).astype(key_ref.dtype)
    value_ref[...] = raw[:, HD:].astype(value_ref.dtype)


def tiled(columns):
    return pl.BlockSpec((TILE, columns), lambda step: (step, 0))


VMEM = pl.BlockSpec(memory_space=pltpu.VMEM)
SMEM = pl.BlockSpec(memory_space=pltpu.SMEM)
PARAMS = pltpu.CompilerParams(vmem_limit_bytes=40 * 1024 * 1024)


def on_device(
    x_one,
    x_two,
    norm_one,
    norm_two,
    key_gain_one,
    key_gain_two,
    wk_one,
    wv_one,
    wk_two,
    wv_two,
    lengths,
    new_flag,
    partner,
):
    rows, width = x_one.shape
    depth = wk_one.shape[0]
    x, z, h, l, c = [lax.axis_index(axis) for axis in AXES]
    slot = (x * 8 + z) * 2 + h
    place = jnp.stack([l, c, lengths[0]]).astype(jnp.int32)

    def scaled(gain, w_key, w_value):
        mine = lax.dynamic_slice(gain, (slot * depth,), (depth,))[:, None]
        both = jnp.concatenate([w_key, w_value], axis=1).astype(jnp.float32)
        return (both * mine).astype(jnp.bfloat16)

    w_one = scaled(norm_one, wk_one, wv_one)
    w_two = scaled(norm_two, wk_two, wv_two)
    one_here = move(w_one, ("x", "l"), lambda x, l: ((l & 2) | (x & 1), (x & 2) | (l & 1)))
    one_there = move(
        w_one, ("x", "h", "l"), lambda x, h, l: ((l & 2) | (x & 1), h ^ 1, (x & 2) | (l & 1))
    )
    two_there = move(w_two, ("h",), lambda h: (h ^ 1,))
    here = jnp.stack([w_two, one_here])
    there = jnp.stack([two_there, one_there])
    weights = jnp.concatenate(
        [jnp.where(h == 0, here, there), jnp.where(h == 0, there, here)], axis=1
    )
    weights = lax.all_gather(weights, "x")
    weights = lax.all_gather(weights, "z")

    def chosen(layer):
        return pl.BlockSpec((8, 4, 1, 2 * depth, 2 * HD), lambda step: (0, 0, layer, 0, 0))

    two_blocks = [x_two] + [
        move(x_two, ("l",), lambda l, apart=apart: (l ^ apart,)) for apart in (1, 2, 3)
    ]
    one_blocks = [x_one, move(x_one, ("l",), lambda l: (l ^ 1,))]
    two_blocks = two_blocks + [move(block, ("c",), lambda c: (c ^ 1,)) for block in two_blocks]
    one_blocks = one_blocks + [move(block, ("c",), lambda c: (c ^ 1,)) for block in one_blocks]

    flops = 2 * rows * 8 * width * 2 * HD
    moved = 8 * rows * width * 2 + 8 * width * 2 * HD * 2
    cost = pl.CostEstimate(flops=flops, bytes_accessed=moved, transcendentals=0)
    both_two = pl.pallas_call(
        two_kernel,
        out_shape=jax.ShapeDtypeStruct((rows, 2 * HD), jnp.bfloat16),
        grid=(rows // TILE,),
        in_specs=[SMEM] + [tiled(width)] * 8 + [chosen(0), VMEM],
        out_specs=tiled(2 * HD),
        compiler_params=PARAMS,
        cost_estimate=cost,
        name="layer_two",
    )(place, *two_blocks, weights, key_gain_two.reshape(1, HD))
    swaps = [
        move(both_two, ("z",), lambda z: (z ^ 2,)),
        move(both_two, ("h",), lambda h: (h ^ 1,)),
        move(both_two, ("z",), lambda z: (z ^ 1,)),
    ]

    own, other, squares = pl.pallas_call(
        one_kernel,
        out_shape=(
            jax.ShapeDtypeStruct((rows, 2 * HD), jnp.float32),
            jax.ShapeDtypeStruct((rows, 2 * HD), jnp.bfloat16),
            jax.ShapeDtypeStruct((rows, HD), jnp.float32),
        ),
        grid=(rows // TILE,),
        in_specs=[SMEM] + [tiled(width)] * 4 + [chosen(1)],
        out_specs=(tiled(2 * HD), tiled(2 * HD), tiled(HD)),
        compiler_params=PARAMS,
        cost_estimate=cost,
        name="layer_one",
    )(place, *one_blocks, weights)
    other = move(other, ("l",), lambda l: (l ^ 2,))
    their_squares = move(squares[:, :1].reshape(-1, HD), ("l",), lambda l: (l ^ 2,))
    their_squares = jnp.broadcast_to(their_squares.reshape(-1, 1), (rows, HD))
    keys_one, values_one = pl.pallas_call(
        functools.partial(finish_kernel, 8 * width),
        out_shape=(jax.ShapeDtypeStruct((rows, HD), jnp.bfloat16),) * 2,
        in_specs=[SMEM] + [VMEM] * 5,
        out_specs=(VMEM, VMEM),
        compiler_params=PARAMS,
        name="finish_one",
    )(place, own, other, squares, their_squares, key_gain_one.reshape(1, HD))

    pair_bit = jnp.bitwise_xor(partner[0], slot)
    received = jnp.where(pair_bit == 4, swaps[0], jnp.where(pair_bit == 1, swaps[1], swaps[2]))
    is_old = new_flag[0] == 0
    held = jnp.concatenate([both_two, received], axis=0)
    held = jnp.where(is_old, held, jnp.zeros_like(held))
    return (keys_one, values_one, held[:, :HD], held[:, HD:])


def solution(mesh):
    split = Mesh(mesh.devices.reshape(SIZES), AXES)
    whole, line = ("x", "z", "h"), ("l", "c")
    sharded = P(whole, line)
    in_specs = (sharded,) * 2 + (P(),) * 4 + (sharded,) * 4 + (P(whole),) * 3
    return jax.shard_map(
        on_device, mesh=split, in_specs=in_specs, out_specs=(sharded,) * 4, check_vma=False
    )
```

time: 774 us -> 175 us (0.23)
  waiting for transfers between devices: 686 us -> 29 us
  starting transfers between devices: 18.4 us -> 89.8 us
  matrix products: 25.7 us -> 0 us
  other arithmetic: 21 us -> 2.73 us
  blocking collectives: 0 us -> 15.5 us
  Pallas kernels: 0 us -> 9.73 us
  local copies, waits for them, and re-layouts: 2.47 us -> 10.4 us
    all_gather x7 -> x1, waiting for transfers between devices: 643 us -> 5.52 us  [on_device(): weights = lax.all_gather(weights, 'z')]
    ppermute x3 -> x18, starting transfers between devices: 18.1 us -> 89.8 us  [move(): return lax.ppermute(value, axes, pairs)]
    dot_general x4 -> x0, matrix products: 25.7 us -> none  [the longest x2 13 us: project_layer(): jnp.dot(normed, lax.all_gather(w_value, 'replica', axis=0, tiled=True), p...]
    ppermute x3 -> x18, waiting for transfers between devices: 39.5 us -> 23.5 us  [move(): return lax.ppermute(value, axes, pairs)]
    all_gather x0 -> x1, blocking collectives: none -> 15.5 us  [on_device(): weights = lax.all_gather(weights, 'x')]
    reduce_sum x2 -> x0, other arithmetic: 11.2 us -> none  [normalize(): scale = lax.rsqrt(jnp.mean(values * values, axis=-1, keepdims=True) + 1e-06)]
    pallas_call x0 -> x3, Pallas kernels: none -> 9.73 us  [the longest x1 4.27 us: on_device(): pl.pallas_call(two_kernel, out_shape=jax.ShapeDtypeStruct((rows, 2 * HD),...]
  transfers between devices with their start and end apart: 10 -> 19, of which waited for: 9 -> 4; matrix products, arithmetic and copies ran while one was open for 5% -> 2% of each run, Pallas kernels for 0% -> 5%
where the time goes in v1:
time: 175 us; the launch traced here: 174 us
  starting transfers between devices  89.8 us (51%)
  waiting for transfers between devices  29 us (17%)
  between operations  16.3 us (9%)
  blocking collectives  15.5 us (9%)
  local copies, waits for them, and re-layouts  10.4 us (6%)
  Pallas kernels  9.73 us (6%)
  other arithmetic  2.73 us (2%)
    ppermute x18, starting transfers between devices, move(): return lax.ppermute(value, axes, pairs)  89.8 us
    ppermute x18, waiting for transfers between devices, move(): return lax.ppermute(value, axes, pairs)  23.5 us
    all_gather x1, blocking collectives, on_device(): weights = lax.all_gather(weights, 'x')  15.5 us
    unnamed x12, local copies, waits for them, and re-layouts  7.8 us
    all_gather x1, waiting for transfers between devices, on_device(): weights = lax.all_gather(weights, 'z')  5.52 us
    pallas_call x1, Pallas kernels, on_device(): pl.pallas_call(two_kernel, out_shape=jax.ShapeDtypeStruct((rows, 2 * HD),...  4.27 us
    pallas_call x1, Pallas kernels, on_device(): pl.pallas_call(one_kernel, out_shape=(jax.ShapeDtypeStruct((rows, 2 * HD)...  4.01 us
  transfers between devices with their start and end apart: 19, of which 4 were waited for; matrix products, arithmetic and copies ran while one was open for 2% of the time, Pallas kernels for 5%

profile of v1, /device:TPU:1, one launch (start us, length us, event | category | flops | bytes accessed | tf_op | source)
XLA Modules:
  0.0 173.6 jit_solution(11902589796233656355)
XLA Ops:
  8.0 0.8 multiply_convert_fusion.1
  9.5 8.3 %collective-permute-start.5 = (bf16[80,256]{1,0:T(8,128)(2,1)S(1)}, bf16[80,256]{1,0:T(8,128)(2,1)S(1)}, u32[]{:S(2)}, u32[]{:S(2)}) collective-permute-start(bf16[80,256]{1,0:T(8,128)(2,1)S(1)} %multiply_convert_fusion.1), channel_id=1, source_target_pairs={{0,8},{2,10},{4,264},{6,266},{8,0},{10,2},{12,256},{14,258},{128,1... | collective-permute-start | bytes 122888 | tf_op jit(solution)/shard_map/ppermute | solution.py:38
  19.4 1.9 %collective-permute-start.4 = (bf16[80,256]{1,0:T(8,128)(2,1)S(1)}, bf16[80,256]{1,0:T(8,128)(2,1)S(1)}, u32[]{:S(2)}, u32[]{:S(2)}) collective-permute-start(bf16[80,256]{1,0:T(8,128)(2,1)S(1)} %multiply_convert_fusion), channel_id=1, source_target_pairs={{0,8},{8,0},{1,9},{9,1},{2,10},{10,2},{3,11},{11,3},{4,12},{12,4},... | collective-permute-start | bytes 122888 | tf_op jit(solution)/shard_map/ppermute | solution.py:38
  21.3 0.8 multiply_convert_fusion.2
  22.2 5.9 %collective-permute-done.4 = bf16[80,256]{1,0:T(8,128)(2,1)S(1)} collective-permute-done((bf16[80,256]{1,0:T(8,128)(2,1)S(1)}, bf16[80,256]{1,0:T(8,128)(2,1)S(1)}, u32[]{:S(2)}, u32[]{:S(2)}) %collective-permute-start.4) | collective-permute-done | bytes 40992 | tf_op jit(solution)/shard_map/ppermute | solution.py:38
  28.1 15.5 %all-gather = bf16[8,160,256]{2,1,0:T(8,128)(2,1)} all-gather(bf16[2,160,256]{2,1,0:T(8,128)(2,1)S(1)} %pad_maximum_fusion), channel_id=2, replica_groups=mesh['x'=4,'z'=8,'h'=2,'l'=4,'c'=2] {'x'}, dimensions={0}, use_global_device_ids=true | all-gather | bytes 819200 | tf_op jit(solution)/shard_map/all_gather | solution.py:147
  43.7 2.3 %collective-permute-start.8 = (bf16[512,640]{1,0:T(8,128)(2,1)}, bf16[512,640]{1,0:T(8,128)(2,1)S(1)}, u32[]{:S(2)}, u32[]{:S(2)}) collective-permute-start(bf16[512,640]{1,0:T(8,128)(2,1)} %refs_0_.3), channel_id=1, source_target_pairs={{0,2},{2,0},{4,6},{6,4},{1,3},{3,1},{5,7},{7,5},{8,10},{10,8},{12,... | collective-permute-start | bytes 1966088 | tf_op jit(solution)/shard_map/ppermute | solution.py:38
  46.0 3.3 %collective-permute-start.9 = (bf16[512,640]{1,0:T(8,128)(2,1)}, bf16[512,640]{1,0:T(8,128)(2,1)S(1)}, u32[]{:S(2)}, u32[]{:S(2)}) collective-permute-start(bf16[512,640]{1,0:T(8,128)(2,1)} %refs_0_.3), channel_id=1, source_target_pairs={{0,4},{2,6},{4,0},{6,2},{1,5},{3,7},{5,1},{7,3},{8,12},{10,14},{12... | collective-permute-start | bytes 1966088 | tf_op jit(solution)/shard_map/ppermute | solution.py:38
  49.3 3.6 %collective-permute-start.10 = (bf16[512,640]{1,0:T(8,128)(2,1)}, bf16[512,640]{1,0:T(8,128)(2,1)S(1)}, u32[]{:S(2)}, u32[]{:S(2)}) collective-permute-start(bf16[512,640]{1,0:T(8,128)(2,1)} %refs_0_.3), channel_id=1, source_target_pairs={{0,6},{2,4},{4,2},{6,0},{1,7},{3,5},{5,3},{7,1},{8,14},{10,12},{12... | collective-permute-start | bytes 1966088 | tf_op jit(solution)/shard_map/ppermute | solution.py:38
  53.0 8.3 %collective-permute-start.11 = (bf16[512,640]{1,0:T(8,128)(2,1)}, bf16[512,640]{1,0:T(8,128)(2,1)S(1)}, u32[]{:S(2)}, u32[]{:S(2)}) collective-permute-start(bf16[512,640]{1,0:T(8,128)(2,1)} %refs_0_.3), channel_id=1, source_target_pairs={{0,1},{1,0},{2,3},{3,2},{4,5},{5,4},{6,7},{7,6},{8,9},{9,8},{10,11... | collective-permute-start | bytes 1966088 | tf_op jit(solution)/shard_map/ppermute | solution.py:38
  61.3 1.9 %collective-permute-start = (bf16[512,640]{1,0:T(8,128)(2,1)}, bf16[512,640]{1,0:T(8,128)(2,1)}, u32[]{:S(2)}, u32[]{:S(2)}) collective-permute-start(bf16[512,640]{1,0:T(8,128)(2,1)} %refs_0_.2), channel_id=1, source_target_pairs={{0,2},{2,0},{4,6},{6,4},{1,3},{3,1},{5,7},{7,5},{8,10},{10,8},{12,... | collective-permute-start | bytes 1966088 | tf_op jit(solution)/shard_map/ppermute | solution.py:38
  63.2 5.9 %collective-permute-done.8.refs_1_ = bf16[512,640]{1,0:T(8,128)(2,1)S(1)} collective-permute-done((bf16[512,640]{1,0:T(8,128)(2,1)}, bf16[512,640]{1,0:T(8,128)(2,1)S(1)}, u32[]{:S(2)}, u32[]{:S(2)}) %collective-permute-start.8) | collective-permute-done | bytes 655392 | tf_op jit(solution)/shard_map/ppermute | solution.py:38
  69.1 11.8 %collective-permute-start.12 = (bf16[512,640]{1,0:T(8,128)(2,1)S(1)}, bf16[512,640]{1,0:T(8,128)(2,1)S(1)}, u32[]{:S(2)}, u32[]{:S(2)}) collective-permute-start(bf16[512,640]{1,0:T(8,128)(2,1)S(1)} %collective-permute-done.8.refs_1_), channel_id=1, source_target_pairs={{0,1},{1,0},{2,3},{3,2},{4,5},{5,4},{6,7},{7,6},{8,9},{9,8},{10,11... | collective-permute-start | bytes 1966088 | tf_op jit(solution)/shard_map/ppermute | solution.py:38
  80.9 21.6 %collective-permute-start.13 = (bf16[512,640]{1,0:T(8,128)(2,1)S(1)}, bf16[512,640]{1,0:T(8,128)(2,1)}, u32[]{:S(2)}, u32[]{:S(2)}) collective-permute-start(bf16[512,640]{1,0:T(8,128)(2,1)S(1)} %collective-permute-done.9.refs_2_), channel_id=1, source_target_pairs={{0,1},{1,0},{2,3},{3,2},{4,5},{5,4},{6,7},{7,6},{8,9},{9,8},{10,11... | collective-permute-start | bytes 1966088 | tf_op jit(solution)/shard_map/ppermute | solution.py:38
  102.5 1.9 %collective-permute-start.14 = (bf16[512,640]{1,0:T(8,128)(2,1)S(1)}, bf16[512,640]{1,0:T(8,128)(2,1)}, u32[]{:S(2)}, u32[]{:S(2)}) collective-permute-start(bf16[512,640]{1,0:T(8,128)(2,1)S(1)} %collective-permute-done.10.refs_3_), channel_id=1, source_target_pairs={{0,1},{1,0},{2,3},{3,2},{4,5},{5,4},{6,7},{7,6},{8,9},{9,8},{10,11... | collective-permute-start | bytes 1966088 | tf_op jit(solution)/shard_map/ppermute | solution.py:38
  104.5 2.4 %collective-permute-start.1 = (bf16[512,640]{1,0:T(8,128)(2,1)}, bf16[512,640]{1,0:T(8,128)(2,1)}, u32[]{:S(2)}, u32[]{:S(2)}) collective-permute-start(bf16[512,640]{1,0:T(8,128)(2,1)} %refs_0_.2), channel_id=1, source_target_pairs={{0,1},{1,0},{2,3},{3,2},{4,5},{5,4},{6,7},{7,6},{8,9},{9,8},{10,11... | collective-permute-start | bytes 1966088 | tf_op jit(solution)/shard_map/ppermute | solution.py:38
  106.9 1.9 %collective-permute-start.2 = (bf16[512,640]{1,0:T(8,128)(2,1)}, bf16[512,640]{1,0:T(8,128)(2,1)}, u32[]{:S(2)}, u32[]{:S(2)}) collective-permute-start(bf16[512,640]{1,0:T(8,128)(2,1)} %collective-permute-done.refs_1_), channel_id=1, source_target_pairs={{0,1},{1,0},{2,3},{3,2},{4,5},{5,4},{6,7},{7,6},{8,9},{9,8},{10,11... | collective-permute-start | bytes 1966088 | tf_op jit(solution)/shard_map/ppermute | solution.py:38
  109.6 5.5 %all-gather.4.cloned.1.call-done = bf16[32,2,160,256]{3,2,1,0:T(8,128)(2,1)} async-done(((bf16[4,2,160,256]{3,2,1,0:T(8,128)(2,1)}), bf16[32,2,160,256]{3,2,1,0:T(8,128)(2,1)}) %all-gather.4.cloned.1.call-update) | async-done | bytes 5242896 | tf_op jit(solution)/shard_map/all_gather | solution.py:148
  115.1 2.5 %copy-done = bf16[32,2,160,256]{3,2,1,0:T(8,128)(2,1)S(1)} copy-done((bf16[32,2,160,256]{3,2,1,0:T(8,128)(2,1)S(1)}, bf16[32,2,160,256]{3,2,1,0:T(8,128)(2,1)}, u32[]{:S(2)}) %copy-start) | copy-done | bytes 5242904
  117.6 1.1 copy-done.2
  119.3 4.3 %layer_two.1 = bf16[512,256]{1,0:T(8,128)(2,1)S(1)} custom-call(s32[3]{0:T(128)S(1)} %pad_add_fusion.place, bf16[512,640]{1,0:T(8,128)(2,1)S(1)} %copy-done.2, bf16[512,640]{1,0:T(8,128)(2,1)S(1)} %collective-permute-done.8.refs_1_, bf16[512,640]{1,0:T(8,128)(2,1)S(1)} %collective-permute-done.9.refs_2_, ...), custom_call_target="tpu_custom_call" | custom-call | flops 1342177280 | bytes 7864320 | tf_op jit(solution)/shard_map/layer_two/pallas_call | solution.py:163
  123.6 2.0 %collective-permute-start.15 = (bf16[512,256]{1,0:T(8,128)(2,1)S(1)}, bf16[512,256]{1,0:T(8,128)(2,1)S(1)}, u32[]{:S(2)}, u32[]{:S(2)}) collective-permute-start(bf16[512,256]{1,0:T(8,128)(2,1)S(1)} %layer_two.1), channel_id=1, source_target_pairs={{0,32},{16,48},{32,0},{48,16},{64,96},{80,112},{96,64},{112,80},{1... | collective-permute-start | bytes 786440 | tf_op jit(solution)/shard_map/ppermute | solution.py:38
  125.6 7.1 %collective-permute-start.16 = (bf16[512,256]{1,0:T(8,128)(2,1)S(1)}, bf16[512,256]{1,0:T(8,128)(2,1)S(1)}, u32[]{:S(2)}, u32[]{:S(2)}) collective-permute-start(bf16[512,256]{1,0:T(8,128)(2,1)S(1)} %layer_two.1), channel_id=1, source_target_pairs={{0,8},{8,0},{1,9},{9,1},{2,10},{10,2},{3,11},{11,3},{4,12},{12,4},... | collective-permute-start | bytes 786440 | tf_op jit(solution)/shard_map/ppermute | solution.py:38
  132.8 4.5 %collective-permute-start.17 = (bf16[512,256]{1,0:T(8,128)(2,1)S(1)}, bf16[512,256]{1,0:T(8,128)(2,1)S(1)}, u32[]{:S(2)}, u32[]{:S(2)}) collective-permute-start(bf16[512,256]{1,0:T(8,128)(2,1)S(1)} %layer_two.1), channel_id=1, source_target_pairs={{0,16},{16,0},{32,48},{48,32},{64,80},{80,64},{96,112},{112,96},{1... | collective-permute-start | bytes 786440 | tf_op jit(solution)/shard_map/ppermute | solution.py:38
  138.6 2.5 %copy-done.1 = bf16[32,2,160,256]{3,2,1,0:T(8,128)(2,1)S(1)} copy-done((bf16[32,2,160,256]{3,2,1,0:T(8,128)(2,1)S(1)}, bf16[32,2,160,256]{3,2,1,0:T(8,128)(2,1)}, u32[]{:S(2)}) %copy-start.1) | copy-done | bytes 5242904
  141.0 1.1 copy-done.3
  142.1 4.0 %layer_one.1 = (f32[512,256]{1,0:T(8,128)S(1)}, bf16[512,256]{1,0:T(8,128)(2,1)S(1)}, f32[512,128]{1,0:T(8,128)S(1)}) custom-call(s32[3]{0:T(128)S(1)} %pad_add_fusion.place, bf16[512,640]{1,0:T(8,128)(2,1)S(1)} %copy-done.3, bf16[512,640]{1,0:T(8,128)(2,1)} %collective-permute-done.refs_1_, bf16[512,640]{1,0:T(8,128)(2,1)} %collective-permute-done.1.refs_2_, ...), custom_call_target="tpu_custom_call" | custom-call | flops 1342177280 | bytes 7864320 | tf_op jit(solution)/shard_map/layer_one/pallas_call | solution.py:179
  146.3 3.3 %collective-permute-start.7 = (f32[4,128]{1,0:T(4,128)S(1)}, f32[4,128]{1,0:T(4,128)S(1)}, u32[]{:S(2)}, u32[]{:S(2)}) collective-permute-start(f32[4,128]{1,0:T(4,128)S(1)} %bitcast.27), channel_id=1, source_target_pairs={{0,4},{2,6},{4,0},{6,2},{1,5},{3,7},{5,1},{7,3},{8,12},{10,14},{12... | collective-permute-start | bytes 6152 | tf_op jit(solution)/shard_map/ppermute | solution.py:38
  149.6 2.9 %collective-permute-start.6 = (bf16[512,256]{1,0:T(8,128)(2,1)S(1)}, bf16[512,256]{1,0:T(8,128)(2,1)S(1)}, u32[]{:S(2)}, u32[]{:S(2)}) collective-permute-start(bf16[512,256]{1,0:T(8,128)(2,1)S(1)} %get-tuple-element.10), channel_id=1, source_target_pairs={{0,4},{2,6},{4,0},{6,2},{1,5},{3,7},{5,1},{7,3},{8,12},{10,14},{12... | collective-permute-start | bytes 786440 | tf_op jit(solution)/shard_map/ppermute | solution.py:38
  152.7 0.8 fusion
  153.5 11.7 %collective-permute-done.6.other_ref = bf16[512,256]{1,0:T(8,128)(2,1)S(1)} collective-permute-done((bf16[512,256]{1,0:T(8,128)(2,1)S(1)}, bf16[512,256]{1,0:T(8,128)(2,1)S(1)}, u32[]{:S(2)}, u32[]{:S(2)}) %collective-permute-start.6) | collective-permute-done | bytes 262176 | tf_op jit(solution)/shard_map/ppermute | solution.py:38
  165.3 1.4 finish_one.1
  (36 shorter events, 4.3 us)
Async XLA Ops:
  7.2 107.9 %all-gather.4.cloned.1.call-start = ((), (), s32[]{:S(2)}) async-start(), calls=%async_computation | async-start | bytes 5898240 | tf_op jit(solution)/shard_map/all_gather | solution.py:148
  8.8 13.3 %collective-permute-start.3 = (bf16[80,256]{1,0:T(8,128)(2,1)S(1)}, bf16[80,256]{1,0:T(8,128)(2,1)S(1)}, u32[]{:S(2)}, u32[]{:S(2)}) collective-permute-start(bf16[80,256]{1,0:T(8,128)(2,1)S(1)} %multiply_convert_fusion.1), channel_id=1, source_target_pairs={{0,0},{2,2},{4,256},{6,258},{128,128},{130,130},{132,384},{134,386... | collective-permute-start | bytes 122888 | tf_op jit(solution)/shard_map/ppermute | solution.py:38
  9.5 18.6 %collective-permute-start.5 = (bf16[80,256]{1,0:T(8,128)(2,1)S(1)}, bf16[80,256]{1,0:T(8,128)(2,1)S(1)}, u32[]{:S(2)}, u32[]{:S(2)}) collective-permute-start(bf16[80,256]{1,0:T(8,128)(2,1)S(1)} %multiply_convert_fusion.1), channel_id=1, source_target_pairs={{0,8},{2,10},{4,264},{6,266},{8,0},{10,2},{12,256},{14,258},{128,1... | collective-permute-start | bytes 122888 | tf_op jit(solution)/shard_map/ppermute | solution.py:38
  19.4 8.7 %collective-permute-start.4 = (bf16[80,256]{1,0:T(8,128)(2,1)S(1)}, bf16[80,256]{1,0:T(8,128)(2,1)S(1)}, u32[]{:S(2)}, u32[]{:S(2)}) collective-permute-start(bf16[80,256]{1,0:T(8,128)(2,1)S(1)} %multiply_convert_fusion), channel_id=1, source_target_pairs={{0,8},{8,0},{1,9},{9,1},{2,10},{10,2},{3,11},{11,3},{4,12},{12,4},... | collective-permute-start | bytes 122888 | tf_op jit(solution)/shard_map/ppermute | solution.py:38
  43.7 25.5 %collective-permute-start.8 = (bf16[512,640]{1,0:T(8,128)(2,1)}, bf16[512,640]{1,0:T(8,128)(2,1)S(1)}, u32[]{:S(2)}, u32[]{:S(2)}) collective-permute-start(bf16[512,640]{1,0:T(8,128)(2,1)} %refs_0_.3), channel_id=1, source_target_pairs={{0,2},{2,0},{4,6},{6,4},{1,3},{3,1},{5,7},{7,5},{8,10},{10,8},{12,... | collective-permute-start | bytes 1966088 | tf_op jit(solution)/shard_map/ppermute | solution.py:38
  46.0 35.0 %collective-permute-start.9 = (bf16[512,640]{1,0:T(8,128)(2,1)}, bf16[512,640]{1,0:T(8,128)(2,1)S(1)}, u32[]{:S(2)}, u32[]{:S(2)}) collective-permute-start(bf16[512,640]{1,0:T(8,128)(2,1)} %refs_0_.3), channel_id=1, source_target_pairs={{0,4},{2,6},{4,0},{6,2},{1,5},{3,7},{5,1},{7,3},{8,12},{10,14},{12... | collective-permute-start | bytes 1966088 | tf_op jit(solution)/shard_map/ppermute | solution.py:38
  49.3 53.2 %collective-permute-start.10 = (bf16[512,640]{1,0:T(8,128)(2,1)}, bf16[512,640]{1,0:T(8,128)(2,1)S(1)}, u32[]{:S(2)}, u32[]{:S(2)}) collective-permute-start(bf16[512,640]{1,0:T(8,128)(2,1)} %refs_0_.3), channel_id=1, source_target_pairs={{0,6},{2,4},{4,2},{6,0},{1,7},{3,5},{5,3},{7,1},{8,14},{10,12},{12... | collective-permute-start | bytes 1966088 | tf_op jit(solution)/shard_map/ppermute | solution.py:38
  53.0 51.5 %collective-permute-start.11 = (bf16[512,640]{1,0:T(8,128)(2,1)}, bf16[512,640]{1,0:T(8,128)(2,1)S(1)}, u32[]{:S(2)}, u32[]{:S(2)}) collective-permute-start(bf16[512,640]{1,0:T(8,128)(2,1)} %refs_0_.3), channel_id=1, source_target_pairs={{0,1},{1,0},{2,3},{3,2},{4,5},{5,4},{6,7},{7,6},{8,9},{9,8},{10,11... | collective-permute-start | bytes 1966088 | tf_op jit(solution)/shard_map/ppermute | solution.py:38
  61.3 45.6 %collective-permute-start = (bf16[512,640]{1,0:T(8,128)(2,1)}, bf16[512,640]{1,0:T(8,128)(2,1)}, u32[]{:S(2)}, u32[]{:S(2)}) collective-permute-start(bf16[512,640]{1,0:T(8,128)(2,1)} %refs_0_.2), channel_id=1, source_target_pairs={{0,2},{2,0},{4,6},{6,4},{1,3},{3,1},{5,7},{7,5},{8,10},{10,8},{12,... | collective-permute-start | bytes 1966088 | tf_op jit(solution)/shard_map/ppermute | solution.py:38
  69.1 40.5 %collective-permute-start.12 = (bf16[512,640]{1,0:T(8,128)(2,1)S(1)}, bf16[512,640]{1,0:T(8,128)(2,1)S(1)}, u32[]{:S(2)}, u32[]{:S(2)}) collective-permute-start(bf16[512,640]{1,0:T(8,128)(2,1)S(1)} %collective-permute-done.8.refs_1_), channel_id=1, source_target_pairs={{0,1},{1,0},{2,3},{3,2},{4,5},{5,4},{6,7},{7,6},{8,9},{9,8},{10,11... | collective-permute-start | bytes 1966088 | tf_op jit(solution)/shard_map/ppermute | solution.py:38
  80.9 28.6 %collective-permute-start.13 = (bf16[512,640]{1,0:T(8,128)(2,1)S(1)}, bf16[512,640]{1,0:T(8,128)(2,1)}, u32[]{:S(2)}, u32[]{:S(2)}) collective-permute-start(bf16[512,640]{1,0:T(8,128)(2,1)S(1)} %collective-permute-done.9.refs_2_), channel_id=1, source_target_pairs={{0,1},{1,0},{2,3},{3,2},{4,5},{5,4},{6,7},{7,6},{8,9},{9,8},{10,11... | collective-permute-start | bytes 1966088 | tf_op jit(solution)/shard_map/ppermute | solution.py:38
  102.5 7.0 %collective-permute-start.14 = (bf16[512,640]{1,0:T(8,128)(2,1)S(1)}, bf16[512,640]{1,0:T(8,128)(2,1)}, u32[]{:S(2)}, u32[]{:S(2)}) collective-permute-start(bf16[512,640]{1,0:T(8,128)(2,1)S(1)} %collective-permute-done.10.refs_3_), channel_id=1, source_target_pairs={{0,1},{1,0},{2,3},{3,2},{4,5},{5,4},{6,7},{7,6},{8,9},{9,8},{10,11... | collective-permute-start | bytes 1966088 | tf_op jit(solution)/shard_map/ppermute | solution.py:38
  104.5 34.1 %collective-permute-start.1 = (bf16[512,640]{1,0:T(8,128)(2,1)}, bf16[512,640]{1,0:T(8,128)(2,1)}, u32[]{:S(2)}, u32[]{:S(2)}) collective-permute-start(bf16[512,640]{1,0:T(8,128)(2,1)} %refs_0_.2), channel_id=1, source_target_pairs={{0,1},{1,0},{2,3},{3,2},{4,5},{5,4},{6,7},{7,6},{8,9},{9,8},{10,11... | collective-permute-start | bytes 1966088 | tf_op jit(solution)/shard_map/ppermute | solution.py:38
  106.9 31.6 %collective-permute-start.2 = (bf16[512,640]{1,0:T(8,128)(2,1)}, bf16[512,640]{1,0:T(8,128)(2,1)}, u32[]{:S(2)}, u32[]{:S(2)}) collective-permute-start(bf16[512,640]{1,0:T(8,128)(2,1)} %collective-permute-done.refs_1_), channel_id=1, source_target_pairs={{0,1},{1,0},{2,3},{3,2},{4,5},{5,4},{6,7},{7,6},{8,9},{9,8},{10,11... | collective-permute-start | bytes 1966088 | tf_op jit(solution)/shard_map/ppermute | solution.py:38
  115.1 2.5 %copy-start = (bf16[32,2,160,256]{3,2,1,0:T(8,128)(2,1)S(1)}, bf16[32,2,160,256]{3,2,1,0:T(8,128)(2,1)}, u32[]{:S(2)}) copy-start(bf16[32,2,160,256]{3,2,1,0:T(8,128)(2,1)} %all-gather.4.cloned.1.call-done) | copy-start | bytes 15728644
  117.6 1.1 copy-start.2
  118.7 0.7 copy-start.4
  123.6 28.9 %collective-permute-start.15 = (bf16[512,256]{1,0:T(8,128)(2,1)S(1)}, bf16[512,256]{1,0:T(8,128)(2,1)S(1)}, u32[]{:S(2)}, u32[]{:S(2)}) collective-permute-start(bf16[512,256]{1,0:T(8,128)(2,1)S(1)} %layer_two.1), channel_id=1, source_target_pairs={{0,32},{16,48},{32,0},{48,16},{64,96},{80,112},{96,64},{112,80},{1... | collective-permute-start | bytes 786440 | tf_op jit(solution)/shard_map/ppermute | solution.py:38
  125.6 26.9 %collective-permute-start.16 = (bf16[512,256]{1,0:T(8,128)(2,1)S(1)}, bf16[512,256]{1,0:T(8,128)(2,1)S(1)}, u32[]{:S(2)}, u32[]{:S(2)}) collective-permute-start(bf16[512,256]{1,0:T(8,128)(2,1)S(1)} %layer_two.1), channel_id=1, source_target_pairs={{0,8},{8,0},{1,9},{9,1},{2,10},{10,2},{3,11},{11,3},{4,12},{12,4},... | collective-permute-start | bytes 786440 | tf_op jit(solution)/shard_map/ppermute | solution.py:38
  132.8 19.8 %collective-permute-start.17 = (bf16[512,256]{1,0:T(8,128)(2,1)S(1)}, bf16[512,256]{1,0:T(8,128)(2,1)S(1)}, u32[]{:S(2)}, u32[]{:S(2)}) collective-permute-start(bf16[512,256]{1,0:T(8,128)(2,1)S(1)} %layer_two.1), channel_id=1, source_target_pairs={{0,16},{16,0},{32,48},{48,32},{64,80},{80,64},{96,112},{112,96},{1... | collective-permute-start | bytes 786440 | tf_op jit(solution)/shard_map/ppermute | solution.py:38
  138.5 26.8 %copy-start.5 = (f32[128]{0:T(128)S(1)}, f32[128]{0:T(128)}, u32[]{:S(2)}) copy-start(f32[128]{0:T(128)} %param.17) | copy-start | bytes 1540
  138.6 2.5 %copy-start.1 = (bf16[32,2,160,256]{3,2,1,0:T(8,128)(2,1)S(1)}, bf16[32,2,160,256]{3,2,1,0:T(8,128)(2,1)}, u32[]{:S(2)}) copy-start(bf16[32,2,160,256]{3,2,1,0:T(8,128)(2,1)} %all-gather.4.cloned.1.call-done) | copy-start | bytes 15728644
  141.0 1.1 copy-start.3
  146.3 7.2 %collective-permute-start.7 = (f32[4,128]{1,0:T(4,128)S(1)}, f32[4,128]{1,0:T(4,128)S(1)}, u32[]{:S(2)}, u32[]{:S(2)}) collective-permute-start(f32[4,128]{1,0:T(4,128)S(1)} %bitcast.27), channel_id=1, source_target_pairs={{0,4},{2,6},{4,0},{6,2},{1,5},{3,7},{5,1},{7,3},{8,12},{10,14},{12... | collective-permute-start | bytes 6152 | tf_op jit(solution)/shard_map/ppermute | solution.py:38
  149.6 15.6 %collective-permute-start.6 = (bf16[512,256]{1,0:T(8,128)(2,1)S(1)}, bf16[512,256]{1,0:T(8,128)(2,1)S(1)}, u32[]{:S(2)}, u32[]{:S(2)}) collective-permute-start(bf16[512,256]{1,0:T(8,128)(2,1)S(1)} %get-tuple-element.10), channel_id=1, source_target_pairs={{0,4},{2,6},{4,0},{6,2},{1,5},{3,7},{5,1},{7,3},{8,12},{10,14},{12... | collective-permute-start | bytes 786440 | tf_op jit(solution)/shard_map/ppermute | solution.py:38
Sparse Core Ops, SparseCore 0:
  43.8 71.2 all-gather.3

commit v2 on v1

v2 whole, which is shorter than its diff:
```python
import jax
import jax.numpy as jnp
from jax import lax
from jax.experimental import pallas as pl
from jax.experimental.pallas import tpu as pltpu
from jax.sharding import Mesh
from jax.sharding import PartitionSpec as P

HD = 128
EPS = 1e-06
AXES = ("x", "z", "h", "l", "c")
SIZES = (4, 8, 2, 4, 2)


def move(value, axes, place):
    sizes = [SIZES[AXES.index(axis)] for axis in axes]
    total = 1
    for size in sizes:
        total *= size

    def coordinates(index):
        found = []
        for size in reversed(sizes):
            found.append(index % size)
            index //= size
        return found[::-1]

    def flat(at):
        index = 0
        for size, one in zip(sizes, at):
            index = index * size + one
        return index

    pairs = [(index, flat(place(*coordinates(index)))) for index in range(total)]
    return lax.ppermute(value, axes, pairs)


def head_norm(raw_key, key_gain):
    mean = jnp.mean(raw_key * raw_key, axis=-1, keepdims=True)
    return raw_key * lax.rsqrt(mean + EPS) * key_gain


def row_scale(squares, width, length):
    rows = lax.broadcasted_iota(jnp.int32, squares.shape, 0)
    return jnp.where(rows < length, lax.rsqrt(squares / width + EPS), 0.0)


def copies_in(pairs, sems):
    started = [
        pltpu.make_async_copy(source, target, sems.at[i]) for i, (source, target) in enumerate(pairs)
    ]
    for copy in started:
        copy.start()
    return started


def matrix(block):
    return block.reshape(block.shape[0] * block.shape[1], block.shape[2])


def two_kernel(place, *refs):
    x_refs, (w_ref, gain_ref, out_ref, x_buf, w_buf, sems) = refs[:8], refs[8:]
    l, c, length = place[1], place[2], place[3]
    pairs = []
    for i, x_ref in enumerate(x_refs):
        cores = pl.ds((c ^ (i // 4)) * 4, 4)
        pairs.append((w_ref.at[cores, l ^ (i % 4)], w_buf.at[i]))
        pairs.append((x_ref, x_buf.at[i]))
    copies = copies_in(pairs, sems)
    raw = jnp.zeros(out_ref.shape, jnp.float32)
    squares = jnp.zeros((out_ref.shape[0], HD), jnp.float32)
    for i in range(len(x_refs)):
        copies[2 * i].wait()
        copies[2 * i + 1].wait()
        raw += jnp.dot(x_buf[i], matrix(w_buf[i]), preferred_element_type=jnp.float32)
        squares += square_sums(x_buf.at[i])
    width = len(x_refs) * x_buf.shape[2]
    raw *= row_scale(jnp.sum(squares, axis=-1, keepdims=True), width, length)
    out_ref[:, :HD] = head_norm(raw[:, :HD], gain_ref[...]).astype(out_ref.dtype)
    out_ref[:, HD:] = raw[:, HD:].astype(out_ref.dtype)


def square_sums(x_ref):
    total = jnp.zeros((x_ref.shape[0], HD), jnp.float32)
    for first in range(0, x_ref.shape[1], HD):
        wide = x_ref[:, first : first + HD].astype(jnp.float32)
        total += wide * wide
    return total


def one_kernel(place, *refs):
    x_refs, w_refs, (own_ref, other_ref, x_buf, w_buf, sems) = refs[:4], refs[4:8], refs[8:]
    x, l, c = place[0], place[1], place[2]
    pairs = []
    for half in range(2):
        cores = pl.ds((c ^ half) * 4, 4)
        pairs += [(w_ref.at[cores], w_buf.at[half, q]) for q, w_ref in enumerate(w_refs)]
        pairs += [(x_refs[2 * half + i], x_buf.at[2 * half + i]) for i in range(2)]
    copies = copies_in(pairs, sems)
    mine = jnp.zeros(own_ref.shape, jnp.float32)
    theirs = jnp.zeros(own_ref.shape, jnp.float32)
    for i in range(4):
        if i % 2 == 0:
            for copy in copies[3 * i : 3 * i + 6]:
                copy.wait()
        near = x ^ l ^ (i % 2)
        own, other = matrix(w_buf[i // 2, near]), matrix(w_buf[i // 2, near ^ 2])
        mine += jnp.dot(x_buf[i], own, preferred_element_type=jnp.float32)
        theirs += jnp.dot(x_buf[i], other, preferred_element_type=jnp.float32)
    own_ref[...] = mine
    other_ref[...] = theirs.astype(other_ref.dtype)


def finish_one_kernel(own_ref, other_ref, scale_ref, gain_ref, key_ref, value_ref):
    raw = own_ref[...] + other_ref[...].astype(jnp.float32)
    key_ref[...] = head_norm(raw[:, :HD] * scale_ref[...], gain_ref[...]).astype(key_ref.dtype)
    value_ref[...] = (raw[:, HD:] * scale_ref[...]).astype(value_ref.dtype)


def finish_two_kernel(place, own_ref, *refs):
    swap_refs, (key_ref, value_ref) = refs[:3], refs[3:]
    rows = own_ref.shape[0]
    pair_bit, is_old = place[4], place[5] == 1
    own = own_ref[...]
    received = jnp.where(pair_bit == 1, swap_refs[0][...], swap_refs[1][...])
    received = jnp.where(pair_bit == 2, swap_refs[2][...], received)
    for first, part in ((0, own), (rows, received)):
        part = jnp.where(is_old, part, jnp.zeros_like(part))
        key_ref[first : first + rows, :] = part[:, :HD]
        value_ref[first : first + rows, :] = part[:, HD:]


VMEM = pl.BlockSpec(memory_space=pltpu.VMEM)
SMEM = pl.BlockSpec(memory_space=pltpu.SMEM)
ANY = pl.BlockSpec(memory_space=pl.ANY)
PARAMS = pltpu.CompilerParams(vmem_limit_bytes=60 * 1024 * 1024)


def on_device(
    x_one,
    x_two,
    norm_one,
    norm_two,
    key_gain_one,
    key_gain_two,
    wk_one,
    wv_one,
    wk_two,
    wv_two,
    lengths,
    new_flag,
    partner,
):
    rows, width = x_one.shape
    depth = wk_one.shape[0]
    x, z, h, l, c = [lax.axis_index(axis) for axis in AXES]
    slot = (x * 8 + z) * 2 + h
    pair_bit = jnp.bitwise_xor(partner[0], slot)
    is_old = (new_flag[0] == 0).astype(jnp.int32)
    place = jnp.stack([x, l, c, lengths[0], pair_bit, is_old]).astype(jnp.int32)

    def scaled(gain, w_key, w_value):
        mine = lax.dynamic_slice(gain, (slot * depth,), (depth,))[:, None]
        both = jnp.concatenate([w_key, w_value], axis=1).astype(jnp.float32)
        return (both * mine).astype(jnp.bfloat16)

    w_one = scaled(norm_one, wk_one, wv_one)
    w_two = scaled(norm_two, wk_two, wv_two)
    two_there = move(w_two, ("h",), lambda h: (h ^ 1,))
    one_here = move(w_one, ("x", "l"), lambda x, l: ((l & 2) | (x & 1), (x & 2) | (l & 1)))
    one_there = move(
        w_one, ("x", "h", "l"), lambda x, h, l: ((l & 2) | (x & 1), h ^ 1, (x & 2) | (l & 1))
    )

    def by_h(here, there):
        return jnp.concatenate([jnp.where(h == 0, here, there), jnp.where(h == 0, there, here)])

    w_two = lax.all_gather(lax.all_gather(by_h(w_two, two_there), "x"), "z")
    w_one = lax.all_gather(by_h(one_here, one_there), "z")
    w_ones = [w_one] + [move(w_one, ("x",), lambda x, apart=apart: (x ^ apart,)) for apart in (1, 2, 3)]

    two_blocks = [x_two] + [
        move(x_two, ("l",), lambda l, apart=apart: (l ^ apart,)) for apart in (1, 2, 3)
    ]
    one_blocks = [x_one, move(x_one, ("l",), lambda l: (l ^ 1,))]
    two_blocks = two_blocks + [move(block, ("c",), lambda c: (c ^ 1,)) for block in two_blocks]
    one_blocks = one_blocks + [move(block, ("c",), lambda c: (c ^ 1,)) for block in one_blocks]

    squares = sum(jnp.sum(jnp.square(block.astype(jnp.float32)), axis=-1) for block in one_blocks)
    squares = squares.reshape(-1, HD)
    squares = squares + move(squares, ("l",), lambda l: (l ^ 2,))
    scale = row_scale(squares.reshape(-1, 1), 8 * width, lengths[0])
    scale = jnp.broadcast_to(scale, (rows, HD))
    place, scale = lax.optimization_barrier((place, scale))

    flops = 2 * rows * 8 * width * 2 * HD
    moved = 8 * rows * width * 2 + 8 * width * 2 * HD * 2
    cost = pl.CostEstimate(flops=flops, bytes_accessed=moved, transcendentals=0)
    both_two = pl.pallas_call(
        two_kernel,
        out_shape=jax.ShapeDtypeStruct((rows, 2 * HD), jnp.bfloat16),
        in_specs=[SMEM] + [ANY] * 9 + [VMEM],
        out_specs=VMEM,
        scratch_shapes=[
            pltpu.VMEM((8, rows, width), jnp.bfloat16),
            pltpu.VMEM((8, 4, 2 * depth, 2 * HD), jnp.bfloat16),
            pltpu.SemaphoreType.DMA((16,)),
        ],
        compiler_params=PARAMS,
        cost_estimate=cost,
        name="layer_two",
    )(place, *two_blocks, w_two, key_gain_two.reshape(1, HD))
    place_one, both_two = lax.optimization_barrier((place, both_two))
    swaps = [
        move(both_two, ("h",), lambda h: (h ^ 1,)),
        move(both_two, ("z",), lambda z: (z ^ 2,)),
        move(both_two, ("z",), lambda z: (z ^ 1,)),
    ]

    own, other = pl.pallas_call(
        one_kernel,
        out_shape=(
            jax.ShapeDtypeStruct((rows, 2 * HD), jnp.float32),
            jax.ShapeDtypeStruct((rows, 2 * HD), jnp.bfloat16),
        ),
        in_specs=[SMEM] + [ANY] * 8,
        out_specs=(VMEM, VMEM),
        scratch_shapes=[
            pltpu.VMEM((4, rows, width), jnp.bfloat16),
            pltpu.VMEM((2, 4, 4, 2 * depth, 2 * HD), jnp.bfloat16),
            pltpu.SemaphoreType.DMA((12,)),
        ],
        compiler_params=PARAMS,
        cost_estimate=cost,
        name="layer_one",
    )(place_one, *one_blocks, *w_ones)
    other = move(other, ("l",), lambda l: (l ^ 2,))
    keys_one, values_one = pl.pallas_call(
        finish_one_kernel,
        out_shape=(jax.ShapeDtypeStruct((rows, HD), jnp.bfloat16),) * 2,
        in_specs=[VMEM] * 4,
        out_specs=(VMEM, VMEM),
        compiler_params=PARAMS,
        name="finish_one",
    )(own, other, scale, key_gain_one.reshape(1, HD))
    keys_two, values_two = pl.pallas_call(
        finish_two_kernel,
        out_shape=(jax.ShapeDtypeStruct((2 * rows, HD), jnp.bfloat16),) * 2,
        in_specs=[SMEM] + [VMEM] * 4,
        out_specs=(VMEM, VMEM),
        compiler_params=PARAMS,
        name="finish_two",
    )(place, both_two, *swaps)
    return (keys_one, values_one, keys_two, values_two)


def solution(mesh):
    split = Mesh(mesh.devices.reshape(SIZES), AXES)
    whole, line = ("x", "z", "h"), ("l", "c")
    sharded = P(whole, line)
    in_specs = (sharded,) * 2 + (P(),) * 4 + (sharded,) * 4 + (P(whole),) * 3
    return jax.shard_map(
        on_device, mesh=split, in_specs=in_specs, out_specs=(sharded,) * 4, check_vma=False
    )
```

time: 175 us -> 213 us (1.22); the launches traced: 174 us -> 209 us
  blocking collectives: 15.5 us -> 39.7 us
  waiting for transfers between devices: 29 us -> 50.8 us
  starting transfers between devices: 89.8 us -> 77.2 us
  Pallas kernels: 9.73 us -> 16.4 us
  local copies, waits for them, and re-layouts: 10.4 us -> 5.41 us
    ppermute x18 -> x21, waiting for transfers between devices: 23.5 us -> 50.8 us  [move(): return lax.ppermute(value, axes, pairs)]
    all_gather x1 -> x2, blocking collectives: 15.5 us -> 39.7 us  [the longest x1 26.4 us: on_device(): w_one = lax.all_gather(by_h(one_here, one_there), 'z')]
    ppermute x18 -> x21, starting transfers between devices: 89.8 us -> 77.1 us  [move(): return lax.ppermute(value, axes, pairs)]
    unnamed x12 -> x28, local copies, waits for them, and re-layouts: 7.8 us -> 2.24 us
    all_gather x1, waiting for transfers between devices: 5.52 us -> 0.01 us  [on_device(): w_two = lax.all_gather(lax.all_gather(by_h(w_two, two_there), 'x'), 'z')]
    pallas_call x1, Pallas kernels: 4.27 us -> 7.14 us  [on_device(): pl.pallas_call(two_kernel, out_shape=jax.ShapeDtypeStruct((rows, 2 * HD),...]
    pallas_call x1 -> x2, Pallas kernels: 1.45 us -> 4.09 us  [the longest x1 2.09 us: on_device(): pl.pallas_call(finish_two_kernel, out_shape=(jax.ShapeDtypeStruct((2 * ro...]
  transfers between devices with their start and end apart: 19 -> 22, of which waited for: 4 -> 6; matrix products, arithmetic and copies ran while one was open for 2% -> 2% of each run, Pallas kernels for 5% -> 7%
where the time goes in v2:
time: 213 us; the launch traced here: 209 us
  starting transfers between devices  77.2 us (36%)
  waiting for transfers between devices  50.8 us (24%)
  blocking collectives  39.7 us (19%)
  between operations  16.5 us (8%)
  Pallas kernels  16.4 us (8%)
  local copies, waits for them, and re-layouts  5.41 us (3%)
  other arithmetic  2.5 us (1%)
    ppermute x21, starting transfers between devices, move(): return lax.ppermute(value, axes, pairs)  77.1 us
    ppermute x21, waiting for transfers between devices, move(): return lax.ppermute(value, axes, pairs)  50.8 us
    all_gather x1, blocking collectives, on_device(): w_one = lax.all_gather(by_h(one_here, one_there), 'z')  26.4 us
    all_gather x1, blocking collectives, on_device(): w_two = lax.all_gather(lax.all_gather(by_h(w_two, two_there), 'x'), 'z')  13.3 us
    pallas_call x1, Pallas kernels, on_device(): pl.pallas_call(two_kernel, out_shape=jax.ShapeDtypeStruct((rows, 2 * HD),...  7.14 us
    pallas_call x1, Pallas kernels, on_device(): pl.pallas_call(one_kernel, out_shape=(jax.ShapeDtypeStruct((rows, 2 * HD)...  5.22 us
  transfers between devices with their start and end apart: 22, of which 6 were waited for; matrix products, arithmetic and copies ran while one was open for 2% of the time, Pallas kernels for 7%

profile of v2, /device:TPU:1, one launch (start us, length us, event | category | flops | bytes accessed | tf_op | source)
XLA Modules:
  0.0 208.5 jit_solution(3409302243443560457)
XLA Ops:
  8.9 8.3 %collective-permute-start.11 = (bf16[80,256]{1,0:T(8,128)(2,1)S(1)}, bf16[80,256]{1,0:T(8,128)(2,1)S(1)}, u32[]{:S(2)}, u32[]{:S(2)}) collective-permute-start(bf16[80,256]{1,0:T(8,128)(2,1)S(1)} %multiply_convert_fusion.1), channel_id=1, source_target_pairs={{0,8},{8,0},{1,9},{9,1},{2,10},{10,2},{3,11},{11,3},{4,12},{12,4},... | collective-permute-start | bytes 122888 | tf_op jit(solution)/shard_map/ppermute | solution.py:35
  19.5 1.9 collective-permute-start.13
  21.5 6.7 %collective-permute-done.13 = bf16[80,256]{1,0:T(8,128)(2,1)S(1)} collective-permute-done((bf16[80,256]{1,0:T(8,128)(2,1)S(1)}, bf16[80,256]{1,0:T(8,128)(2,1)S(1)}, u32[]{:S(2)}, u32[]{:S(2)}) %collective-permute-start.13) | collective-permute-done | bytes 40992 | tf_op jit(solution)/shard_map/ppermute | solution.py:35
  28.2 13.3 %all-gather = bf16[640,256]{1,0:T(8,128)(2,1)} all-gather(bf16[160,256]{1,0:T(8,128)(2,1)S(1)} %pad_maximum_fusion), channel_id=2, replica_groups=mesh['x'=4,'z'=8,'h'=2,'l'=4,'c'=2] {'x'}, dimensions={0}, use_global_device_ids=true | all-gather | bytes 409600 | tf_op jit(solution)/shard_map/all_gather | solution.py:178
  41.5 2.6 %collective-permute-start = (bf16[512,640]{1,0:T(8,128)(2,1)S(1)}, bf16[512,640]{1,0:T(8,128)(2,1)S(1)}, u32[]{:S(2)}, u32[]{:S(2)}) collective-permute-start(bf16[512,640]{1,0:T(8,128)(2,1)S(1)} %copy-done), channel_id=1, source_target_pairs={{0,2},{2,0},{4,6},{6,4},{1,3},{3,1},{5,7},{7,5},{8,10},{10,8},{12,... | collective-permute-start | bytes 1966088 | tf_op jit(solution)/shard_map/ppermute | solution.py:35
  44.1 6.9 %collective-permute-start.1 = (bf16[512,640]{1,0:T(8,128)(2,1)S(1)}, bf16[512,640]{1,0:T(8,128)(2,1)S(1)}, u32[]{:S(2)}, u32[]{:S(2)}) collective-permute-start(bf16[512,640]{1,0:T(8,128)(2,1)S(1)} %copy-done), channel_id=1, source_target_pairs={{0,1},{1,0},{2,3},{3,2},{4,5},{5,4},{6,7},{7,6},{8,9},{9,8},{10,11... | collective-permute-start | bytes 1966088 | tf_op jit(solution)/shard_map/ppermute | solution.py:35
  51.0 7.1 %collective-permute-start.6 = (bf16[512,640]{1,0:T(8,128)(2,1)S(1)}, bf16[512,640]{1,0:T(8,128)(2,1)S(1)}, u32[]{:S(2)}, u32[]{:S(2)}) collective-permute-start(bf16[512,640]{1,0:T(8,128)(2,1)S(1)} %copy-done.5), channel_id=1, source_target_pairs={{0,6},{2,4},{4,2},{6,0},{1,7},{3,5},{5,3},{7,1},{8,14},{10,12},{12... | collective-permute-start | bytes 1966088 | tf_op jit(solution)/shard_map/ppermute | solution.py:35
  58.1 1.9 collective-permute-start.4
  60.0 2.2 %collective-permute-start.5 = (bf16[512,640]{1,0:T(8,128)(2,1)S(1)}, bf16[512,640]{1,0:T(8,128)(2,1)}, u32[]{:S(2)}, u32[]{:S(2)}) collective-permute-start(bf16[512,640]{1,0:T(8,128)(2,1)S(1)} %copy-done.5), channel_id=1, source_target_pairs={{0,4},{2,6},{4,0},{6,2},{1,5},{3,7},{5,1},{7,3},{8,12},{10,14},{12... | collective-permute-start | bytes 1966088 | tf_op jit(solution)/shard_map/ppermute | solution.py:35
  62.2 2.5 %collective-permute-start.2 = (bf16[512,640]{1,0:T(8,128)(2,1)S(1)}, bf16[512,640]{1,0:T(8,128)(2,1)S(1)}, u32[]{:S(2)}, u32[]{:S(2)}) collective-permute-start(bf16[512,640]{1,0:T(8,128)(2,1)S(1)} %collective-permute-done.refs_1_), channel_id=1, source_target_pairs={{0,1},{1,0},{2,3},{3,2},{4,5},{5,4},{6,7},{7,6},{8,9},{9,8},{10,11... | collective-permute-start | bytes 1966088 | tf_op jit(solution)/shard_map/ppermute | solution.py:35
  65.2 1.9 collective-permute-start.7
  67.1 6.5 %collective-permute-done.6.refs_3_ = bf16[512,640]{1,0:T(8,128)(2,1)S(1)} collective-permute-done((bf16[512,640]{1,0:T(8,128)(2,1)S(1)}, bf16[512,640]{1,0:T(8,128)(2,1)S(1)}, u32[]{:S(2)}, u32[]{:S(2)}) %collective-permute-start.6) | collective-permute-done | bytes 655392 | tf_op jit(solution)/shard_map/ppermute | solution.py:35
  73.6 12.5 %collective-permute-start.10 = (bf16[512,640]{1,0:T(8,128)(2,1)S(1)}, bf16[512,640]{1,0:T(8,128)(2,1)S(1)}, u32[]{:S(2)}, u32[]{:S(2)}) collective-permute-start(bf16[512,640]{1,0:T(8,128)(2,1)S(1)} %collective-permute-done.6.refs_3_), channel_id=1, source_target_pairs={{0,1},{1,0},{2,3},{3,2},{4,5},{5,4},{6,7},{7,6},{8,9},{9,8},{10,11... | collective-permute-start | bytes 1966088 | tf_op jit(solution)/shard_map/ppermute | solution.py:35
  86.1 6.7 %collective-permute-done.4.refs_1_ = bf16[512,640]{1,0:T(8,128)(2,1)} collective-permute-done((bf16[512,640]{1,0:T(8,128)(2,1)S(1)}, bf16[512,640]{1,0:T(8,128)(2,1)}, u32[]{:S(2)}, u32[]{:S(2)}) %collective-permute-start.4) | collective-permute-done | bytes 655392 | tf_op jit(solution)/shard_map/ppermute | solution.py:35
  92.8 3.0 %collective-permute-start.8 = (bf16[512,640]{1,0:T(8,128)(2,1)}, bf16[512,640]{1,0:T(8,128)(2,1)}, u32[]{:S(2)}, u32[]{:S(2)}) collective-permute-start(bf16[512,640]{1,0:T(8,128)(2,1)} %collective-permute-done.4.refs_1_), channel_id=1, source_target_pairs={{0,1},{1,0},{2,3},{3,2},{4,5},{5,4},{6,7},{7,6},{8,9},{9,8},{10,11... | collective-permute-start | bytes 1966088 | tf_op jit(solution)/shard_map/ppermute | solution.py:35
  95.8 18.5 %collective-permute-done.5.refs_2_ = bf16[512,640]{1,0:T(8,128)(2,1)} collective-permute-done((bf16[512,640]{1,0:T(8,128)(2,1)S(1)}, bf16[512,640]{1,0:T(8,128)(2,1)}, u32[]{:S(2)}, u32[]{:S(2)}) %collective-permute-start.5) | collective-permute-done | bytes 655392 | tf_op jit(solution)/shard_map/ppermute | solution.py:35
  114.3 2.5 %collective-permute-start.9 = (bf16[512,640]{1,0:T(8,128)(2,1)}, bf16[512,640]{1,0:T(8,128)(2,1)}, u32[]{:S(2)}, u32[]{:S(2)}) collective-permute-start(bf16[512,640]{1,0:T(8,128)(2,1)} %collective-permute-done.5.refs_2_), channel_id=1, source_target_pairs={{0,1},{1,0},{2,3},{3,2},{4,5},{5,4},{6,7},{7,6},{8,9},{9,8},{10,11... | collective-permute-start | bytes 1966088 | tf_op jit(solution)/shard_map/ppermute | solution.py:35
  117.3 1.9 collective-permute-start.3
  119.2 26.4 %all-gather.2 = bf16[1280,256]{1,0:T(8,128)(2,1)S(1)} all-gather(bf16[160,256]{1,0:T(8,128)(2,1)S(1)} %pad_maximum_fusion.1), channel_id=4, replica_groups=mesh['x'=4,'z'=8,'h'=2,'l'=4,'c'=2] {'z'}, dimensions={0}, use_global_device_ids=true | all-gather | bytes 737280 | tf_op jit(solution)/shard_map/all_gather | solution.py:179
  145.6 1.9 collective-permute-start.14
  147.6 4.2 %collective-permute-start.15 = (bf16[8,160,256]{2,1,0:T(8,128)(2,1)S(1)}, bf16[8,160,256]{2,1,0:T(8,128)(2,1)}, u32[]{:S(2)}, u32[]{:S(2)}) collective-permute-start(bf16[8,160,256]{2,1,0:T(8,128)(2,1)S(1)} %bitcast.21), channel_id=1, source_target_pairs={{0,256},{128,384},{256,0},{384,128},{1,257},{129,385},{257,1},{385... | collective-permute-start | bytes 1966088 | tf_op jit(solution)/shard_map/ppermute | solution.py:35
  151.8 3.5 %collective-permute-start.16 = (bf16[8,160,256]{2,1,0:T(8,128)(2,1)S(1)}, bf16[8,160,256]{2,1,0:T(8,128)(2,1)}, u32[]{:S(2)}, u32[]{:S(2)}) collective-permute-start(bf16[8,160,256]{2,1,0:T(8,128)(2,1)S(1)} %bitcast.22), channel_id=1, source_target_pairs={{0,384},{128,256},{256,128},{384,0},{1,385},{129,257},{257,129},{3... | collective-permute-start | bytes 1966088 | tf_op jit(solution)/shard_map/ppermute | solution.py:35
  158.8 7.1 %layer_two.1.own_ref = bf16[512,256]{1,0:T(8,128)(2,1)} custom-call(s32[6]{0:T(128)} %stack.20.place, bf16[512,640]{1,0:T(8,128)(2,1)} %refs_0_.2, bf16[512,640]{1,0:T(8,128)(2,1)} %collective-permute-done.4.refs_1_, bf16[512,640]{1,0:T(8,128)(2,1)} %collective-permute-done.5.refs_2_, bf16[512,640]{1,0:T(8,128)(2,1)} %copy-done.6, ...), custom_call_target="tpu_custom_call" | custom-call | flops 1342177280 | bytes 7864320 | tf_op jit(solution)/shard_map/layer_two/pallas_call | solution.py:199
  166.0 2.5 %collective-permute-start.18 = (bf16[512,256]{1,0:T(8,128)(2,1)}, bf16[512,256]{1,0:T(8,128)(2,1)S(1)}, u32[]{:S(2)}, u32[]{:S(2)}) collective-permute-start(bf16[512,256]{1,0:T(8,128)(2,1)} %layer_two.1.own_ref), channel_id=1, source_target_pairs={{0,8},{8,0},{1,9},{9,1},{2,10},{10,2},{3,11},{11,3},{4,12},{12,4},... | collective-permute-start | bytes 786440 | tf_op jit(solution)/shard_map/ppermute | solution.py:35
  168.5 2.2 %collective-permute-start.19 = (bf16[512,256]{1,0:T(8,128)(2,1)}, bf16[512,256]{1,0:T(8,128)(2,1)S(1)}, u32[]{:S(2)}, u32[]{:S(2)}) collective-permute-start(bf16[512,256]{1,0:T(8,128)(2,1)} %layer_two.1.own_ref), channel_id=1, source_target_pairs={{0,32},{16,48},{32,0},{48,16},{64,96},{80,112},{96,64},{112,80},{1... | collective-permute-start | bytes 786440 | tf_op jit(solution)/shard_map/ppermute | solution.py:35
  170.7 3.2 %collective-permute-start.20 = (bf16[512,256]{1,0:T(8,128)(2,1)}, bf16[512,256]{1,0:T(8,128)(2,1)S(1)}, u32[]{:S(2)}, u32[]{:S(2)}) collective-permute-start(bf16[512,256]{1,0:T(8,128)(2,1)} %layer_two.1.own_ref), channel_id=1, source_target_pairs={{0,16},{16,0},{32,48},{48,32},{64,80},{80,64},{96,112},{112,96},{1... | collective-permute-start | bytes 786440 | tf_op jit(solution)/shard_map/ppermute | solution.py:35
  173.9 7.8 %collective-permute-done.16.refs_7_ = bf16[8,160,256]{2,1,0:T(8,128)(2,1)} collective-permute-done((bf16[8,160,256]{2,1,0:T(8,128)(2,1)S(1)}, bf16[8,160,256]{2,1,0:T(8,128)(2,1)}, u32[]{:S(2)}, u32[]{:S(2)}) %collective-permute-start.16) | collective-permute-done | bytes 655392 | tf_op jit(solution)/shard_map/ppermute | solution.py:35
  181.8 5.2 %layer_one.1 = (f32[512,256]{1,0:T(8,128)}, bf16[512,256]{1,0:T(8,128)(2,1)}) custom-call(s32[6]{0:T(128)} %stack.20.place, bf16[512,640]{1,0:T(8,128)(2,1)} %refs_0_.3, bf16[512,640]{1,0:T(8,128)(2,1)} %copy-done.1, bf16[512,640]{1,0:T(8,128)(2,1)} %copy-done.2, bf16[512,640]{1,0:T(8,128)(2,1)} %copy-done.3, bf16[8,160,256]{2,1,0:T(8,128)(2,1)} %bitcast.23, ...), custom_call_target="tpu_custom_call" | custom-call | flops 1342177280 | bytes 7864320 | tf_op jit(solution)/shard_map/layer_one/pallas_call | solution.py:220
  187.0 3.8 %collective-permute-start.17 = (bf16[512,256]{1,0:T(8,128)(2,1)}, bf16[512,256]{1,0:T(8,128)(2,1)S(1)}, u32[]{:S(2)}, u32[]{:S(2)}) collective-permute-start(bf16[512,256]{1,0:T(8,128)(2,1)} %get-tuple-element.17), channel_id=1, source_target_pairs={{0,4},{2,6},{4,0},{6,2},{1,5},{3,7},{5,1},{7,3},{8,12},{10,14},{12... | collective-permute-start | bytes 786440 | tf_op jit(solution)/shard_map/ppermute | solution.py:35
  192.3 2.1 %finish_two.1 = (bf16[1024,128]{1,0:T(8,128)(2,1)}, bf16[1024,128]{1,0:T(8,128)(2,1)}) custom-call(s32[6]{0:T(128)} %stack.20.place, bf16[512,256]{1,0:T(8,128)(2,1)} %layer_two.1.own_ref, bf16[512,256]{1,0:T(8,128)(2,1)} %copy-done.10, bf16[512,256]{1,0:T(8,128)(2,1)} %copy-done.11, bf16[512,256]{1,0:T(8,128)(2,1)} %copy-done.12), custom_call_target="tpu_custom_call" | custom-call | tf_op jit(solution)/shard_map/finish_two/pallas_call | solution.py:246
  194.4 4.5 %collective-permute-done.17.other_ref = bf16[512,256]{1,0:T(8,128)(2,1)S(1)} collective-permute-done((bf16[512,256]{1,0:T(8,128)(2,1)}, bf16[512,256]{1,0:T(8,128)(2,1)S(1)}, u32[]{:S(2)}, u32[]{:S(2)}) %collective-permute-start.17) | collective-permute-done | bytes 262176 | tf_op jit(solution)/shard_map/ppermute | solution.py:35
  199.7 2.0 finish_one.1
  (62 shorter events, 8.7 us)
Async XLA Ops:
  7.2 34.3 %copy-start = (bf16[512,640]{1,0:T(8,128)(2,1)S(1)}, bf16[512,640]{1,0:T(8,128)(2,1)}, u32[]{:S(2)}) copy-start(bf16[512,640]{1,0:T(8,128)(2,1)} %refs_0_.3) | copy-start | bytes 1966084
  7.2 43.8 %copy-start.5 = (bf16[512,640]{1,0:T(8,128)(2,1)S(1)}, bf16[512,640]{1,0:T(8,128)(2,1)}, u32[]{:S(2)}) copy-start(bf16[512,640]{1,0:T(8,128)(2,1)} %refs_0_.2) | copy-start | bytes 1966084
  7.2 151.6 %all-gather.5.cloned.1.call-start = ((), (), s32[]{:S(2)}) async-start(), calls=%async_computation | async-start | bytes 2949120 | tf_op jit(solution)/shard_map/all_gather | solution.py:178
  8.9 12.5 %collective-permute-start.11 = (bf16[80,256]{1,0:T(8,128)(2,1)S(1)}, bf16[80,256]{1,0:T(8,128)(2,1)S(1)}, u32[]{:S(2)}, u32[]{:S(2)}) collective-permute-start(bf16[80,256]{1,0:T(8,128)(2,1)S(1)} %multiply_convert_fusion.1), channel_id=1, source_target_pairs={{0,8},{8,0},{1,9},{9,1},{2,10},{10,2},{3,11},{11,3},{4,12},{12,4},... | collective-permute-start | bytes 122888 | tf_op jit(solution)/shard_map/ppermute | solution.py:35
  18.8 2.6 %collective-permute-start.12 = (bf16[80,256]{1,0:T(8,128)(2,1)S(1)}, bf16[80,256]{1,0:T(8,128)(2,1)S(1)}, u32[]{:S(2)}, u32[]{:S(2)}) collective-permute-start(bf16[80,256]{1,0:T(8,128)(2,1)S(1)} %multiply_convert_fusion), channel_id=1, source_target_pairs={{0,0},{2,2},{4,256},{6,258},{128,128},{130,130},{132,384},{134,386... | collective-permute-start | bytes 122888 | tf_op jit(solution)/shard_map/ppermute | solution.py:35
  19.5 8.7 %collective-permute-start.13 = (bf16[80,256]{1,0:T(8,128)(2,1)S(1)}, bf16[80,256]{1,0:T(8,128)(2,1)S(1)}, u32[]{:S(2)}, u32[]{:S(2)}) collective-permute-start(bf16[80,256]{1,0:T(8,128)(2,1)S(1)} %multiply_convert_fusion), channel_id=1, source_target_pairs={{0,8},{2,10},{4,264},{6,266},{8,0},{10,2},{12,256},{14,258},{128,1... | collective-permute-start | bytes 122888 | tf_op jit(solution)/shard_map/ppermute | solution.py:35
  41.5 20.7 %collective-permute-start = (bf16[512,640]{1,0:T(8,128)(2,1)S(1)}, bf16[512,640]{1,0:T(8,128)(2,1)S(1)}, u32[]{:S(2)}, u32[]{:S(2)}) collective-permute-start(bf16[512,640]{1,0:T(8,128)(2,1)S(1)} %copy-done), channel_id=1, source_target_pairs={{0,2},{2,0},{4,6},{6,4},{1,3},{3,1},{5,7},{7,5},{8,10},{10,8},{12,... | collective-permute-start | bytes 1966088 | tf_op jit(solution)/shard_map/ppermute | solution.py:35
  44.1 21.1 %collective-permute-start.1 = (bf16[512,640]{1,0:T(8,128)(2,1)S(1)}, bf16[512,640]{1,0:T(8,128)(2,1)S(1)}, u32[]{:S(2)}, u32[]{:S(2)}) collective-permute-start(bf16[512,640]{1,0:T(8,128)(2,1)S(1)} %copy-done), channel_id=1, source_target_pairs={{0,1},{1,0},{2,3},{3,2},{4,5},{5,4},{6,7},{7,6},{8,9},{9,8},{10,11... | collective-permute-start | bytes 1966088 | tf_op jit(solution)/shard_map/ppermute | solution.py:35
  51.0 22.6 %collective-permute-start.6 = (bf16[512,640]{1,0:T(8,128)(2,1)S(1)}, bf16[512,640]{1,0:T(8,128)(2,1)S(1)}, u32[]{:S(2)}, u32[]{:S(2)}) collective-permute-start(bf16[512,640]{1,0:T(8,128)(2,1)S(1)} %copy-done.5), channel_id=1, source_target_pairs={{0,6},{2,4},{4,2},{6,0},{1,7},{3,5},{5,3},{7,1},{8,14},{10,12},{12... | collective-permute-start | bytes 1966088 | tf_op jit(solution)/shard_map/ppermute | solution.py:35
  58.1 34.7 %collective-permute-start.4 = (bf16[512,640]{1,0:T(8,128)(2,1)S(1)}, bf16[512,640]{1,0:T(8,128)(2,1)}, u32[]{:S(2)}, u32[]{:S(2)}) collective-permute-start(bf16[512,640]{1,0:T(8,128)(2,1)S(1)} %copy-done.5), channel_id=1, source_target_pairs={{0,2},{2,0},{4,6},{6,4},{1,3},{3,1},{5,7},{7,5},{8,10},{10,8},{12,... | collective-permute-start | bytes 1966088 | tf_op jit(solution)/shard_map/ppermute | solution.py:35
  60.0 54.3 %collective-permute-start.5 = (bf16[512,640]{1,0:T(8,128)(2,1)S(1)}, bf16[512,640]{1,0:T(8,128)(2,1)}, u32[]{:S(2)}, u32[]{:S(2)}) collective-permute-start(bf16[512,640]{1,0:T(8,128)(2,1)S(1)} %copy-done.5), channel_id=1, source_target_pairs={{0,4},{2,6},{4,0},{6,2},{1,5},{3,7},{5,1},{7,3},{8,12},{10,14},{12... | collective-permute-start | bytes 1966088 | tf_op jit(solution)/shard_map/ppermute | solution.py:35
  62.2 55.0 %copy-start.1 = (bf16[512,640]{1,0:T(8,128)(2,1)}, bf16[512,640]{1,0:T(8,128)(2,1)S(1)}, u32[]{:S(2)}) copy-start(bf16[512,640]{1,0:T(8,128)(2,1)S(1)} %collective-permute-done.refs_1_) | copy-start | bytes 1966084
  62.2 54.8 %collective-permute-start.2 = (bf16[512,640]{1,0:T(8,128)(2,1)S(1)}, bf16[512,640]{1,0:T(8,128)(2,1)S(1)}, u32[]{:S(2)}, u32[]{:S(2)}) collective-permute-start(bf16[512,640]{1,0:T(8,128)(2,1)S(1)} %collective-permute-done.refs_1_), channel_id=1, source_target_pairs={{0,1},{1,0},{2,3},{3,2},{4,5},{5,4},{6,7},{7,6},{8,9},{9,8},{10,11... | collective-permute-start | bytes 1966088 | tf_op jit(solution)/shard_map/ppermute | solution.py:35
  65.2 100.8 %copy-start.2 = (bf16[512,640]{1,0:T(8,128)(2,1)}, bf16[512,640]{1,0:T(8,128)(2,1)S(1)}, u32[]{:S(2)}) copy-start(bf16[512,640]{1,0:T(8,128)(2,1)S(1)} %collective-permute-done.1.refs_2_) | copy-start | bytes 1966084
  65.2 80.5 %collective-permute-start.7 = (bf16[512,640]{1,0:T(8,128)(2,1)S(1)}, bf16[512,640]{1,0:T(8,128)(2,1)S(1)}, u32[]{:S(2)}, u32[]{:S(2)}) collective-permute-start(bf16[512,640]{1,0:T(8,128)(2,1)S(1)} %copy-done.5), channel_id=1, source_target_pairs={{0,1},{1,0},{2,3},{3,2},{4,5},{5,4},{6,7},{7,6},{8,9},{9,8},{10,11... | collective-permute-start | bytes 1966088 | tf_op jit(solution)/shard_map/ppermute | solution.py:35
  73.6 85.2 %copy-start.6 = (bf16[512,640]{1,0:T(8,128)(2,1)}, bf16[512,640]{1,0:T(8,128)(2,1)S(1)}, u32[]{:S(2)}) copy-start(bf16[512,640]{1,0:T(8,128)(2,1)S(1)} %collective-permute-done.6.refs_3_) | copy-start | bytes 1966084
  73.6 74.0 %collective-permute-start.10 = (bf16[512,640]{1,0:T(8,128)(2,1)S(1)}, bf16[512,640]{1,0:T(8,128)(2,1)S(1)}, u32[]{:S(2)}, u32[]{:S(2)}) collective-permute-start(bf16[512,640]{1,0:T(8,128)(2,1)S(1)} %collective-permute-done.6.refs_3_), channel_id=1, source_target_pairs={{0,1},{1,0},{2,3},{3,2},{4,5},{5,4},{6,7},{7,6},{8,9},{9,8},{10,11... | collective-permute-start | bytes 1966088 | tf_op jit(solution)/shard_map/ppermute | solution.py:35
  92.8 66.0 %collective-permute-start.8 = (bf16[512,640]{1,0:T(8,128)(2,1)}, bf16[512,640]{1,0:T(8,128)(2,1)}, u32[]{:S(2)}, u32[]{:S(2)}) collective-permute-start(bf16[512,640]{1,0:T(8,128)(2,1)} %collective-permute-done.4.refs_1_), channel_id=1, source_target_pairs={{0,1},{1,0},{2,3},{3,2},{4,5},{5,4},{6,7},{7,6},{8,9},{9,8},{10,11... | collective-permute-start | bytes 1966088 | tf_op jit(solution)/shard_map/ppermute | solution.py:35
  114.3 44.5 %collective-permute-start.9 = (bf16[512,640]{1,0:T(8,128)(2,1)}, bf16[512,640]{1,0:T(8,128)(2,1)}, u32[]{:S(2)}, u32[]{:S(2)}) collective-permute-start(bf16[512,640]{1,0:T(8,128)(2,1)} %collective-permute-done.5.refs_2_), channel_id=1, source_target_pairs={{0,1},{1,0},{2,3},{3,2},{4,5},{5,4},{6,7},{7,6},{8,9},{9,8},{10,11... | collective-permute-start | bytes 1966088 | tf_op jit(solution)/shard_map/ppermute | solution.py:35
  117.0 48.9 %copy-start.3 = (bf16[512,640]{1,0:T(8,128)(2,1)}, bf16[512,640]{1,0:T(8,128)(2,1)S(1)}, u32[]{:S(2)}) copy-start(bf16[512,640]{1,0:T(8,128)(2,1)S(1)} %collective-permute-done.2.refs_3_) | copy-start | bytes 1966084
  117.3 34.5 %collective-permute-start.3 = (f32[4,128]{1,0:T(4,128)S(1)}, f32[4,128]{1,0:T(4,128)S(1)}, u32[]{:S(2)}, u32[]{:S(2)}) collective-permute-start(f32[4,128]{1,0:T(4,128)S(1)} %add_bitcast_fusion), channel_id=1, source_target_pairs={{0,4},{2,6},{4,0},{6,2},{1,5},{3,7},{5,1},{7,3},{8,12},{10,14},{12... | collective-permute-start | bytes 6152 | tf_op jit(solution)/shard_map/ppermute | solution.py:35
  145.6 20.3 %copy-start.4 = (bf16[1280,256]{1,0:T(8,128)(2,1)}, bf16[1280,256]{1,0:T(8,128)(2,1)S(1)}, u32[]{:S(2)}) copy-start(bf16[1280,256]{1,0:T(8,128)(2,1)S(1)} %all-gather.2) | copy-start | bytes 1966084
  145.6 6.1 %copy-start.7 = (bf16[512,640]{1,0:T(8,128)(2,1)}, bf16[512,640]{1,0:T(8,128)(2,1)S(1)}, u32[]{:S(2)}) copy-start(bf16[512,640]{1,0:T(8,128)(2,1)S(1)} %collective-permute-done.7.refs_4_) | copy-start | bytes 1966084
  145.6 25.1 %collective-permute-start.14 = (bf16[8,160,256]{2,1,0:T(8,128)(2,1)S(1)}, bf16[8,160,256]{2,1,0:T(8,128)(2,1)S(1)}, u32[]{:S(2)}, u32[]{:S(2)}) collective-permute-start(bf16[8,160,256]{2,1,0:T(8,128)(2,1)S(1)} %bitcast.20), channel_id=1, source_target_pairs={{0,128},{128,0},{256,384},{384,256},{1,129},{129,1},{257,385},{385... | collective-permute-start | bytes 1966088 | tf_op jit(solution)/shard_map/ppermute | solution.py:35
  147.6 4.2 %copy-start.8 = (bf16[512,640]{1,0:T(8,128)(2,1)}, bf16[512,640]{1,0:T(8,128)(2,1)S(1)}, u32[]{:S(2)}) copy-start(bf16[512,640]{1,0:T(8,128)(2,1)S(1)} %collective-permute-done.10.refs_7_) | copy-start | bytes 1966084
  147.6 26.3 %collective-permute-start.15 = (bf16[8,160,256]{2,1,0:T(8,128)(2,1)S(1)}, bf16[8,160,256]{2,1,0:T(8,128)(2,1)}, u32[]{:S(2)}, u32[]{:S(2)}) collective-permute-start(bf16[8,160,256]{2,1,0:T(8,128)(2,1)S(1)} %bitcast.21), channel_id=1, source_target_pairs={{0,256},{128,384},{256,0},{384,128},{1,257},{129,385},{257,1},{385... | collective-permute-start | bytes 1966088 | tf_op jit(solution)/shard_map/ppermute | solution.py:35
  151.8 30.0 %collective-permute-start.16 = (bf16[8,160,256]{2,1,0:T(8,128)(2,1)S(1)}, bf16[8,160,256]{2,1,0:T(8,128)(2,1)}, u32[]{:S(2)}, u32[]{:S(2)}) collective-permute-start(bf16[8,160,256]{2,1,0:T(8,128)(2,1)S(1)} %bitcast.22), channel_id=1, source_target_pairs={{0,384},{128,256},{256,128},{384,0},{1,385},{129,257},{257,129},{3... | collective-permute-start | bytes 1966088 | tf_op jit(solution)/shard_map/ppermute | solution.py:35
  166.0 24.8 %collective-permute-start.18 = (bf16[512,256]{1,0:T(8,128)(2,1)}, bf16[512,256]{1,0:T(8,128)(2,1)S(1)}, u32[]{:S(2)}, u32[]{:S(2)}) collective-permute-start(bf16[512,256]{1,0:T(8,128)(2,1)} %layer_two.1.own_ref), channel_id=1, source_target_pairs={{0,8},{8,0},{1,9},{9,1},{2,10},{10,2},{3,11},{11,3},{4,12},{12,4},... | collective-permute-start | bytes 786440 | tf_op jit(solution)/shard_map/ppermute | solution.py:35
  168.5 22.3 %collective-permute-start.19 = (bf16[512,256]{1,0:T(8,128)(2,1)}, bf16[512,256]{1,0:T(8,128)(2,1)S(1)}, u32[]{:S(2)}, u32[]{:S(2)}) collective-permute-start(bf16[512,256]{1,0:T(8,128)(2,1)} %layer_two.1.own_ref), channel_id=1, source_target_pairs={{0,32},{16,48},{32,0},{48,16},{64,96},{80,112},{96,64},{112,80},{1... | collective-permute-start | bytes 786440 | tf_op jit(solution)/shard_map/ppermute | solution.py:35
  170.7 11.1 %copy-start.9 = (bf16[8,160,256]{2,1,0:T(8,128)(2,1)}, bf16[8,160,256]{2,1,0:T(8,128)(2,1)S(1)}, u32[]{:S(2)}) copy-start(bf16[8,160,256]{2,1,0:T(8,128)(2,1)S(1)} %collective-permute-done.14.refs_5_) | copy-start | bytes 1966084
  170.7 20.1 %collective-permute-start.20 = (bf16[512,256]{1,0:T(8,128)(2,1)}, bf16[512,256]{1,0:T(8,128)(2,1)S(1)}, u32[]{:S(2)}, u32[]{:S(2)}) collective-permute-start(bf16[512,256]{1,0:T(8,128)(2,1)} %layer_two.1.own_ref), channel_id=1, source_target_pairs={{0,16},{16,0},{32,48},{48,32},{64,80},{80,64},{96,112},{112,96},{1... | collective-permute-start | bytes 786440 | tf_op jit(solution)/shard_map/ppermute | solution.py:35
  187.0 12.0 %collective-permute-start.17 = (bf16[512,256]{1,0:T(8,128)(2,1)}, bf16[512,256]{1,0:T(8,128)(2,1)S(1)}, u32[]{:S(2)}, u32[]{:S(2)}) collective-permute-start(bf16[512,256]{1,0:T(8,128)(2,1)} %get-tuple-element.17), channel_id=1, source_target_pairs={{0,4},{2,6},{4,0},{6,2},{1,5},{3,7},{5,1},{7,3},{8,12},{10,14},{12... | collective-permute-start | bytes 786440 | tf_op jit(solution)/shard_map/ppermute | solution.py:35
  (4 other events, 2.9 us)
Sparse Core Ops, SparseCore 0:
  41.6 48.7 all-gather.4

commit v3 on v1

v3 whole, which is shorter than its diff:
```python
import functools

import jax
import jax.numpy as jnp
from jax import lax
from jax.experimental import pallas as pl
from jax.experimental.pallas import tpu as pltpu
from jax.sharding import Mesh
from jax.sharding import PartitionSpec as P

HD = 128
EPS = 1e-06
TILE = 128
AXES = ("x", "z", "h", "l", "c")
SIZES = (4, 8, 2, 4, 2)


def move(value, axes, place):
    sizes = [SIZES[AXES.index(axis)] for axis in axes]
    total = 1
    for size in sizes:
        total *= size

    def coordinates(index):
        found = []
        for size in reversed(sizes):
            found.append(index % size)
            index //= size
        return found[::-1]

    def flat(at):
        index = 0
        for size, one in zip(sizes, at):
            index = index * size + one
        return index

    pairs = [(index, flat(place(*coordinates(index)))) for index in range(total)]
    return lax.ppermute(value, axes, pairs)


def head_norm(raw_key, key_gain):
    mean = jnp.mean(raw_key * raw_key, axis=-1, keepdims=True)
    return raw_key * lax.rsqrt(mean + EPS) * key_gain


def row_scale(squares, width, live):
    return jnp.where(live, lax.rsqrt(squares / width + EPS), 0.0)


def square_sums(x):
    wide = x.astype(jnp.float32)
    wide = wide * wide
    return sum(wide[:, first : first + HD] for first in range(0, x.shape[1], HD))


def joined(blocks, weights):
    x = jnp.concatenate([block[...] for block in blocks], axis=1)
    w = jnp.concatenate([w.reshape(-1, w.shape[-1]) for w in weights])
    return jnp.dot(x, w, preferred_element_type=jnp.float32)


def squares_kernel(near, near1, far3, far2, squares_ref):
    blocks = [near.at[1], near1.at[1], far2, far3]
    squares_ref[...] = sum(square_sums(block[...]) for block in blocks)


def two_kernel(place, near, near1, far3, far2, near_c, near1_c, far3_c, far2_c, *refs):
    squares_ref, w_ref, gain_ref, out_ref = refs
    l, c = place[1], place[2]
    blocks = [near.at[1], near1.at[1], far2, far3, near_c.at[1], near1_c.at[1], far2_c, far3_c]

    def weights(i):
        return w_ref[pl.ds((c ^ (i // 4)) * 4, 4), l ^ (i % 4), 0]

    raw = sum(joined(blocks[i : i + 2], [weights(i), weights(i + 1)]) for i in (0, 2, 4, 6))
    squares = squares_ref[...] + sum(square_sums(block[...]) for block in blocks[4:])
    squares = jnp.sum(squares, axis=-1, keepdims=True)
    live = lax.broadcasted_iota(jnp.int32, squares.shape, 0) < place[3]
    raw *= row_scale(squares, len(blocks) * far2.shape[1], live)
    out_ref[:, :HD] = head_norm(raw[:, :HD], gain_ref[...]).astype(out_ref.dtype)
    out_ref[:, HD:] = raw[:, HD:].astype(out_ref.dtype)


def one_kernel(place, near, near1, near_c, near1_c, *refs):
    w_ref, own_ref, other_ref, squares_ref = refs
    l, c = place[1], place[2]
    blocks = [near.at[0], near1.at[0], near_c.at[0], near1_c.at[0]]
    squares = sum(square_sums(block[...]) for block in blocks)

    def product(side):
        total = 0.0
        for core in range(2):
            cores = pl.ds((c ^ core) * 4, 4)
            weights = [w_ref[cores, l ^ side, 1], w_ref[cores, l ^ side ^ 1, 1]]
            total += joined(blocks[2 * core : 2 * core + 2], weights)
        return total

    own_ref[...] = product(0)
    other = product(2)
    rows = own_ref.shape[0]
    other_ref[:rows, :] = other.astype(other_ref.dtype)
    for first in range(0, rows, TILE):
        line = jnp.sum(squares[first : first + TILE].T, axis=0, keepdims=True)
        squares_ref[first // TILE : first // TILE + 1, :] = line
    squares = squares_ref[...]
    high = squares.astype(other_ref.dtype).astype(jnp.float32)
    tail = jnp.concatenate([high, squares - high], axis=1)
    tail = jnp.concatenate([tail, jnp.zeros((16 - tail.shape[0], 2 * HD), jnp.float32)])
    other_ref[rows : rows + 16, :] = tail.astype(other_ref.dtype)


def finish_one_kernel(width, place, own_ref, other_ref, squares_ref, gain_ref, key_ref, value_ref):
    rows_all = own_ref.shape[0]
    theirs = other_ref[rows_all : rows_all + 16, :].astype(jnp.float32)
    for first in range(0, rows_all, TILE):
        rows = slice(first, first + TILE)
        step = first // TILE
        line = squares_ref[step : step + 1, :] + theirs[step : step + 1, :HD]
        line += theirs[step : step + 1, HD:]
        live = first + lax.broadcasted_iota(jnp.int32, line.shape, 1) < place[3]
        scale = jnp.broadcast_to(row_scale(line, width, live), (HD, TILE)).T
        raw = own_ref[rows, :] + other_ref[rows, :].astype(jnp.float32)
        key_ref[rows, :] = head_norm(raw[:, :HD] * scale, gain_ref[...]).astype(key_ref.dtype)
        value_ref[rows, :] = (raw[:, HD:] * scale).astype(value_ref.dtype)


def finish_two_kernel(place, own_ref, *refs):
    swap_refs, (key_ref, value_ref) = refs[:3], refs[3:]
    rows = own_ref.shape[0]
    pair_bit, is_old = place[4], place[5] == 1
    own = own_ref[...]
    received = jnp.where(pair_bit == 2, swap_refs[0][...], swap_refs[1][...])
    received = jnp.where(pair_bit == 1, swap_refs[2][...], received)
    for first, part in ((0, own), (rows, received)):
        part = jnp.where(is_old, part, jnp.zeros_like(part))
        key_ref[first : first + rows, :] = part[:, :HD]
        value_ref[first : first + rows, :] = part[:, HD:]


VMEM = pl.BlockSpec(memory_space=pltpu.VMEM)
SMEM = pl.BlockSpec(memory_space=pltpu.SMEM)
PARAMS = pltpu.CompilerParams(vmem_limit_bytes=24 * 1024 * 1024)


def on_device(
    x_one,
    x_two,
    norm_one,
    norm_two,
    key_gain_one,
    key_gain_two,
    wk_one,
    wv_one,
    wk_two,
    wv_two,
    lengths,
    new_flag,
    partner,
):
    rows, width = x_one.shape
    depth = wk_one.shape[0]
    x, z, h, l, c = [lax.axis_index(axis) for axis in AXES]
    slot = (x * 8 + z) * 2 + h
    pair_bit = jnp.bitwise_xor(partner[0], slot)
    is_old = (new_flag[0] == 0).astype(jnp.int32)
    def scaled(gain, w_key, w_value):
        mine = lax.dynamic_slice(gain, (slot * depth,), (depth,))[:, None]
        both = jnp.concatenate([w_key, w_value], axis=1).astype(jnp.float32)
        return (both * mine).astype(jnp.bfloat16)

    w_one = scaled(norm_one, wk_one, wv_one)
    w_two = scaled(norm_two, wk_two, wv_two)
    two_there = move(w_two, ("h",), lambda h: (h ^ 1,))
    one_here = move(w_one, ("x", "l"), lambda x, l: ((l & 2) | (x & 1), (x & 2) | (l & 1)))
    one_there = move(
        w_one, ("x", "h", "l"), lambda x, h, l: ((l & 2) | (x & 1), h ^ 1, (x & 2) | (l & 1))
    )

    def by_h(here, there):
        return jnp.concatenate([jnp.where(h == 0, here, there), jnp.where(h == 0, there, here)])

    weights = jnp.stack([by_h(w_two, two_there), by_h(one_here, one_there)])
    weights = lax.all_gather(weights, "x")
    weights = lax.all_gather(weights, "z")

    def swapped(block):
        return move(block, ("c",), lambda c: (c ^ 1,))

    near = jnp.stack([x_one, x_two])
    near1 = move(near, ("l",), lambda l: (l ^ 1,))
    far3 = move(x_two, ("l",), lambda l: (l ^ 3,))
    far2 = move(x_two, ("l",), lambda l: (l ^ 2,))
    near1, far2 = lax.optimization_barrier((near1, far2))
    two_blocks = [near, near1, far3, far2]
    two_blocks += [swapped(block) for block in two_blocks]
    one_blocks = [two_blocks[i] for i in (0, 1, 4, 5)]
    place = jnp.stack([x, l, c, lengths[0], pair_bit, is_old]).astype(jnp.int32)

    flops = 2 * rows * 8 * width * 2 * HD
    moved = 8 * rows * width * 2 + 8 * width * 2 * HD * 2
    cost = pl.CostEstimate(flops=flops, bytes_accessed=moved, transcendentals=0)
    squares_two = pl.pallas_call(
        squares_kernel,
        out_shape=jax.ShapeDtypeStruct((rows, HD), jnp.float32),
        in_specs=[VMEM] * 4,
        out_specs=VMEM,
        compiler_params=PARAMS,
        cost_estimate=pl.CostEstimate(flops=1_000_000_000, bytes_accessed=0, transcendentals=0),
        name="squares_two",
    )(*two_blocks[:4])
    both_two = pl.pallas_call(
        two_kernel,
        out_shape=jax.ShapeDtypeStruct((rows, 2 * HD), jnp.bfloat16),
        in_specs=[SMEM] + [VMEM] * 11,
        out_specs=VMEM,
        compiler_params=PARAMS,
        cost_estimate=cost,
        name="layer_two",
    )(place, *two_blocks, squares_two, weights, key_gain_two.reshape(1, HD))
    place, both_two = lax.optimization_barrier((place, both_two))
    swaps = [
        move(both_two, ("z",), lambda z: (z ^ 1,)),
        move(both_two, ("z",), lambda z: (z ^ 2,)),
        move(both_two, ("h",), lambda h: (h ^ 1,)),
    ]

    own, other, squares = pl.pallas_call(
        one_kernel,
        out_shape=(
            jax.ShapeDtypeStruct((rows, 2 * HD), jnp.float32),
            jax.ShapeDtypeStruct((rows + 16, 2 * HD), jnp.bfloat16),
            jax.ShapeDtypeStruct((rows // TILE, HD), jnp.float32),
        ),
        in_specs=[SMEM] + [VMEM] * 5,
        out_specs=(VMEM, VMEM, VMEM),
        compiler_params=PARAMS,
        cost_estimate=cost,
        name="layer_one",
    )(place, *one_blocks, weights)
    other = move(other, ("l",), lambda l: (l ^ 2,))
    keys_one, values_one = pl.pallas_call(
        functools.partial(finish_one_kernel, 8 * width),
        out_shape=(jax.ShapeDtypeStruct((rows, HD), jnp.bfloat16),) * 2,
        in_specs=[SMEM] + [VMEM] * 4,
        out_specs=(VMEM, VMEM),
        compiler_params=PARAMS,
        name="finish_one",
    )(place, own, other, squares, key_gain_one.reshape(1, HD))
    keys_two, values_two = pl.pallas_call(
        finish_two_kernel,
        out_shape=(jax.ShapeDtypeStruct((2 * rows, HD), jnp.bfloat16),) * 2,
        in_specs=[SMEM] + [VMEM] * 4,
        out_specs=(VMEM, VMEM),
        compiler_params=PARAMS,
        name="finish_two",
    )(place, both_two, *swaps)
    return (keys_one, values_one, keys_two, values_two)


def solution(mesh):
    split = Mesh(mesh.devices.reshape(SIZES), AXES)
    whole, line = ("x", "z", "h"), ("l", "c")
    sharded = P(whole, line)
    in_specs = (sharded,) * 2 + (P(),) * 4 + (sharded,) * 4 + (P(whole),) * 3
    return jax.shard_map(
        on_device, mesh=split, in_specs=in_specs, out_specs=(sharded,) * 4, check_vma=False
    )
```

time: 175 us -> 163 us (0.931)
  starting transfers between devices: 89.8 us -> 65 us
  waiting for transfers between devices: 29 us -> 46.7 us
  local copies, waits for them, and re-layouts: 10.4 us -> 4.15 us
  Pallas kernels: 9.73 us -> 12 us
    ppermute x18 -> x14, starting transfers between devices: 89.8 us -> 65 us  [move(): return lax.ppermute(value, axes, pairs)]
    ppermute x18 -> x14, waiting for transfers between devices: 23.5 us -> 45.6 us  [move(): return lax.ppermute(value, axes, pairs)]
    unnamed x12, local copies, waits for them, and re-layouts: 7.8 us -> 2.51 us
    all_gather x1, waiting for transfers between devices: 5.52 us -> 1.09 us  [on_device(): weights = lax.all_gather(weights, 'z')]
    pallas_call x1 -> x3, Pallas kernels: 1.45 us -> 4.53 us  [the longest x1 1.61 us: on_device(): pl.pallas_call(squares_kernel, out_shape=jax.ShapeDtypeStruct((rows, HD),...]
  transfers between devices with their start and end apart: 19 -> 15, of which waited for: 4 -> 7; matrix products, arithmetic and copies ran while one was open for 2% -> 1% of each run, Pallas kernels for 5% -> 2%
where the time goes in v3:
time: 163 us; the launch traced here: 162 us
  starting transfers between devices  65 us (40%)
  waiting for transfers between devices  46.7 us (29%)
  between operations  16.3 us (10%)
  blocking collectives  15.5 us (10%)
  Pallas kernels  12 us (7%)
  local copies, waits for them, and re-layouts  4.15 us (3%)
  other arithmetic  1.93 us (1%)
    ppermute x14, starting transfers between devices, move(): return lax.ppermute(value, axes, pairs)  65 us
    ppermute x14, waiting for transfers between devices, move(): return lax.ppermute(value, axes, pairs)  45.6 us
    all_gather x1, blocking collectives, on_device(): weights = lax.all_gather(weights, 'x')  15.5 us
    pallas_call x1, Pallas kernels, on_device(): pl.pallas_call(two_kernel, out_shape=jax.ShapeDtypeStruct((rows, 2 * HD),...  4 us
    pallas_call x1, Pallas kernels, on_device(): pl.pallas_call(one_kernel, out_shape=(jax.ShapeDtypeStruct((rows, 2 * HD)...  3.43 us
  transfers between devices with their start and end apart: 15, of which 7 were waited for; matrix products, arithmetic and copies ran while one was open for 1% of the time, Pallas kernels for 2%

profile of v3, /device:TPU:1, one launch (start us, length us, event | category | flops | bytes accessed | tf_op | source)
XLA Modules:
  0.0 161.6 jit_solution(10682167420209628822)
XLA Ops:
  7.2 0.8 dynamic_slice.7
  8.0 0.9 multiply_convert_fusion
  8.9 8.3 %collective-permute-start.9 = (bf16[80,256]{1,0:T(8,128)(2,1)S(1)}, bf16[80,256]{1,0:T(8,128)(2,1)S(1)}, u32[]{:S(2)}, u32[]{:S(2)}) collective-permute-start(bf16[80,256]{1,0:T(8,128)(2,1)S(1)} %multiply_convert_fusion), channel_id=1, source_target_pairs={{0,8},{2,10},{4,264},{6,266},{8,0},{10,2},{12,256},{14,258},{128,1... | collective-permute-start | bytes 122888 | tf_op jit(solution)/shard_map/ppermute | solution.py:38
  17.2 0.7 collective-permute-start.8
  17.9 0.8 dynamic_slice.6
  18.7 0.8 multiply_convert_fusion.1
  19.5 1.9 %collective-permute-start.7 = (bf16[80,256]{1,0:T(8,128)(2,1)S(1)}, bf16[80,256]{1,0:T(8,128)(2,1)S(1)}, u32[]{:S(2)}, u32[]{:S(2)}) collective-permute-start(bf16[80,256]{1,0:T(8,128)(2,1)S(1)} %multiply_convert_fusion.1), channel_id=1, source_target_pairs={{0,8},{8,0},{1,9},{9,1},{2,10},{10,2},{3,11},{11,3},{4,12},{12,4},... | collective-permute-start | bytes 122888 | tf_op jit(solution)/shard_map/ppermute | solution.py:38
  21.5 6.7 %collective-permute-done.7 = bf16[80,256]{1,0:T(8,128)(2,1)S(1)} collective-permute-done((bf16[80,256]{1,0:T(8,128)(2,1)S(1)}, bf16[80,256]{1,0:T(8,128)(2,1)S(1)}, u32[]{:S(2)}, u32[]{:S(2)}) %collective-permute-start.7) | collective-permute-done | bytes 40992 | tf_op jit(solution)/shard_map/ppermute | solution.py:38
  28.2 15.5 %all-gather = bf16[8,160,256]{2,1,0:T(8,128)(2,1)} all-gather(bf16[2,160,256]{2,1,0:T(8,128)(2,1)S(1)} %pad_maximum_fusion.1), channel_id=2, replica_groups=mesh['x'=4,'z'=8,'h'=2,'l'=4,'c'=2] {'x'}, dimensions={0}, use_global_device_ids=true | all-gather | bytes 819200 | tf_op jit(solution)/shard_map/all_gather | solution.py:183
  44.0 2.4 %collective-permute-start = (bf16[2,512,640]{2,1,0:T(8,128)(2,1)S(1)}, bf16[2,512,640]{2,1,0:T(8,128)(2,1)S(1)}, u32[]{:S(2)}, u32[]{:S(2)}) collective-permute-start(bf16[2,512,640]{2,1,0:T(8,128)(2,1)S(1)} %pad_maximum_fusion.near), channel_id=1, source_target_pairs={{0,2},{2,0},{4,6},{6,4},{1,3},{3,1},{5,7},{7,5},{8,10},{10,8},{12,... | collective-permute-start | bytes 3932168 | tf_op jit(solution)/shard_map/ppermute | solution.py:38
  46.4 3.3 %collective-permute-start.1 = (bf16[512,640]{1,0:T(8,128)(2,1)S(1)}, bf16[512,640]{1,0:T(8,128)(2,1)S(1)}, u32[]{:S(2)}, u32[]{:S(2)}) collective-permute-start(bf16[512,640]{1,0:T(8,128)(2,1)S(1)} %copy-done.5), channel_id=1, source_target_pairs={{0,4},{2,6},{4,0},{6,2},{1,5},{3,7},{5,1},{7,3},{8,12},{10,14},{12... | collective-permute-start | bytes 1966088 | tf_op jit(solution)/shard_map/ppermute | solution.py:38
  49.8 3.6 %collective-permute-start.2 = (bf16[512,640]{1,0:T(8,128)(2,1)S(1)}, bf16[512,640]{1,0:T(8,128)(2,1)}, u32[]{:S(2)}, u32[]{:S(2)}) collective-permute-start(bf16[512,640]{1,0:T(8,128)(2,1)S(1)} %copy-done.5), channel_id=1, source_target_pairs={{0,6},{2,4},{4,2},{6,0},{1,7},{3,5},{5,3},{7,1},{8,14},{10,12},{12... | collective-permute-start | bytes 1966088 | tf_op jit(solution)/shard_map/ppermute | solution.py:38
  53.4 8.3 %collective-permute-start.3 = (bf16[2,512,640]{2,1,0:T(8,128)(2,1)S(1)}, bf16[2,512,640]{2,1,0:T(8,128)(2,1)}, u32[]{:S(2)}, u32[]{:S(2)}) collective-permute-start(bf16[2,512,640]{2,1,0:T(8,128)(2,1)S(1)} %pad_maximum_fusion.near), channel_id=1, source_target_pairs={{0,1},{1,0},{2,3},{3,2},{4,5},{5,4},{6,7},{7,6},{8,9},{9,8},{10,11... | collective-permute-start | bytes 3932168 | tf_op jit(solution)/shard_map/ppermute | solution.py:38
  61.7 21.3 %collective-permute-done.1.far2 = bf16[512,640]{1,0:T(8,128)(2,1)S(1)} collective-permute-done((bf16[512,640]{1,0:T(8,128)(2,1)S(1)}, bf16[512,640]{1,0:T(8,128)(2,1)S(1)}, u32[]{:S(2)}, u32[]{:S(2)}) %collective-permute-start.1) | collective-permute-done | bytes 655392 | tf_op jit(solution)/shard_map/ppermute | solution.py:38
  83.0 4.9 %collective-permute-done.near1 = bf16[2,512,640]{2,1,0:T(8,128)(2,1)S(1)} collective-permute-done((bf16[2,512,640]{2,1,0:T(8,128)(2,1)S(1)}, bf16[2,512,640]{2,1,0:T(8,128)(2,1)S(1)}, u32[]{:S(2)}, u32[]{:S(2)}) %collective-permute-start) | collective-permute-done | bytes 1310752 | tf_op jit(solution)/shard_map/ppermute | solution.py:38
  87.8 9.6 %collective-permute-start.4 = (bf16[2,512,640]{2,1,0:T(8,128)(2,1)S(1)}, bf16[2,512,640]{2,1,0:T(8,128)(2,1)}, u32[]{:S(2)}, u32[]{:S(2)}) collective-permute-start(bf16[2,512,640]{2,1,0:T(8,128)(2,1)S(1)} %collective-permute-done.near1), channel_id=1, source_target_pairs={{0,1},{1,0},{2,3},{3,2},{4,5},{5,4},{6,7},{7,6},{8,9},{9,8},{10,11... | collective-permute-start | bytes 3932168 | tf_op jit(solution)/shard_map/ppermute | solution.py:38
  97.5 3.8 %collective-permute-done.2.far3 = bf16[512,640]{1,0:T(8,128)(2,1)} collective-permute-done((bf16[512,640]{1,0:T(8,128)(2,1)S(1)}, bf16[512,640]{1,0:T(8,128)(2,1)}, u32[]{:S(2)}, u32[]{:S(2)}) %collective-permute-start.2) | collective-permute-done | bytes 655392 | tf_op jit(solution)/shard_map/ppermute | solution.py:38
  101.2 7.3 %collective-permute-start.5 = (bf16[512,640]{1,0:T(8,128)(2,1)}, bf16[512,640]{1,0:T(8,128)(2,1)}, u32[]{:S(2)}, u32[]{:S(2)}) collective-permute-start(bf16[512,640]{1,0:T(8,128)(2,1)} %collective-permute-done.2.far3), channel_id=1, source_target_pairs={{0,1},{1,0},{2,3},{3,2},{4,5},{5,4},{6,7},{7,6},{8,9},{9,8},{10,11... | collective-permute-start | bytes 1966088 | tf_op jit(solution)/shard_map/ppermute | solution.py:38
  108.5 1.9 %collective-permute-start.6 = (bf16[512,640]{1,0:T(8,128)(2,1)S(1)}, bf16[512,640]{1,0:T(8,128)(2,1)}, u32[]{:S(2)}, u32[]{:S(2)}) collective-permute-start(bf16[512,640]{1,0:T(8,128)(2,1)S(1)} %collective-permute-done.1.far2), channel_id=1, source_target_pairs={{0,1},{1,0},{2,3},{3,2},{4,5},{5,4},{6,7},{7,6},{8,9},{9,8},{10,11... | collective-permute-start | bytes 1966088 | tf_op jit(solution)/shard_map/ppermute | solution.py:38
  112.5 1.6 squares_two.1.refs_0_
  114.1 1.1 all-gather.4.cloned.1.call-done
  115.2 2.5 %copy-done = bf16[32,2,160,256]{3,2,1,0:T(8,128)(2,1)S(1)} copy-done((bf16[32,2,160,256]{3,2,1,0:T(8,128)(2,1)S(1)}, bf16[32,2,160,256]{3,2,1,0:T(8,128)(2,1)}, u32[]{:S(2)}) %copy-start) | copy-done | bytes 5242904
  117.7 4.0 %layer_two.1.own_ref = bf16[512,256]{1,0:T(8,128)(2,1)S(1)} custom-call(s32[6]{0:T(128)S(1)} %stack.38.place, bf16[2,512,640]{2,1,0:T(8,128)(2,1)S(1)} %pad_maximum_fusion.near, bf16[2,512,640]{2,1,0:T(8,128)(2,1)S(1)} %collective-permute-done.near1, bf16[512,640]{1,0:T(8,128)(2,1)} %collective-permute-done.2.far3, ...), custom_call_target="tpu_custom_call" | custom-call | flops 1342177280 | bytes 7864320 | tf_op jit(solution)/shard_map/layer_two/pallas_call | solution.py:211
  121.7 3.4 %layer_one.1 = (f32[512,256]{1,0:T(8,128)S(1)}, bf16[528,256]{1,0:T(8,128)(2,1)S(1)}, f32[4,128]{1,0:T(4,128)S(1)}) custom-call(s32[6]{0:T(128)S(1)} %stack.38.place, bf16[2,512,640]{2,1,0:T(8,128)(2,1)S(1)} %pad_maximum_fusion.near, bf16[2,512,640]{2,1,0:T(8,128)(2,1)S(1)} %collective-permute-done.near1, ...), custom_call_target="tpu_custom_call" | custom-call | flops 1342177280 | bytes 7864320 | tf_op jit(solution)/shard_map/layer_one/pallas_call | solution.py:227
  125.2 4.2 %collective-permute-start.10 = (bf16[528,256]{1,0:T(8,128)(2,1)S(1)}, bf16[528,256]{1,0:T(8,128)(2,1)S(1)}, u32[]{:S(2)}, u32[]{:S(2)}) collective-permute-start(bf16[528,256]{1,0:T(8,128)(2,1)S(1)} %get-tuple-element.19), channel_id=1, source_target_pairs={{0,4},{2,6},{4,0},{6,2},{1,5},{3,7},{5,1},{7,3},{8,12},{10,14},{12... | collective-permute-start | bytes 811016 | tf_op jit(solution)/shard_map/ppermute | solution.py:38
  129.4 5.1 %collective-permute-start.13 = (bf16[512,256]{1,0:T(8,128)(2,1)S(1)}, bf16[512,256]{1,0:T(8,128)(2,1)S(1)}, u32[]{:S(2)}, u32[]{:S(2)}) collective-permute-start(bf16[512,256]{1,0:T(8,128)(2,1)S(1)} %layer_two.1.own_ref), channel_id=1, source_target_pairs={{0,8},{8,0},{1,9},{9,1},{2,10},{10,2},{3,11},{11,3},{4,12},{12,4},... | collective-permute-start | bytes 786440 | tf_op jit(solution)/shard_map/ppermute | solution.py:38
  134.5 4.3 %collective-permute-start.12 = (bf16[512,256]{1,0:T(8,128)(2,1)S(1)}, bf16[512,256]{1,0:T(8,128)(2,1)S(1)}, u32[]{:S(2)}, u32[]{:S(2)}) collective-permute-start(bf16[512,256]{1,0:T(8,128)(2,1)S(1)} %layer_two.1.own_ref), channel_id=1, source_target_pairs={{0,32},{16,48},{32,0},{48,16},{64,96},{80,112},{96,64},{112,80},{1... | collective-permute-start | bytes 786440 | tf_op jit(solution)/shard_map/ppermute | solution.py:38
  138.8 4.0 %collective-permute-start.11 = (bf16[512,256]{1,0:T(8,128)(2,1)S(1)}, bf16[512,256]{1,0:T(8,128)(2,1)S(1)}, u32[]{:S(2)}, u32[]{:S(2)}) collective-permute-start(bf16[512,256]{1,0:T(8,128)(2,1)S(1)} %layer_two.1.own_ref), channel_id=1, source_target_pairs={{0,16},{16,0},{32,48},{48,32},{64,80},{80,64},{96,112},{112,96},{1... | collective-permute-start | bytes 786440 | tf_op jit(solution)/shard_map/ppermute | solution.py:38
  142.8 7.0 %collective-permute-done.13.refs_2_ = bf16[512,256]{1,0:T(8,128)(2,1)S(1)} collective-permute-done((bf16[512,256]{1,0:T(8,128)(2,1)S(1)}, bf16[512,256]{1,0:T(8,128)(2,1)S(1)}, u32[]{:S(2)}, u32[]{:S(2)}) %collective-permute-start.13) | collective-permute-done | bytes 262176 | tf_op jit(solution)/shard_map/ppermute | solution.py:38
  149.8 2.0 %collective-permute-done.11.refs_0_ = bf16[512,256]{1,0:T(8,128)(2,1)S(1)} collective-permute-done((bf16[512,256]{1,0:T(8,128)(2,1)S(1)}, bf16[512,256]{1,0:T(8,128)(2,1)S(1)}, u32[]{:S(2)}, u32[]{:S(2)}) %collective-permute-start.11) | collective-permute-done | bytes 262176 | tf_op jit(solution)/shard_map/ppermute | solution.py:38
  151.8 1.4 finish_two.1
  153.2 1.5 finish_one.1
  (27 shorter events, 0.4 us)
Async XLA Ops:
  7.2 108.1 %all-gather.4.cloned.1.call-start = ((), (), s32[]{:S(2)}) async-start(), calls=%async_computation | async-start | bytes 5898240 | tf_op jit(solution)/shard_map/all_gather | solution.py:184
  8.0 35.8 %copy-start.3 = (bf16[512,640]{1,0:T(8,128)(2,1)S(1)}, bf16[512,640]{1,0:T(8,128)(2,1)}, u32[]{:S(2)}) copy-start(bf16[512,640]{1,0:T(8,128)(2,1)} %param.13) | copy-start | bytes 1966084
  8.0 35.8 %copy-start.4 = (bf16[512,640]{1,0:T(8,128)(2,1)S(1)}, bf16[512,640]{1,0:T(8,128)(2,1)}, u32[]{:S(2)}) copy-start(bf16[512,640]{1,0:T(8,128)(2,1)} %param.14) | copy-start | bytes 1966084
  8.9 12.5 %collective-permute-start.9 = (bf16[80,256]{1,0:T(8,128)(2,1)S(1)}, bf16[80,256]{1,0:T(8,128)(2,1)S(1)}, u32[]{:S(2)}, u32[]{:S(2)}) collective-permute-start(bf16[80,256]{1,0:T(8,128)(2,1)S(1)} %multiply_convert_fusion), channel_id=1, source_target_pairs={{0,8},{2,10},{4,264},{6,266},{8,0},{10,2},{12,256},{14,258},{128,1... | collective-permute-start | bytes 122888 | tf_op jit(solution)/shard_map/ppermute | solution.py:38
  17.2 4.2 %collective-permute-start.8 = (bf16[80,256]{1,0:T(8,128)(2,1)S(1)}, bf16[80,256]{1,0:T(8,128)(2,1)S(1)}, u32[]{:S(2)}, u32[]{:S(2)}) collective-permute-start(bf16[80,256]{1,0:T(8,128)(2,1)S(1)} %multiply_convert_fusion), channel_id=1, source_target_pairs={{0,0},{2,2},{4,256},{6,258},{128,128},{130,130},{132,384},{134,386... | collective-permute-start | bytes 122888 | tf_op jit(solution)/shard_map/ppermute | solution.py:38
  19.5 8.7 %collective-permute-start.7 = (bf16[80,256]{1,0:T(8,128)(2,1)S(1)}, bf16[80,256]{1,0:T(8,128)(2,1)S(1)}, u32[]{:S(2)}, u32[]{:S(2)}) collective-permute-start(bf16[80,256]{1,0:T(8,128)(2,1)S(1)} %multiply_convert_fusion.1), channel_id=1, source_target_pairs={{0,8},{8,0},{1,9},{9,1},{2,10},{10,2},{3,11},{11,3},{4,12},{12,4},... | collective-permute-start | bytes 122888 | tf_op jit(solution)/shard_map/ppermute | solution.py:38
  43.8 2.6 %copy-start.5 = (bf16[512,640]{1,0:T(8,128)(2,1)S(1)}, bf16[512,640]{1,0:T(8,128)(2,1)}, u32[]{:S(2)}) copy-start(bf16[512,640]{1,0:T(8,128)(2,1)} %param.14) | copy-start | bytes 1966084
  44.0 43.9 %collective-permute-start = (bf16[2,512,640]{2,1,0:T(8,128)(2,1)S(1)}, bf16[2,512,640]{2,1,0:T(8,128)(2,1)S(1)}, u32[]{:S(2)}, u32[]{:S(2)}) collective-permute-start(bf16[2,512,640]{2,1,0:T(8,128)(2,1)S(1)} %pad_maximum_fusion.near), channel_id=1, source_target_pairs={{0,2},{2,0},{4,6},{6,4},{1,3},{3,1},{5,7},{7,5},{8,10},{10,8},{12,... | collective-permute-start | bytes 3932168 | tf_op jit(solution)/shard_map/ppermute | solution.py:38
  46.4 36.6 %collective-permute-start.1 = (bf16[512,640]{1,0:T(8,128)(2,1)S(1)}, bf16[512,640]{1,0:T(8,128)(2,1)S(1)}, u32[]{:S(2)}, u32[]{:S(2)}) collective-permute-start(bf16[512,640]{1,0:T(8,128)(2,1)S(1)} %copy-done.5), channel_id=1, source_target_pairs={{0,4},{2,6},{4,0},{6,2},{1,5},{3,7},{5,1},{7,3},{8,12},{10,14},{12... | collective-permute-start | bytes 1966088 | tf_op jit(solution)/shard_map/ppermute | solution.py:38
  49.8 51.5 %collective-permute-start.2 = (bf16[512,640]{1,0:T(8,128)(2,1)S(1)}, bf16[512,640]{1,0:T(8,128)(2,1)}, u32[]{:S(2)}, u32[]{:S(2)}) collective-permute-start(bf16[512,640]{1,0:T(8,128)(2,1)S(1)} %copy-done.5), channel_id=1, source_target_pairs={{0,6},{2,4},{4,2},{6,0},{1,7},{3,5},{5,3},{7,1},{8,14},{10,12},{12... | collective-permute-start | bytes 1966088 | tf_op jit(solution)/shard_map/ppermute | solution.py:38
  53.4 60.7 %collective-permute-start.3 = (bf16[2,512,640]{2,1,0:T(8,128)(2,1)S(1)}, bf16[2,512,640]{2,1,0:T(8,128)(2,1)}, u32[]{:S(2)}, u32[]{:S(2)}) collective-permute-start(bf16[2,512,640]{2,1,0:T(8,128)(2,1)S(1)} %pad_maximum_fusion.near), channel_id=1, source_target_pairs={{0,1},{1,0},{2,3},{3,2},{4,5},{5,4},{6,7},{7,6},{8,9},{9,8},{10,11... | collective-permute-start | bytes 3932168 | tf_op jit(solution)/shard_map/ppermute | solution.py:38
  87.8 26.3 %collective-permute-start.4 = (bf16[2,512,640]{2,1,0:T(8,128)(2,1)S(1)}, bf16[2,512,640]{2,1,0:T(8,128)(2,1)}, u32[]{:S(2)}, u32[]{:S(2)}) collective-permute-start(bf16[2,512,640]{2,1,0:T(8,128)(2,1)S(1)} %collective-permute-done.near1), channel_id=1, source_target_pairs={{0,1},{1,0},{2,3},{3,2},{4,5},{5,4},{6,7},{7,6},{8,9},{9,8},{10,11... | collective-permute-start | bytes 3932168 | tf_op jit(solution)/shard_map/ppermute | solution.py:38
  101.2 12.9 %collective-permute-start.5 = (bf16[512,640]{1,0:T(8,128)(2,1)}, bf16[512,640]{1,0:T(8,128)(2,1)}, u32[]{:S(2)}, u32[]{:S(2)}) collective-permute-start(bf16[512,640]{1,0:T(8,128)(2,1)} %collective-permute-done.2.far3), channel_id=1, source_target_pairs={{0,1},{1,0},{2,3},{3,2},{4,5},{5,4},{6,7},{7,6},{8,9},{9,8},{10,11... | collective-permute-start | bytes 1966088 | tf_op jit(solution)/shard_map/ppermute | solution.py:38
  108.5 5.6 %collective-permute-start.6 = (bf16[512,640]{1,0:T(8,128)(2,1)S(1)}, bf16[512,640]{1,0:T(8,128)(2,1)}, u32[]{:S(2)}, u32[]{:S(2)}) collective-permute-start(bf16[512,640]{1,0:T(8,128)(2,1)S(1)} %collective-permute-done.1.far2), channel_id=1, source_target_pairs={{0,1},{1,0},{2,3},{3,2},{4,5},{5,4},{6,7},{7,6},{8,9},{9,8},{10,11... | collective-permute-start | bytes 1966088 | tf_op jit(solution)/shard_map/ppermute | solution.py:38
  112.5 2.7 %copy-start.1 = (f32[128]{0:T(128)S(1)}, f32[128]{0:T(128)}, u32[]{:S(2)}) copy-start(f32[128]{0:T(128)} %param.18) | copy-start | bytes 1540
  115.2 2.5 %copy-start = (bf16[32,2,160,256]{3,2,1,0:T(8,128)(2,1)S(1)}, bf16[32,2,160,256]{3,2,1,0:T(8,128)(2,1)}, u32[]{:S(2)}) copy-start(bf16[32,2,160,256]{3,2,1,0:T(8,128)(2,1)} %all-gather.4.cloned.1.call-done) | copy-start | bytes 15728644
  121.7 31.5 %copy-start.2 = (f32[128]{0:T(128)S(1)}, f32[128]{0:T(128)}, u32[]{:S(2)}) copy-start(f32[128]{0:T(128)} %param.17) | copy-start | bytes 1540
  125.2 28.1 %collective-permute-start.10 = (bf16[528,256]{1,0:T(8,128)(2,1)S(1)}, bf16[528,256]{1,0:T(8,128)(2,1)S(1)}, u32[]{:S(2)}, u32[]{:S(2)}) collective-permute-start(bf16[528,256]{1,0:T(8,128)(2,1)S(1)} %get-tuple-element.19), channel_id=1, source_target_pairs={{0,4},{2,6},{4,0},{6,2},{1,5},{3,7},{5,1},{7,3},{8,12},{10,14},{12... | collective-permute-start | bytes 811016 | tf_op jit(solution)/shard_map/ppermute | solution.py:38
  129.4 20.4 %collective-permute-start.13 = (bf16[512,256]{1,0:T(8,128)(2,1)S(1)}, bf16[512,256]{1,0:T(8,128)(2,1)S(1)}, u32[]{:S(2)}, u32[]{:S(2)}) collective-permute-start(bf16[512,256]{1,0:T(8,128)(2,1)S(1)} %layer_two.1.own_ref), channel_id=1, source_target_pairs={{0,8},{8,0},{1,9},{9,1},{2,10},{10,2},{3,11},{11,3},{4,12},{12,4},... | collective-permute-start | bytes 786440 | tf_op jit(solution)/shard_map/ppermute | solution.py:38
  134.5 15.3 %collective-permute-start.12 = (bf16[512,256]{1,0:T(8,128)(2,1)S(1)}, bf16[512,256]{1,0:T(8,128)(2,1)S(1)}, u32[]{:S(2)}, u32[]{:S(2)}) collective-permute-start(bf16[512,256]{1,0:T(8,128)(2,1)S(1)} %layer_two.1.own_ref), channel_id=1, source_target_pairs={{0,32},{16,48},{32,0},{48,16},{64,96},{80,112},{96,64},{112,80},{1... | collective-permute-start | bytes 786440 | tf_op jit(solution)/shard_map/ppermute | solution.py:38
  138.8 13.0 %collective-permute-start.11 = (bf16[512,256]{1,0:T(8,128)(2,1)S(1)}, bf16[512,256]{1,0:T(8,128)(2,1)S(1)}, u32[]{:S(2)}, u32[]{:S(2)}) collective-permute-start(bf16[512,256]{1,0:T(8,128)(2,1)S(1)} %layer_two.1.own_ref), channel_id=1, source_target_pairs={{0,16},{16,0},{32,48},{48,32},{64,80},{80,64},{96,112},{112,96},{1... | collective-permute-start | bytes 786440 | tf_op jit(solution)/shard_map/ppermute | solution.py:38
Sparse Core Ops, SparseCore 0:
  43.9 71.2 all-gather.3

commit v4 on v3

v4 whole, which is shorter than its diff:
```python
import jax
import jax.numpy as jnp
from jax import lax
from jax.experimental import pallas as pl
from jax.experimental.pallas import tpu as pltpu
from jax.sharding import Mesh
from jax.sharding import PartitionSpec as P

HD = 128
EPS = 1e-06
AXES = ("x", "z", "h", "l", "c")
SIZES = (4, 8, 2, 4, 2)


def move(value, axes, place):
    sizes = [SIZES[AXES.index(axis)] for axis in axes]
    total = 1
    for size in sizes:
        total *= size

    def coordinates(index):
        found = []
        for size in reversed(sizes):
            found.append(index % size)
            index //= size
        return found[::-1]

    def flat(at):
        index = 0
        for size, one in zip(sizes, at):
            index = index * size + one
        return index

    pairs = [(index, flat(place(*coordinates(index)))) for index in range(total)]
    return lax.ppermute(value, axes, pairs)


def head_norm(raw_key, key_gain):
    mean = jnp.mean(raw_key * raw_key, axis=-1, keepdims=True)
    return raw_key * lax.rsqrt(mean + EPS) * key_gain


def row_scale(squares, width, live):
    return jnp.where(live, lax.rsqrt(squares / width + EPS), 0.0)


def square_sums(x):
    wide = x.astype(jnp.float32)
    wide = wide * wide
    return sum(wide[:, first : first + HD] for first in range(0, x.shape[1], HD))


def project(place, layer, x_refs, w_ref, gain_ref, squares=0.0):
    l, c, length = place[0], place[1], place[2]
    raw = 0.0
    known = len(x_refs) // 2 if isinstance(squares, jax.Array) else 0
    for i in range(0, len(x_refs), 2):
        x = jnp.concatenate([x_ref[...] for x_ref in x_refs[i : i + 2]], axis=1)
        cores = pl.ds((c ^ (i // 4)) * 4, 4)
        w = [w_ref[cores, l ^ (i % 4), layer], w_ref[cores, l ^ (i % 4 + 1), layer]]
        w = jnp.concatenate([half.reshape(-1, 2 * HD) for half in w])
        raw += jnp.dot(x, w, preferred_element_type=jnp.float32)
        if i >= known:
            squares += square_sums(x)
    squares = jnp.sum(squares, axis=-1, keepdims=True)
    live = lax.broadcasted_iota(jnp.int32, squares.shape, 0) < length
    raw *= row_scale(squares, len(x_refs) * x_refs[0].shape[1], live)
    return head_norm(raw[:, :HD], gain_ref[...]).astype(jnp.bfloat16), raw[:, HD:].astype(jnp.bfloat16)


def squares_kernel(*refs):
    refs[-1][...] = sum(square_sums(x_ref[...]) for x_ref in refs[:-1])


def one_kernel(place, *refs):
    key_ref, value_ref = refs[10:]
    key_ref[...], value_ref[...] = project(place, 0, refs[:8], refs[8], refs[9])


def two_kernel(place, *refs):
    out_ref = refs[11]
    keys, values = project(place, 1, refs[:8], refs[8], refs[9], refs[10][...])
    out_ref[:, :HD], out_ref[:, HD:] = keys, values


def finish_two_kernel(place, own_ref, *refs):
    swap_refs, (key_ref, value_ref) = refs[:3], refs[3:]
    rows = own_ref.shape[0]
    pair_bit, is_old = place[3], place[4] == 1
    own = own_ref[...]
    received = jnp.where(pair_bit == 1, swap_refs[0][...], swap_refs[1][...])
    received = jnp.where(pair_bit == 2, swap_refs[2][...], received)
    for first, part in ((0, own), (rows, received)):
        part = jnp.where(is_old, part, jnp.zeros_like(part))
        key_ref[first : first + rows, :] = part[:, :HD]
        value_ref[first : first + rows, :] = part[:, HD:]


VMEM = pl.BlockSpec(memory_space=pltpu.VMEM)
SMEM = pl.BlockSpec(memory_space=pltpu.SMEM)
PARAMS = pltpu.CompilerParams(vmem_limit_bytes=24 * 1024 * 1024)


def on_device(
    x_one,
    x_two,
    norm_one,
    norm_two,
    key_gain_one,
    key_gain_two,
    wk_one,
    wv_one,
    wk_two,
    wv_two,
    lengths,
    new_flag,
    partner,
):
    rows, width = x_one.shape
    depth = wk_one.shape[0]
    x, z, h, l, c = [lax.axis_index(axis) for axis in AXES]
    slot = (x * 8 + z) * 2 + h
    pair_bit = jnp.bitwise_xor(partner[0], slot)
    is_old = (new_flag[0] == 0).astype(jnp.int32)
    def scaled(gain, w_key, w_value):
        mine = lax.dynamic_slice(gain, (slot * depth,), (depth,))[:, None]
        both = jnp.concatenate([w_key, w_value], axis=1).astype(jnp.float32)
        return (both * mine).astype(jnp.bfloat16)

    here = jnp.stack([scaled(norm_one, wk_one, wv_one), scaled(norm_two, wk_two, wv_two)])
    there = move(here, ("h",), lambda h: (h ^ 1,))
    weights = jnp.concatenate(
        [jnp.where(h == 0, here, there), jnp.where(h == 0, there, here)], axis=1
    )
    weights = lax.all_gather(lax.all_gather(weights, "x"), "z")

    def from_line(block, apart):
        return move(block, ("l",), lambda l: (l ^ apart,))

    def from_core(block):
        return move(block, ("c",), lambda c: (c ^ 1,))

    two_far = from_line(x_two, 2)
    two_near = from_line(x_two, 1)
    two_blocks = [x_two, two_near, two_far, from_line(two_far, 1)]
    squares_two = pl.pallas_call(
        squares_kernel,
        out_shape=jax.ShapeDtypeStruct((rows, HD), jnp.float32),
        in_specs=[VMEM] * 4,
        out_specs=VMEM,
        compiler_params=PARAMS,
        cost_estimate=pl.CostEstimate(flops=90_000_000_000, bytes_accessed=0, transcendentals=0),
        name="squares_two",
    )(*two_blocks)
    two_blocks += [from_core(block) for block in two_blocks]
    x_first, two_far = lax.optimization_barrier((x_one, two_far))
    one_near, one_far = from_line(x_first, 1), from_line(x_first, 2)
    one_near, one_far = lax.optimization_barrier((one_near, one_far))
    one_last = from_line(one_far, 1)
    place = jnp.stack([l, c, lengths[0], pair_bit, is_old]).astype(jnp.int32)

    flops = 2 * rows * 8 * width * 2 * HD
    moved = 8 * rows * width * 2 + 8 * width * 2 * HD * 2
    cost = pl.CostEstimate(flops=flops, bytes_accessed=moved, transcendentals=0)
    both_two = pl.pallas_call(
        two_kernel,
        out_shape=jax.ShapeDtypeStruct((rows, 2 * HD), jnp.bfloat16),
        in_specs=[SMEM] + [VMEM] * 11,
        out_specs=VMEM,
        compiler_params=PARAMS,
        cost_estimate=cost,
        name="layer_two",
    )(place, *two_blocks, weights, key_gain_two.reshape(1, HD), squares_two)
    swaps = [
        move(both_two, ("h",), lambda h: (h ^ 1,)),
        move(both_two, ("z",), lambda z: (z ^ 2,)),
        move(both_two, ("z",), lambda z: (z ^ 1,)),
    ]

    one_last, both_two = lax.optimization_barrier((one_last, both_two))
    one_blocks = [x_one, one_near, one_far, one_last]
    one_blocks += [from_core(block) for block in one_blocks]
    keys_one, values_one = pl.pallas_call(
        one_kernel,
        out_shape=(jax.ShapeDtypeStruct((rows, HD), jnp.bfloat16),) * 2,
        in_specs=[SMEM] + [VMEM] * 10,
        out_specs=(VMEM, VMEM),
        compiler_params=PARAMS,
        cost_estimate=cost,
        name="layer_one",
    )(place, *one_blocks, weights, key_gain_one.reshape(1, HD))
    place, keys_one, values_one = lax.optimization_barrier((place, keys_one, values_one))
    keys_two, values_two = pl.pallas_call(
        finish_two_kernel,
        out_shape=(jax.ShapeDtypeStruct((2 * rows, HD), jnp.bfloat16),) * 2,
        in_specs=[SMEM] + [VMEM] * 4,
        out_specs=(VMEM, VMEM),
        compiler_params=PARAMS,
        name="finish_two",
    )(place, both_two, *swaps)
    return (keys_one, values_one, keys_two, values_two)


def solution(mesh):
    split = Mesh(mesh.devices.reshape(SIZES), AXES)
    whole, line = ("x", "z", "h"), ("l", "c")
    sharded = P(whole, line)
    in_specs = (sharded,) * 2 + (P(),) * 4 + (sharded,) * 4 + (P(whole),) * 3
    return jax.shard_map(
        on_device, mesh=split, in_specs=in_specs, out_specs=(sharded,) * 4, check_vma=False
    )
```

time: 163 us -> 154 us (0.945)
  local copies, waits for them, and re-layouts: 4.15 us -> 11 us
  starting transfers between devices: 65 us -> 61.1 us
  blocking collectives: 15.5 us -> 11.7 us
  waiting for transfers between devices: 46.7 us -> 43.1 us
  Pallas kernels: 12 us -> 8.55 us
    unnamed x12 -> x26, local copies, waits for them, and re-layouts: 2.51 us -> 9.36 us
    ppermute x14 -> x18, starting transfers between devices: 65 us -> 61.1 us  [move(): return lax.ppermute(value, axes, pairs)]
    all_gather x1, blocking collectives: 15.5 us -> 11.7 us  [on_device(): weights = lax.all_gather(lax.all_gather(weights, 'x'), 'z')]
    ppermute x14 -> x18, waiting for transfers between devices: 45.6 us -> 43.1 us  [move(): return lax.ppermute(value, axes, pairs)]
    pallas_call x1, Pallas kernels: 4 us -> 2.16 us  [on_device(): pl.pallas_call(two_kernel, out_shape=jax.ShapeDtypeStruct((rows, 2 * HD),...]
    pallas_call x2 -> x1, Pallas kernels: 4.92 us -> 4.45 us  [on_device(): pl.pallas_call(one_kernel, out_shape=(jax.ShapeDtypeStruct((rows, HD), jn...]
  transfers between devices with their start and end apart: 15 -> 19, of which waited for: 7 -> 6; matrix products, arithmetic and copies ran while one was open for 1% -> 0% of each run, Pallas kernels for 2% -> 5%
where the time goes in v4:
time: 154 us; the launch traced here: 153 us
  starting transfers between devices  61.1 us (40%)
  waiting for transfers between devices  43.1 us (28%)
  between operations  16.3 us (11%)
  blocking collectives  11.7 us (8%)
  local copies, waits for them, and re-layouts  11 us (7%)
  Pallas kernels  8.55 us (6%)
    ppermute x18, starting transfers between devices, move(): return lax.ppermute(value, axes, pairs)  61.1 us
    ppermute x18, waiting for transfers between devices, move(): return lax.ppermute(value, axes, pairs)  43.1 us
    all_gather x1, blocking collectives, on_device(): weights = lax.all_gather(lax.all_gather(weights, 'x'), 'z')  11.7 us
    unnamed x26, local copies, waits for them, and re-layouts  9.36 us
    pallas_call x1, Pallas kernels, on_device(): pl.pallas_call(one_kernel, out_shape=(jax.ShapeDtypeStruct((rows, HD), jn...  4.45 us
  transfers between devices with their start and end apart: 19, of which 6 were waited for; matrix products, arithmetic and copies ran while one was open for 0% of the time, Pallas kernels for 5%

profile of v4, /device:TPU:1, one launch (start us, length us, event | category | flops | bytes accessed | tf_op | source)
XLA Modules:
  0.0 152.7 jit_solution(16265243834948193288)
XLA Ops:
  9.7 8.3 %collective-permute-start.10 = (bf16[2,80,256]{2,1,0:T(8,128)(2,1)S(1)}, bf16[2,80,256]{2,1,0:T(8,128)(2,1)S(1)}, u32[]{:S(2)}, u32[]{:S(2)}) collective-permute-start(bf16[2,80,256]{2,1,0:T(8,128)(2,1)S(1)} %pad_maximum_fusion.1), channel_id=1, source_target_pairs={{0,8},{8,0},{1,9},{9,1},{2,10},{10,2},{3,11},{11,3},{4,12},{12,4},... | collective-permute-start | bytes 245768 | tf_op jit(solution)/shard_map/ppermute | solution.py:35
  18.0 2.4 %collective-permute-start = (bf16[512,640]{1,0:T(8,128)(2,1)}, bf16[512,640]{1,0:T(8,128)(2,1)S(1)}, u32[]{:S(2)}, u32[]{:S(2)}) collective-permute-start(bf16[512,640]{1,0:T(8,128)(2,1)} %refs_0_.4), channel_id=1, source_target_pairs={{0,4},{2,6},{4,0},{6,2},{1,5},{3,7},{5,1},{7,3},{8,12},{10,14},{12... | collective-permute-start | bytes 1966088 | tf_op jit(solution)/shard_map/ppermute | solution.py:35
  20.4 2.3 %collective-permute-start.4 = (bf16[512,640]{1,0:T(8,128)(2,1)}, bf16[512,640]{1,0:T(8,128)(2,1)S(1)}, u32[]{:S(2)}, u32[]{:S(2)}) collective-permute-start(bf16[512,640]{1,0:T(8,128)(2,1)} %refs_0_.4), channel_id=1, source_target_pairs={{0,2},{2,0},{4,6},{6,4},{1,3},{3,1},{5,7},{7,5},{8,10},{10,8},{12,... | collective-permute-start | bytes 1966088 | tf_op jit(solution)/shard_map/ppermute | solution.py:35
  22.8 11.7 %all-gather = bf16[8,160,256]{2,1,0:T(8,128)(2,1)} all-gather(bf16[2,160,256]{2,1,0:T(8,128)(2,1)S(1)} %pad_maximum_fusion), channel_id=2, replica_groups=mesh['x'=4,'z'=8,'h'=2,'l'=4,'c'=2] {'x'}, dimensions={0}, use_global_device_ids=true | all-gather | bytes 819200 | tf_op jit(solution)/shard_map/all_gather | solution.py:135
  34.5 17.1 %collective-permute-done.refs_2_ = bf16[512,640]{1,0:T(8,128)(2,1)S(1)} collective-permute-done((bf16[512,640]{1,0:T(8,128)(2,1)}, bf16[512,640]{1,0:T(8,128)(2,1)S(1)}, u32[]{:S(2)}, u32[]{:S(2)}) %collective-permute-start) | collective-permute-done | bytes 655392 | tf_op jit(solution)/shard_map/ppermute | solution.py:35
  51.6 1.9 %collective-permute-start.1 = (bf16[512,640]{1,0:T(8,128)(2,1)}, bf16[512,640]{1,0:T(8,128)(2,1)}, u32[]{:S(2)}, u32[]{:S(2)}) collective-permute-start(bf16[512,640]{1,0:T(8,128)(2,1)} %refs_0_.5), channel_id=1, source_target_pairs={{0,2},{2,0},{4,6},{6,4},{1,3},{3,1},{5,7},{7,5},{8,10},{10,8},{12,... | collective-permute-start | bytes 1966088 | tf_op jit(solution)/shard_map/ppermute | solution.py:35
  53.5 4.6 %collective-permute-start.2 = (bf16[512,640]{1,0:T(8,128)(2,1)}, bf16[512,640]{1,0:T(8,128)(2,1)}, u32[]{:S(2)}, u32[]{:S(2)}) collective-permute-start(bf16[512,640]{1,0:T(8,128)(2,1)} %refs_0_.5), channel_id=1, source_target_pairs={{0,4},{2,6},{4,0},{6,2},{1,5},{3,7},{5,1},{7,3},{8,12},{10,14},{12... | collective-permute-start | bytes 1966088 | tf_op jit(solution)/shard_map/ppermute | solution.py:35
  58.1 3.0 %collective-permute-start.6 = (bf16[512,640]{1,0:T(8,128)(2,1)}, bf16[512,640]{1,0:T(8,128)(2,1)S(1)}, u32[]{:S(2)}, u32[]{:S(2)}) collective-permute-start(bf16[512,640]{1,0:T(8,128)(2,1)} %refs_0_.4), channel_id=1, source_target_pairs={{0,1},{1,0},{2,3},{3,2},{4,5},{5,4},{6,7},{7,6},{8,9},{9,8},{10,11... | collective-permute-start | bytes 1966088 | tf_op jit(solution)/shard_map/ppermute | solution.py:35
  61.1 1.9 %collective-permute-start.5 = (bf16[512,640]{1,0:T(8,128)(2,1)S(1)}, bf16[512,640]{1,0:T(8,128)(2,1)S(1)}, u32[]{:S(2)}, u32[]{:S(2)}) collective-permute-start(bf16[512,640]{1,0:T(8,128)(2,1)S(1)} %collective-permute-done.refs_2_), channel_id=1, source_target_pairs={{0,2},{2,0},{4,6},{6,4},{1,3},{3,1},{5,7},{7,5},{8,10},{10,8},{12,... | collective-permute-start | bytes 1966088 | tf_op jit(solution)/shard_map/ppermute | solution.py:35
  63.0 1.9 %collective-permute-start.8 = (bf16[512,640]{1,0:T(8,128)(2,1)S(1)}, bf16[512,640]{1,0:T(8,128)(2,1)S(1)}, u32[]{:S(2)}, u32[]{:S(2)}) collective-permute-start(bf16[512,640]{1,0:T(8,128)(2,1)S(1)} %collective-permute-done.refs_2_), channel_id=1, source_target_pairs={{0,1},{1,0},{2,3},{3,2},{4,5},{5,4},{6,7},{7,6},{8,9},{9,8},{10,11... | collective-permute-start | bytes 1966088 | tf_op jit(solution)/shard_map/ppermute | solution.py:35
  67.0 14.3 %collective-permute-done.1.refs_1_ = bf16[512,640]{1,0:T(8,128)(2,1)} collective-permute-done((bf16[512,640]{1,0:T(8,128)(2,1)}, bf16[512,640]{1,0:T(8,128)(2,1)}, u32[]{:S(2)}, u32[]{:S(2)}) %collective-permute-start.1) | collective-permute-done | bytes 655392 | tf_op jit(solution)/shard_map/ppermute | solution.py:35
  81.3 4.6 %collective-permute-start.11 = (bf16[512,640]{1,0:T(8,128)(2,1)}, bf16[512,640]{1,0:T(8,128)(2,1)}, u32[]{:S(2)}, u32[]{:S(2)}) collective-permute-start(bf16[512,640]{1,0:T(8,128)(2,1)} %refs_0_.5), channel_id=1, source_target_pairs={{0,1},{1,0},{2,3},{3,2},{4,5},{5,4},{6,7},{7,6},{8,9},{9,8},{10,11... | collective-permute-start | bytes 1966088 | tf_op jit(solution)/shard_map/ppermute | solution.py:35
  86.8 3.4 %collective-permute-start.7 = (bf16[512,640]{1,0:T(8,128)(2,1)S(1)}, bf16[512,640]{1,0:T(8,128)(2,1)S(1)}, u32[]{:S(2)}, u32[]{:S(2)}) collective-permute-start(bf16[512,640]{1,0:T(8,128)(2,1)S(1)} %collective-permute-done.4.refs_1_), channel_id=1, source_target_pairs={{0,1},{1,0},{2,3},{3,2},{4,5},{5,4},{6,7},{7,6},{8,9},{9,8},{10,11... | collective-permute-start | bytes 1966088 | tf_op jit(solution)/shard_map/ppermute | solution.py:35
  90.2 1.9 %collective-permute-start.3 = (bf16[512,640]{1,0:T(8,128)(2,1)}, bf16[512,640]{1,0:T(8,128)(2,1)}, u32[]{:S(2)}, u32[]{:S(2)}) collective-permute-start(bf16[512,640]{1,0:T(8,128)(2,1)} %collective-permute-done.2.refs_2_), channel_id=1, source_target_pairs={{0,2},{2,0},{4,6},{6,4},{1,3},{3,1},{5,7},{7,5},{8,10},{10,8},{12,... | collective-permute-start | bytes 1966088 | tf_op jit(solution)/shard_map/ppermute | solution.py:35
  92.1 5.4 %collective-permute-done.5.refs_3_ = bf16[512,640]{1,0:T(8,128)(2,1)S(1)} collective-permute-done((bf16[512,640]{1,0:T(8,128)(2,1)S(1)}, bf16[512,640]{1,0:T(8,128)(2,1)S(1)}, u32[]{:S(2)}, u32[]{:S(2)}) %collective-permute-start.5) | collective-permute-done | bytes 655392 | tf_op jit(solution)/shard_map/ppermute | solution.py:35
  97.5 4.5 %collective-permute-start.13 = (bf16[512,640]{1,0:T(8,128)(2,1)}, bf16[512,640]{1,0:T(8,128)(2,1)}, u32[]{:S(2)}, u32[]{:S(2)}) collective-permute-start(bf16[512,640]{1,0:T(8,128)(2,1)} %collective-permute-done.2.refs_2_), channel_id=1, source_target_pairs={{0,1},{1,0},{2,3},{3,2},{4,5},{5,4},{6,7},{7,6},{8,9},{9,8},{10,11... | collective-permute-start | bytes 1966088 | tf_op jit(solution)/shard_map/ppermute | solution.py:35
  102.8 1.9 %collective-permute-start.9 = (bf16[512,640]{1,0:T(8,128)(2,1)S(1)}, bf16[512,640]{1,0:T(8,128)(2,1)S(1)}, u32[]{:S(2)}, u32[]{:S(2)}) collective-permute-start(bf16[512,640]{1,0:T(8,128)(2,1)S(1)} %collective-permute-done.5.refs_3_), channel_id=1, source_target_pairs={{0,1},{1,0},{2,3},{3,2},{4,5},{5,4},{6,7},{7,6},{8,9},{9,8},{10,11... | collective-permute-start | bytes 1966088 | tf_op jit(solution)/shard_map/ppermute | solution.py:35
  104.8 1.1 copy-done.2
  107.2 2.4 %collective-permute-start.12 = (bf16[512,640]{1,0:T(8,128)(2,1)}, bf16[512,640]{1,0:T(8,128)(2,1)}, u32[]{:S(2)}, u32[]{:S(2)}) collective-permute-start(bf16[512,640]{1,0:T(8,128)(2,1)} %collective-permute-done.1.refs_1_), channel_id=1, source_target_pairs={{0,1},{1,0},{2,3},{3,2},{4,5},{5,4},{6,7},{7,6},{8,9},{9,8},{10,11... | collective-permute-start | bytes 1966088 | tf_op jit(solution)/shard_map/ppermute | solution.py:35
  110.5 2.5 %copy-done = bf16[32,2,160,256]{3,2,1,0:T(8,128)(2,1)S(1)} copy-done((bf16[32,2,160,256]{3,2,1,0:T(8,128)(2,1)S(1)}, bf16[32,2,160,256]{3,2,1,0:T(8,128)(2,1)}, u32[]{:S(2)}) %copy-start) | copy-done | bytes 5242904
  113.0 1.1 copy-done.5
  114.0 1.1 copy-done.7
  115.1 1.1 copy-done.9
  116.2 2.2 %layer_two.1.own_ref = bf16[512,256]{1,0:T(8,128)(2,1)S(1)} custom-call(s32[5]{0:T(128)S(1)} %stack.21.place, bf16[512,640]{1,0:T(8,128)(2,1)S(1)} %copy-done.3, bf16[512,640]{1,0:T(8,128)(2,1)S(1)} %collective-permute-done.4.refs_1_, bf16[512,640]{1,0:T(8,128)(2,1)S(1)} %collective-permute-done.refs_2_, ...), custom_call_target="tpu_custom_call" | custom-call | flops 1342177280 | bytes 7864320 | tf_op jit(solution)/shard_map/layer_two/pallas_call | solution.py:165
  118.4 1.9 %collective-permute-start.14 = (bf16[512,640]{1,0:T(8,128)(2,1)}, bf16[512,640]{1,0:T(8,128)(2,1)S(1)}, u32[]{:S(2)}, u32[]{:S(2)}) collective-permute-start(bf16[512,640]{1,0:T(8,128)(2,1)} %collective-permute-done.3.refs_3_), channel_id=1, source_target_pairs={{0,1},{1,0},{2,3},{3,2},{4,5},{5,4},{6,7},{7,6},{8,9},{9,8},{10,11... | collective-permute-start | bytes 1966088 | tf_op jit(solution)/shard_map/ppermute | solution.py:35
  120.3 6.5 %collective-permute-start.15 = (bf16[512,256]{1,0:T(8,128)(2,1)S(1)}, bf16[512,256]{1,0:T(8,128)(2,1)S(1)}, u32[]{:S(2)}, u32[]{:S(2)}) collective-permute-start(bf16[512,256]{1,0:T(8,128)(2,1)S(1)} %layer_two.1.own_ref), channel_id=1, source_target_pairs={{0,8},{8,0},{1,9},{9,1},{2,10},{10,2},{3,11},{11,3},{4,12},{12,4},... | collective-permute-start | bytes 786440 | tf_op jit(solution)/shard_map/ppermute | solution.py:35
  126.9 3.6 %collective-permute-start.16 = (bf16[512,256]{1,0:T(8,128)(2,1)S(1)}, bf16[512,256]{1,0:T(8,128)(2,1)S(1)}, u32[]{:S(2)}, u32[]{:S(2)}) collective-permute-start(bf16[512,256]{1,0:T(8,128)(2,1)S(1)} %layer_two.1.own_ref), channel_id=1, source_target_pairs={{0,32},{16,48},{32,0},{48,16},{64,96},{80,112},{96,64},{112,80},{1... | collective-permute-start | bytes 786440 | tf_op jit(solution)/shard_map/ppermute | solution.py:35
  130.5 4.0 %collective-permute-start.17 = (bf16[512,256]{1,0:T(8,128)(2,1)S(1)}, bf16[512,256]{1,0:T(8,128)(2,1)S(1)}, u32[]{:S(2)}, u32[]{:S(2)}) collective-permute-start(bf16[512,256]{1,0:T(8,128)(2,1)S(1)} %layer_two.1.own_ref), channel_id=1, source_target_pairs={{0,16},{16,0},{32,48},{48,32},{64,80},{80,64},{96,112},{112,96},{1... | collective-permute-start | bytes 786440 | tf_op jit(solution)/shard_map/ppermute | solution.py:35
  134.6 4.5 %layer_one.1 = (bf16[512,128]{1,0:T(8,128)(2,1)}, bf16[512,128]{1,0:T(8,128)(2,1)}) custom-call(s32[5]{0:T(128)S(1)} %stack.21.place, bf16[512,640]{1,0:T(8,128)(2,1)S(1)} %copy-done.10, bf16[512,640]{1,0:T(8,128)(2,1)} %collective-permute-done.1.refs_1_, bf16[512,640]{1,0:T(8,128)(2,1)} %collective-permute-done.2.refs_2_, ...), custom_call_target="tpu_custom_call" | custom-call | flops 1342177280 | bytes 7864320 | tf_op jit(solution)/shard_map/layer_one/pallas_call | solution.py:183
  139.0 3.9 %collective-permute-done.16.refs_1_ = bf16[512,256]{1,0:T(8,128)(2,1)S(1)} collective-permute-done((bf16[512,256]{1,0:T(8,128)(2,1)S(1)}, bf16[512,256]{1,0:T(8,128)(2,1)S(1)}, u32[]{:S(2)}, u32[]{:S(2)}) %collective-permute-start.16) | collective-permute-done | bytes 262176 | tf_op jit(solution)/shard_map/ppermute | solution.py:35
  142.9 1.5 collective-permute-done.17.refs_2_
  144.4 1.4 finish_two.1
  (45 shorter events, 6.6 us)
Async XLA Ops:
  7.2 103.3 %all-gather.4.cloned.1.call-start = ((), (), s32[]{:S(2)}) async-start(), calls=%async_computation | async-start | bytes 5898240 | tf_op jit(solution)/shard_map/all_gather | solution.py:135
  9.7 13.0 %collective-permute-start.10 = (bf16[2,80,256]{2,1,0:T(8,128)(2,1)S(1)}, bf16[2,80,256]{2,1,0:T(8,128)(2,1)S(1)}, u32[]{:S(2)}, u32[]{:S(2)}) collective-permute-start(bf16[2,80,256]{2,1,0:T(8,128)(2,1)S(1)} %pad_maximum_fusion.1), channel_id=1, source_target_pairs={{0,8},{8,0},{1,9},{9,1},{2,10},{10,2},{3,11},{11,3},{4,12},{12,4},... | collective-permute-start | bytes 245768 | tf_op jit(solution)/shard_map/ppermute | solution.py:35
  18.0 33.6 %collective-permute-start = (bf16[512,640]{1,0:T(8,128)(2,1)}, bf16[512,640]{1,0:T(8,128)(2,1)S(1)}, u32[]{:S(2)}, u32[]{:S(2)}) collective-permute-start(bf16[512,640]{1,0:T(8,128)(2,1)} %refs_0_.4), channel_id=1, source_target_pairs={{0,4},{2,6},{4,0},{6,2},{1,5},{3,7},{5,1},{7,3},{8,12},{10,14},{12... | collective-permute-start | bytes 1966088 | tf_op jit(solution)/shard_map/ppermute | solution.py:35
  20.4 42.7 %collective-permute-start.4 = (bf16[512,640]{1,0:T(8,128)(2,1)}, bf16[512,640]{1,0:T(8,128)(2,1)S(1)}, u32[]{:S(2)}, u32[]{:S(2)}) collective-permute-start(bf16[512,640]{1,0:T(8,128)(2,1)} %refs_0_.4), channel_id=1, source_target_pairs={{0,2},{2,0},{4,6},{6,4},{1,3},{3,1},{5,7},{7,5},{8,10},{10,8},{12,... | collective-permute-start | bytes 1966088 | tf_op jit(solution)/shard_map/ppermute | solution.py:35
  51.6 29.7 %collective-permute-start.1 = (bf16[512,640]{1,0:T(8,128)(2,1)}, bf16[512,640]{1,0:T(8,128)(2,1)}, u32[]{:S(2)}, u32[]{:S(2)}) collective-permute-start(bf16[512,640]{1,0:T(8,128)(2,1)} %refs_0_.5), channel_id=1, source_target_pairs={{0,2},{2,0},{4,6},{6,4},{1,3},{3,1},{5,7},{7,5},{8,10},{10,8},{12,... | collective-permute-start | bytes 1966088 | tf_op jit(solution)/shard_map/ppermute | solution.py:35
  53.5 33.3 %collective-permute-start.2 = (bf16[512,640]{1,0:T(8,128)(2,1)}, bf16[512,640]{1,0:T(8,128)(2,1)}, u32[]{:S(2)}, u32[]{:S(2)}) collective-permute-start(bf16[512,640]{1,0:T(8,128)(2,1)} %refs_0_.5), channel_id=1, source_target_pairs={{0,4},{2,6},{4,0},{6,2},{1,5},{3,7},{5,1},{7,3},{8,12},{10,14},{12... | collective-permute-start | bytes 1966088 | tf_op jit(solution)/shard_map/ppermute | solution.py:35
  58.1 32.1 %collective-permute-start.6 = (bf16[512,640]{1,0:T(8,128)(2,1)}, bf16[512,640]{1,0:T(8,128)(2,1)S(1)}, u32[]{:S(2)}, u32[]{:S(2)}) collective-permute-start(bf16[512,640]{1,0:T(8,128)(2,1)} %refs_0_.4), channel_id=1, source_target_pairs={{0,1},{1,0},{2,3},{3,2},{4,5},{5,4},{6,7},{7,6},{8,9},{9,8},{10,11... | collective-permute-start | bytes 1966088 | tf_op jit(solution)/shard_map/ppermute | solution.py:35
  61.1 36.4 %collective-permute-start.5 = (bf16[512,640]{1,0:T(8,128)(2,1)S(1)}, bf16[512,640]{1,0:T(8,128)(2,1)S(1)}, u32[]{:S(2)}, u32[]{:S(2)}) collective-permute-start(bf16[512,640]{1,0:T(8,128)(2,1)S(1)} %collective-permute-done.refs_2_), channel_id=1, source_target_pairs={{0,2},{2,0},{4,6},{6,4},{1,3},{3,1},{5,7},{7,5},{8,10},{10,8},{12,... | collective-permute-start | bytes 1966088 | tf_op jit(solution)/shard_map/ppermute | solution.py:35
  63.0 38.9 %collective-permute-start.8 = (bf16[512,640]{1,0:T(8,128)(2,1)S(1)}, bf16[512,640]{1,0:T(8,128)(2,1)S(1)}, u32[]{:S(2)}, u32[]{:S(2)}) collective-permute-start(bf16[512,640]{1,0:T(8,128)(2,1)S(1)} %collective-permute-done.refs_2_), channel_id=1, source_target_pairs={{0,1},{1,0},{2,3},{3,2},{4,5},{5,4},{6,7},{7,6},{8,9},{9,8},{10,11... | collective-permute-start | bytes 1966088 | tf_op jit(solution)/shard_map/ppermute | solution.py:35
  66.9 43.5 %copy-start.11 = (f32[128]{0:T(128)S(1)}, f32[128]{0:T(128)}, u32[]{:S(2)}) copy-start(f32[128]{0:T(128)} %param.18) | copy-start | bytes 1540
  81.3 45.6 %collective-permute-start.11 = (bf16[512,640]{1,0:T(8,128)(2,1)}, bf16[512,640]{1,0:T(8,128)(2,1)}, u32[]{:S(2)}, u32[]{:S(2)}) collective-permute-start(bf16[512,640]{1,0:T(8,128)(2,1)} %refs_0_.5), channel_id=1, source_target_pairs={{0,1},{1,0},{2,3},{3,2},{4,5},{5,4},{6,7},{7,6},{8,9},{9,8},{10,11... | collective-permute-start | bytes 1966088 | tf_op jit(solution)/shard_map/ppermute | solution.py:35
  86.8 19.6 %collective-permute-start.7 = (bf16[512,640]{1,0:T(8,128)(2,1)S(1)}, bf16[512,640]{1,0:T(8,128)(2,1)S(1)}, u32[]{:S(2)}, u32[]{:S(2)}) collective-permute-start(bf16[512,640]{1,0:T(8,128)(2,1)S(1)} %collective-permute-done.4.refs_1_), channel_id=1, source_target_pairs={{0,1},{1,0},{2,3},{3,2},{4,5},{5,4},{6,7},{7,6},{8,9},{9,8},{10,11... | collective-permute-start | bytes 1966088 | tf_op jit(solution)/shard_map/ppermute | solution.py:35
  90.2 28.2 %collective-permute-start.3 = (bf16[512,640]{1,0:T(8,128)(2,1)}, bf16[512,640]{1,0:T(8,128)(2,1)}, u32[]{:S(2)}, u32[]{:S(2)}) collective-permute-start(bf16[512,640]{1,0:T(8,128)(2,1)} %collective-permute-done.2.refs_2_), channel_id=1, source_target_pairs={{0,2},{2,0},{4,6},{6,4},{1,3},{3,1},{5,7},{7,5},{8,10},{10,8},{12,... | collective-permute-start | bytes 1966088 | tf_op jit(solution)/shard_map/ppermute | solution.py:35
  97.5 33.0 %collective-permute-start.13 = (bf16[512,640]{1,0:T(8,128)(2,1)}, bf16[512,640]{1,0:T(8,128)(2,1)}, u32[]{:S(2)}, u32[]{:S(2)}) collective-permute-start(bf16[512,640]{1,0:T(8,128)(2,1)} %collective-permute-done.2.refs_2_), channel_id=1, source_target_pairs={{0,1},{1,0},{2,3},{3,2},{4,5},{5,4},{6,7},{7,6},{8,9},{9,8},{10,11... | collective-permute-start | bytes 1966088 | tf_op jit(solution)/shard_map/ppermute | solution.py:35
  102.0 0.8 copy-start.4
  102.8 6.8 %collective-permute-start.9 = (bf16[512,640]{1,0:T(8,128)(2,1)S(1)}, bf16[512,640]{1,0:T(8,128)(2,1)S(1)}, u32[]{:S(2)}, u32[]{:S(2)}) collective-permute-start(bf16[512,640]{1,0:T(8,128)(2,1)S(1)} %collective-permute-done.5.refs_3_), channel_id=1, source_target_pairs={{0,1},{1,0},{2,3},{3,2},{4,5},{5,4},{6,7},{7,6},{8,9},{9,8},{10,11... | collective-permute-start | bytes 1966088 | tf_op jit(solution)/shard_map/ppermute | solution.py:35
  104.7 1.1 copy-start.2
  105.8 4.6 %copy-start.3 = (bf16[512,640]{1,0:T(8,128)(2,1)S(1)}, bf16[512,640]{1,0:T(8,128)(2,1)}, u32[]{:S(2)}) copy-start(bf16[512,640]{1,0:T(8,128)(2,1)} %refs_0_.4) | copy-start | bytes 1966084
  106.3 0.9 copy-start.6
  107.2 27.3 %collective-permute-start.12 = (bf16[512,640]{1,0:T(8,128)(2,1)}, bf16[512,640]{1,0:T(8,128)(2,1)}, u32[]{:S(2)}, u32[]{:S(2)}) collective-permute-start(bf16[512,640]{1,0:T(8,128)(2,1)} %collective-permute-done.1.refs_1_), channel_id=1, source_target_pairs={{0,1},{1,0},{2,3},{3,2},{4,5},{5,4},{6,7},{7,6},{8,9},{9,8},{10,11... | collective-permute-start | bytes 1966088 | tf_op jit(solution)/shard_map/ppermute | solution.py:35
  109.6 0.8 copy-start.8
  110.5 2.5 %copy-start = (bf16[32,2,160,256]{3,2,1,0:T(8,128)(2,1)S(1)}, bf16[32,2,160,256]{3,2,1,0:T(8,128)(2,1)}, u32[]{:S(2)}) copy-start(bf16[32,2,160,256]{3,2,1,0:T(8,128)(2,1)} %all-gather.4.cloned.1.call-done) | copy-start | bytes 15728644
  113.0 1.1 copy-start.5
  114.0 1.1 copy-start.7
  115.1 1.1 copy-start.9
  116.2 18.3 %copy-start.1 = (bf16[32,2,160,256]{3,2,1,0:T(8,128)(2,1)S(1)}, bf16[32,2,160,256]{3,2,1,0:T(8,128)(2,1)}, u32[]{:S(2)}) copy-start(bf16[32,2,160,256]{3,2,1,0:T(8,128)(2,1)} %all-gather.4.cloned.1.call-done) | copy-start | bytes 15728644
  116.2 18.3 %copy-start.10 = (bf16[512,640]{1,0:T(8,128)(2,1)S(1)}, bf16[512,640]{1,0:T(8,128)(2,1)}, u32[]{:S(2)}) copy-start(bf16[512,640]{1,0:T(8,128)(2,1)} %refs_0_.5) | copy-start | bytes 1966084
  116.2 18.3 %copy-start.12 = (f32[128]{0:T(128)S(1)}, f32[128]{0:T(128)}, u32[]{:S(2)}) copy-start(f32[128]{0:T(128)} %param.17) | copy-start | bytes 1540
  118.4 16.1 %collective-permute-start.14 = (bf16[512,640]{1,0:T(8,128)(2,1)}, bf16[512,640]{1,0:T(8,128)(2,1)S(1)}, u32[]{:S(2)}, u32[]{:S(2)}) collective-permute-start(bf16[512,640]{1,0:T(8,128)(2,1)} %collective-permute-done.3.refs_3_), channel_id=1, source_target_pairs={{0,1},{1,0},{2,3},{3,2},{4,5},{5,4},{6,7},{7,6},{8,9},{9,8},{10,11... | collective-permute-start | bytes 1966088 | tf_op jit(solution)/shard_map/ppermute | solution.py:35
  120.3 18.7 %collective-permute-start.15 = (bf16[512,256]{1,0:T(8,128)(2,1)S(1)}, bf16[512,256]{1,0:T(8,128)(2,1)S(1)}, u32[]{:S(2)}, u32[]{:S(2)}) collective-permute-start(bf16[512,256]{1,0:T(8,128)(2,1)S(1)} %layer_two.1.own_ref), channel_id=1, source_target_pairs={{0,8},{8,0},{1,9},{9,1},{2,10},{10,2},{3,11},{11,3},{4,12},{12,4},... | collective-permute-start | bytes 786440 | tf_op jit(solution)/shard_map/ppermute | solution.py:35
  126.9 16.1 %collective-permute-start.16 = (bf16[512,256]{1,0:T(8,128)(2,1)S(1)}, bf16[512,256]{1,0:T(8,128)(2,1)S(1)}, u32[]{:S(2)}, u32[]{:S(2)}) collective-permute-start(bf16[512,256]{1,0:T(8,128)(2,1)S(1)} %layer_two.1.own_ref), channel_id=1, source_target_pairs={{0,32},{16,48},{32,0},{48,16},{64,96},{80,112},{96,64},{112,80},{1... | collective-permute-start | bytes 786440 | tf_op jit(solution)/shard_map/ppermute | solution.py:35
  130.5 13.9 %collective-permute-start.17 = (bf16[512,256]{1,0:T(8,128)(2,1)S(1)}, bf16[512,256]{1,0:T(8,128)(2,1)S(1)}, u32[]{:S(2)}, u32[]{:S(2)}) collective-permute-start(bf16[512,256]{1,0:T(8,128)(2,1)S(1)} %layer_two.1.own_ref), channel_id=1, source_target_pairs={{0,16},{16,0},{32,48},{48,32},{64,80},{80,64},{96,112},{112,96},{1... | collective-permute-start | bytes 786440 | tf_op jit(solution)/shard_map/ppermute | solution.py:35
Sparse Core Ops, SparseCore 0:
  34.6 74.5 all-gather.3

commit v5 on v4

--- a/solution.py
+++ b/solution.py
@@ -153,9 +153,9 @@
         name="squares_two",
     )(*two_blocks)
     two_blocks += [from_core(block) for block in two_blocks]
-    x_first, two_far = lax.optimization_barrier((x_one, two_far))
-    one_near, one_far = from_line(x_first, 1), from_line(x_first, 2)
-    one_near, one_far = lax.optimization_barrier((one_near, one_far))
+    one_far = from_line(x_one, 2)
+    x_first, two_near = lax.optimization_barrier((x_one, two_near))
+    one_near = from_line(x_first, 1)
     one_last = from_line(one_far, 1)
     place = jnp.stack([l, c, lengths[0], pair_bit, is_old]).astype(jnp.int32)
 

time: 154 us -> 154 us (level)
  starting transfers between devices: 61.1 us -> 63.7 us
  local copies, waits for them, and re-layouts: 11 us -> 9.05 us
    ppermute x18, waiting for transfers between devices: 43.1 us -> 35.7 us  [move(): return lax.ppermute(value, axes, pairs)]
    all_gather x1, waiting for transfers between devices: 0.01 us -> 6.14 us  [on_device(): weights = lax.all_gather(lax.all_gather(weights, 'x'), 'z')]
    ppermute x18, starting transfers between devices: 61.1 us -> 63.7 us  [move(): return lax.ppermute(value, axes, pairs)]
    unnamed x26 -> x22, local copies, waits for them, and re-layouts: 9.36 us -> 7.42 us
  transfers between devices with their start and end apart: 19 -> 19, of which waited for: 6 -> 7; matrix products, arithmetic and copies ran while one was open for 0% -> 0% of each run, Pallas kernels for 5% -> 5%
where the time goes in v5:
time: 154 us; the launch traced here: 153 us
  starting transfers between devices  63.7 us (41%)
  waiting for transfers between devices  41.9 us (27%)
  between operations  16.3 us (11%)
  blocking collectives  11.7 us (8%)
  Pallas kernels  9.27 us (6%)
  local copies, waits for them, and re-layouts  9.05 us (6%)
    ppermute x18, starting transfers between devices, move(): return lax.ppermute(value, axes, pairs)  63.7 us
    ppermute x18, waiting for transfers between devices, move(): return lax.ppermute(value, axes, pairs)  35.7 us
    all_gather x1, blocking collectives, on_device(): weights = lax.all_gather(lax.all_gather(weights, 'x'), 'z')  11.7 us
    unnamed x22, local copies, waits for them, and re-layouts  7.42 us
    all_gather x1, waiting for transfers between devices, on_device(): weights = lax.all_gather(lax.all_gather(weights, 'x'), 'z')  6.14 us
    pallas_call x1, Pallas kernels, on_device(): pl.pallas_call(one_kernel, out_shape=(jax.ShapeDtypeStruct((rows, HD), jn...  4.46 us
  transfers between devices with their start and end apart: 19, of which 7 were waited for; matrix products, arithmetic and copies ran while one was open for 0% of the time, Pallas kernels for 5%

profile of v5, /device:TPU:1, one launch (start us, length us, event | category | flops | bytes accessed | tf_op | source)
XLA Modules:
  0.0 152.9 jit_solution(2105207591780963571)
XLA Ops:
  9.7 8.3 %collective-permute-start.10 = (bf16[2,80,256]{2,1,0:T(8,128)(2,1)S(1)}, bf16[2,80,256]{2,1,0:T(8,128)(2,1)S(1)}, u32[]{:S(2)}, u32[]{:S(2)}) collective-permute-start(bf16[2,80,256]{2,1,0:T(8,128)(2,1)S(1)} %pad_maximum_fusion.1), channel_id=1, source_target_pairs={{0,8},{8,0},{1,9},{9,1},{2,10},{10,2},{3,11},{11,3},{4,12},{12,4},... | collective-permute-start | bytes 245768 | tf_op jit(solution)/shard_map/ppermute | solution.py:35
  18.0 2.4 %collective-permute-start.4 = (bf16[512,640]{1,0:T(8,128)(2,1)}, bf16[512,640]{1,0:T(8,128)(2,1)S(1)}, u32[]{:S(2)}, u32[]{:S(2)}) collective-permute-start(bf16[512,640]{1,0:T(8,128)(2,1)} %refs_0_.4), channel_id=1, source_target_pairs={{0,4},{2,6},{4,0},{6,2},{1,5},{3,7},{5,1},{7,3},{8,12},{10,14},{12... | collective-permute-start | bytes 1966088 | tf_op jit(solution)/shard_map/ppermute | solution.py:35
  20.4 2.3 %collective-permute-start = (bf16[512,640]{1,0:T(8,128)(2,1)}, bf16[512,640]{1,0:T(8,128)(2,1)S(1)}, u32[]{:S(2)}, u32[]{:S(2)}) collective-permute-start(bf16[512,640]{1,0:T(8,128)(2,1)} %refs_0_.4), channel_id=1, source_target_pairs={{0,2},{2,0},{4,6},{6,4},{1,3},{3,1},{5,7},{7,5},{8,10},{10,8},{12,... | collective-permute-start | bytes 1966088 | tf_op jit(solution)/shard_map/ppermute | solution.py:35
  22.8 11.7 %all-gather = bf16[8,160,256]{2,1,0:T(8,128)(2,1)} all-gather(bf16[2,160,256]{2,1,0:T(8,128)(2,1)S(1)} %pad_maximum_fusion), channel_id=2, replica_groups=mesh['x'=4,'z'=8,'h'=2,'l'=4,'c'=2] {'x'}, dimensions={0}, use_global_device_ids=true | all-gather | bytes 819200 | tf_op jit(solution)/shard_map/all_gather | solution.py:135
  34.5 9.7 %collective-permute-start.6 = (bf16[512,640]{1,0:T(8,128)(2,1)}, bf16[512,640]{1,0:T(8,128)(2,1)S(1)}, u32[]{:S(2)}, u32[]{:S(2)}) collective-permute-start(bf16[512,640]{1,0:T(8,128)(2,1)} %refs_0_.4), channel_id=1, source_target_pairs={{0,1},{1,0},{2,3},{3,2},{4,5},{5,4},{6,7},{7,6},{8,9},{9,8},{10,11... | collective-permute-start | bytes 1966088 | tf_op jit(solution)/shard_map/ppermute | solution.py:35
  44.2 1.9 %collective-permute-start.2 = (bf16[512,640]{1,0:T(8,128)(2,1)}, bf16[512,640]{1,0:T(8,128)(2,1)}, u32[]{:S(2)}, u32[]{:S(2)}) collective-permute-start(bf16[512,640]{1,0:T(8,128)(2,1)} %refs_0_.5), channel_id=1, source_target_pairs={{0,4},{2,6},{4,0},{6,2},{1,5},{3,7},{5,1},{7,3},{8,12},{10,14},{12... | collective-permute-start | bytes 1966088 | tf_op jit(solution)/shard_map/ppermute | solution.py:35
  46.1 6.6 %collective-permute-done.4.refs_2_ = bf16[512,640]{1,0:T(8,128)(2,1)S(1)} collective-permute-done((bf16[512,640]{1,0:T(8,128)(2,1)}, bf16[512,640]{1,0:T(8,128)(2,1)S(1)}, u32[]{:S(2)}, u32[]{:S(2)}) %collective-permute-start.4) | collective-permute-done | bytes 655392 | tf_op jit(solution)/shard_map/ppermute | solution.py:35
  52.7 1.9 %collective-permute-start.5 = (bf16[512,640]{1,0:T(8,128)(2,1)S(1)}, bf16[512,640]{1,0:T(8,128)(2,1)S(1)}, u32[]{:S(2)}, u32[]{:S(2)}) collective-permute-start(bf16[512,640]{1,0:T(8,128)(2,1)S(1)} %collective-permute-done.4.refs_2_), channel_id=1, source_target_pairs={{0,2},{2,0},{4,6},{6,4},{1,3},{3,1},{5,7},{7,5},{8,10},{10,8},{12,... | collective-permute-start | bytes 1966088 | tf_op jit(solution)/shard_map/ppermute | solution.py:35
  54.6 3.1 %collective-permute-start.7 = (bf16[512,640]{1,0:T(8,128)(2,1)S(1)}, bf16[512,640]{1,0:T(8,128)(2,1)S(1)}, u32[]{:S(2)}, u32[]{:S(2)}) collective-permute-start(bf16[512,640]{1,0:T(8,128)(2,1)S(1)} %collective-permute-done.refs_1_), channel_id=1, source_target_pairs={{0,1},{1,0},{2,3},{3,2},{4,5},{5,4},{6,7},{7,6},{8,9},{9,8},{10,11... | collective-permute-start | bytes 1966088 | tf_op jit(solution)/shard_map/ppermute | solution.py:35
  57.7 1.9 %collective-permute-start.8 = (bf16[512,640]{1,0:T(8,128)(2,1)S(1)}, bf16[512,640]{1,0:T(8,128)(2,1)}, u32[]{:S(2)}, u32[]{:S(2)}) collective-permute-start(bf16[512,640]{1,0:T(8,128)(2,1)S(1)} %collective-permute-done.4.refs_2_), channel_id=1, source_target_pairs={{0,1},{1,0},{2,3},{3,2},{4,5},{5,4},{6,7},{7,6},{8,9},{9,8},{10,11... | collective-permute-start | bytes 1966088 | tf_op jit(solution)/shard_map/ppermute | solution.py:35
  61.7 2.4 %collective-permute-start.11 = (bf16[512,640]{1,0:T(8,128)(2,1)}, bf16[512,640]{1,0:T(8,128)(2,1)}, u32[]{:S(2)}, u32[]{:S(2)}) collective-permute-start(bf16[512,640]{1,0:T(8,128)(2,1)} %refs_0_.5), channel_id=1, source_target_pairs={{0,1},{1,0},{2,3},{3,2},{4,5},{5,4},{6,7},{7,6},{8,9},{9,8},{10,11... | collective-permute-start | bytes 1966088 | tf_op jit(solution)/shard_map/ppermute | solution.py:35
  64.1 15.8 %collective-permute-done.2.refs_2_ = bf16[512,640]{1,0:T(8,128)(2,1)} collective-permute-done((bf16[512,640]{1,0:T(8,128)(2,1)}, bf16[512,640]{1,0:T(8,128)(2,1)}, u32[]{:S(2)}, u32[]{:S(2)}) %collective-permute-start.2) | collective-permute-done | bytes 655392 | tf_op jit(solution)/shard_map/ppermute | solution.py:35
  79.8 1.9 %collective-permute-start.1 = (bf16[512,640]{1,0:T(8,128)(2,1)}, bf16[512,640]{1,0:T(8,128)(2,1)}, u32[]{:S(2)}, u32[]{:S(2)}) collective-permute-start(bf16[512,640]{1,0:T(8,128)(2,1)} %refs_0_.5), channel_id=1, source_target_pairs={{0,2},{2,0},{4,6},{6,4},{1,3},{3,1},{5,7},{7,5},{8,10},{10,8},{12,... | collective-permute-start | bytes 1966088 | tf_op jit(solution)/shard_map/ppermute | solution.py:35
  81.8 1.8 %collective-permute-done.5.refs_3_ = bf16[512,640]{1,0:T(8,128)(2,1)S(1)} collective-permute-done((bf16[512,640]{1,0:T(8,128)(2,1)S(1)}, bf16[512,640]{1,0:T(8,128)(2,1)S(1)}, u32[]{:S(2)}, u32[]{:S(2)}) %collective-permute-start.5) | collective-permute-done | bytes 655392 | tf_op jit(solution)/shard_map/ppermute | solution.py:35
  83.6 1.9 %collective-permute-start.3 = (bf16[512,640]{1,0:T(8,128)(2,1)}, bf16[512,640]{1,0:T(8,128)(2,1)}, u32[]{:S(2)}, u32[]{:S(2)}) collective-permute-start(bf16[512,640]{1,0:T(8,128)(2,1)} %collective-permute-done.2.refs_2_), channel_id=1, source_target_pairs={{0,2},{2,0},{4,6},{6,4},{1,3},{3,1},{5,7},{7,5},{8,10},{10,8},{12,... | collective-permute-start | bytes 1966088 | tf_op jit(solution)/shard_map/ppermute | solution.py:35
  86.3 4.3 %collective-permute-start.13 = (bf16[512,640]{1,0:T(8,128)(2,1)}, bf16[512,640]{1,0:T(8,128)(2,1)}, u32[]{:S(2)}, u32[]{:S(2)}) collective-permute-start(bf16[512,640]{1,0:T(8,128)(2,1)} %collective-permute-done.2.refs_2_), channel_id=1, source_target_pairs={{0,1},{1,0},{2,3},{3,2},{4,5},{5,4},{6,7},{7,6},{8,9},{9,8},{10,11... | collective-permute-start | bytes 1966088 | tf_op jit(solution)/shard_map/ppermute | solution.py:35
  90.7 1.9 %collective-permute-start.9 = (bf16[512,640]{1,0:T(8,128)(2,1)S(1)}, bf16[512,640]{1,0:T(8,128)(2,1)S(1)}, u32[]{:S(2)}, u32[]{:S(2)}) collective-permute-start(bf16[512,640]{1,0:T(8,128)(2,1)S(1)} %collective-permute-done.5.refs_3_), channel_id=1, source_target_pairs={{0,1},{1,0},{2,3},{3,2},{4,5},{5,4},{6,7},{7,6},{8,9},{9,8},{10,11... | collective-permute-start | bytes 1966088 | tf_op jit(solution)/shard_map/ppermute | solution.py:35
  94.2 4.5 %collective-permute-done.1.refs_1_ = bf16[512,640]{1,0:T(8,128)(2,1)} collective-permute-done((bf16[512,640]{1,0:T(8,128)(2,1)}, bf16[512,640]{1,0:T(8,128)(2,1)}, u32[]{:S(2)}, u32[]{:S(2)}) %collective-permute-start.1) | collective-permute-done | bytes 655392 | tf_op jit(solution)/shard_map/ppermute | solution.py:35
  98.7 3.6 %collective-permute-start.12 = (bf16[512,640]{1,0:T(8,128)(2,1)}, bf16[512,640]{1,0:T(8,128)(2,1)}, u32[]{:S(2)}, u32[]{:S(2)}) collective-permute-start(bf16[512,640]{1,0:T(8,128)(2,1)} %collective-permute-done.1.refs_1_), channel_id=1, source_target_pairs={{0,1},{1,0},{2,3},{3,2},{4,5},{5,4},{6,7},{7,6},{8,9},{9,8},{10,11... | collective-permute-start | bytes 1966088 | tf_op jit(solution)/shard_map/ppermute | solution.py:35
  103.1 6.1 %all-gather.4.cloned.1.call-done = bf16[32,2,160,256]{3,2,1,0:T(8,128)(2,1)} async-done(((bf16[4,2,160,256]{3,2,1,0:T(8,128)(2,1)}), bf16[32,2,160,256]{3,2,1,0:T(8,128)(2,1)}) %all-gather.4.cloned.1.call-update) | async-done | bytes 5242896 | tf_op jit(solution)/shard_map/all_gather | solution.py:135
  109.2 2.5 %copy-done = bf16[32,2,160,256]{3,2,1,0:T(8,128)(2,1)S(1)} copy-done((bf16[32,2,160,256]{3,2,1,0:T(8,128)(2,1)S(1)}, bf16[32,2,160,256]{3,2,1,0:T(8,128)(2,1)}, u32[]{:S(2)}) %copy-start) | copy-done | bytes 5242904
  111.7 1.1 copy-done.5
  112.8 1.1 copy-done.7
  113.9 2.9 %layer_two.1.own_ref = bf16[512,256]{1,0:T(8,128)(2,1)S(1)} custom-call(s32[5]{0:T(128)S(1)} %stack.21.place, bf16[512,640]{1,0:T(8,128)(2,1)S(1)} %copy-done.3, bf16[512,640]{1,0:T(8,128)(2,1)S(1)} %collective-permute-done.refs_1_, bf16[512,640]{1,0:T(8,128)(2,1)S(1)} %collective-permute-done.4.refs_2_, ...), custom_call_target="tpu_custom_call" | custom-call | flops 1342177280 | bytes 7864320 | tf_op jit(solution)/shard_map/layer_two/pallas_call | solution.py:165
  116.8 2.6 %collective-permute-start.14 = (bf16[512,640]{1,0:T(8,128)(2,1)}, bf16[512,640]{1,0:T(8,128)(2,1)S(1)}, u32[]{:S(2)}, u32[]{:S(2)}) collective-permute-start(bf16[512,640]{1,0:T(8,128)(2,1)} %collective-permute-done.3.refs_3_), channel_id=1, source_target_pairs={{0,1},{1,0},{2,3},{3,2},{4,5},{5,4},{6,7},{7,6},{8,9},{9,8},{10,11... | collective-permute-start | bytes 1966088 | tf_op jit(solution)/shard_map/ppermute | solution.py:35
  119.4 7.1 %collective-permute-start.15 = (bf16[512,256]{1,0:T(8,128)(2,1)S(1)}, bf16[512,256]{1,0:T(8,128)(2,1)S(1)}, u32[]{:S(2)}, u32[]{:S(2)}) collective-permute-start(bf16[512,256]{1,0:T(8,128)(2,1)S(1)} %layer_two.1.own_ref), channel_id=1, source_target_pairs={{0,8},{8,0},{1,9},{9,1},{2,10},{10,2},{3,11},{11,3},{4,12},{12,4},... | collective-permute-start | bytes 786440 | tf_op jit(solution)/shard_map/ppermute | solution.py:35
  126.5 2.0 %collective-permute-start.16 = (bf16[512,256]{1,0:T(8,128)(2,1)S(1)}, bf16[512,256]{1,0:T(8,128)(2,1)S(1)}, u32[]{:S(2)}, u32[]{:S(2)}) collective-permute-start(bf16[512,256]{1,0:T(8,128)(2,1)S(1)} %layer_two.1.own_ref), channel_id=1, source_target_pairs={{0,32},{16,48},{32,0},{48,16},{64,96},{80,112},{96,64},{112,80},{1... | collective-permute-start | bytes 786440 | tf_op jit(solution)/shard_map/ppermute | solution.py:35
  128.5 4.5 %collective-permute-start.17 = (bf16[512,256]{1,0:T(8,128)(2,1)S(1)}, bf16[512,256]{1,0:T(8,128)(2,1)S(1)}, u32[]{:S(2)}, u32[]{:S(2)}) collective-permute-start(bf16[512,256]{1,0:T(8,128)(2,1)S(1)} %layer_two.1.own_ref), channel_id=1, source_target_pairs={{0,16},{16,0},{32,48},{48,32},{64,80},{80,64},{96,112},{112,96},{1... | collective-permute-start | bytes 786440 | tf_op jit(solution)/shard_map/ppermute | solution.py:35
  133.1 4.5 %layer_one.1 = (bf16[512,128]{1,0:T(8,128)(2,1)}, bf16[512,128]{1,0:T(8,128)(2,1)}) custom-call(s32[5]{0:T(128)S(1)} %stack.21.place, bf16[512,640]{1,0:T(8,128)(2,1)S(1)} %copy-done.8, bf16[512,640]{1,0:T(8,128)(2,1)} %collective-permute-done.1.refs_1_, bf16[512,640]{1,0:T(8,128)(2,1)} %collective-permute-done.2.refs_2_, ...), custom_call_target="tpu_custom_call" | custom-call | flops 1342177280 | bytes 7864320 | tf_op jit(solution)/shard_map/layer_one/pallas_call | solution.py:183
  137.5 5.6 %collective-permute-done.16.refs_1_ = bf16[512,256]{1,0:T(8,128)(2,1)S(1)} collective-permute-done((bf16[512,256]{1,0:T(8,128)(2,1)S(1)}, bf16[512,256]{1,0:T(8,128)(2,1)S(1)}, u32[]{:S(2)}, u32[]{:S(2)}) %collective-permute-start.16) | collective-permute-done | bytes 262176 | tf_op jit(solution)/shard_map/ppermute | solution.py:35
  143.1 1.5 collective-permute-done.17.refs_2_
  144.6 1.4 finish_two.1
  (41 shorter events, 5.9 us)
Async XLA Ops:
  7.2 102.1 %all-gather.4.cloned.1.call-start = ((), (), s32[]{:S(2)}) async-start(), calls=%async_computation | async-start | bytes 5898240 | tf_op jit(solution)/shard_map/all_gather | solution.py:135
  9.7 13.0 %collective-permute-start.10 = (bf16[2,80,256]{2,1,0:T(8,128)(2,1)S(1)}, bf16[2,80,256]{2,1,0:T(8,128)(2,1)S(1)}, u32[]{:S(2)}, u32[]{:S(2)}) collective-permute-start(bf16[2,80,256]{2,1,0:T(8,128)(2,1)S(1)} %pad_maximum_fusion.1), channel_id=1, source_target_pairs={{0,8},{8,0},{1,9},{9,1},{2,10},{10,2},{3,11},{11,3},{4,12},{12,4},... | collective-permute-start | bytes 245768 | tf_op jit(solution)/shard_map/ppermute | solution.py:35
  18.0 34.7 %collective-permute-start.4 = (bf16[512,640]{1,0:T(8,128)(2,1)}, bf16[512,640]{1,0:T(8,128)(2,1)S(1)}, u32[]{:S(2)}, u32[]{:S(2)}) collective-permute-start(bf16[512,640]{1,0:T(8,128)(2,1)} %refs_0_.4), channel_id=1, source_target_pairs={{0,4},{2,6},{4,0},{6,2},{1,5},{3,7},{5,1},{7,3},{8,12},{10,14},{12... | collective-permute-start | bytes 1966088 | tf_op jit(solution)/shard_map/ppermute | solution.py:35
  20.4 34.2 %collective-permute-start = (bf16[512,640]{1,0:T(8,128)(2,1)}, bf16[512,640]{1,0:T(8,128)(2,1)S(1)}, u32[]{:S(2)}, u32[]{:S(2)}) collective-permute-start(bf16[512,640]{1,0:T(8,128)(2,1)} %refs_0_.4), channel_id=1, source_target_pairs={{0,2},{2,0},{4,6},{6,4},{1,3},{3,1},{5,7},{7,5},{8,10},{10,8},{12,... | collective-permute-start | bytes 1966088 | tf_op jit(solution)/shard_map/ppermute | solution.py:35
  34.5 27.2 %collective-permute-start.6 = (bf16[512,640]{1,0:T(8,128)(2,1)}, bf16[512,640]{1,0:T(8,128)(2,1)S(1)}, u32[]{:S(2)}, u32[]{:S(2)}) collective-permute-start(bf16[512,640]{1,0:T(8,128)(2,1)} %refs_0_.4), channel_id=1, source_target_pairs={{0,1},{1,0},{2,3},{3,2},{4,5},{5,4},{6,7},{7,6},{8,9},{9,8},{10,11... | collective-permute-start | bytes 1966088 | tf_op jit(solution)/shard_map/ppermute | solution.py:35
  44.2 35.7 %collective-permute-start.2 = (bf16[512,640]{1,0:T(8,128)(2,1)}, bf16[512,640]{1,0:T(8,128)(2,1)}, u32[]{:S(2)}, u32[]{:S(2)}) collective-permute-start(bf16[512,640]{1,0:T(8,128)(2,1)} %refs_0_.5), channel_id=1, source_target_pairs={{0,4},{2,6},{4,0},{6,2},{1,5},{3,7},{5,1},{7,3},{8,12},{10,14},{12... | collective-permute-start | bytes 1966088 | tf_op jit(solution)/shard_map/ppermute | solution.py:35
  52.7 30.9 %collective-permute-start.5 = (bf16[512,640]{1,0:T(8,128)(2,1)S(1)}, bf16[512,640]{1,0:T(8,128)(2,1)S(1)}, u32[]{:S(2)}, u32[]{:S(2)}) collective-permute-start(bf16[512,640]{1,0:T(8,128)(2,1)S(1)} %collective-permute-done.4.refs_2_), channel_id=1, source_target_pairs={{0,2},{2,0},{4,6},{6,4},{1,3},{3,1},{5,7},{7,5},{8,10},{10,8},{12,... | collective-permute-start | bytes 1966088 | tf_op jit(solution)/shard_map/ppermute | solution.py:35
  54.6 30.9 %collective-permute-start.7 = (bf16[512,640]{1,0:T(8,128)(2,1)S(1)}, bf16[512,640]{1,0:T(8,128)(2,1)S(1)}, u32[]{:S(2)}, u32[]{:S(2)}) collective-permute-start(bf16[512,640]{1,0:T(8,128)(2,1)S(1)} %collective-permute-done.refs_1_), channel_id=1, source_target_pairs={{0,1},{1,0},{2,3},{3,2},{4,5},{5,4},{6,7},{7,6},{8,9},{9,8},{10,11... | collective-permute-start | bytes 1966088 | tf_op jit(solution)/shard_map/ppermute | solution.py:35
  57.7 33.0 %collective-permute-start.8 = (bf16[512,640]{1,0:T(8,128)(2,1)S(1)}, bf16[512,640]{1,0:T(8,128)(2,1)}, u32[]{:S(2)}, u32[]{:S(2)}) collective-permute-start(bf16[512,640]{1,0:T(8,128)(2,1)S(1)} %collective-permute-done.4.refs_2_), channel_id=1, source_target_pairs={{0,1},{1,0},{2,3},{3,2},{4,5},{5,4},{6,7},{7,6},{8,9},{9,8},{10,11... | collective-permute-start | bytes 1966088 | tf_op jit(solution)/shard_map/ppermute | solution.py:35
  61.6 47.7 %copy-start.9 = (f32[128]{0:T(128)S(1)}, f32[128]{0:T(128)}, u32[]{:S(2)}) copy-start(f32[128]{0:T(128)} %param.18) | copy-start | bytes 1540
  61.7 64.8 %collective-permute-start.11 = (bf16[512,640]{1,0:T(8,128)(2,1)}, bf16[512,640]{1,0:T(8,128)(2,1)}, u32[]{:S(2)}, u32[]{:S(2)}) collective-permute-start(bf16[512,640]{1,0:T(8,128)(2,1)} %refs_0_.5), channel_id=1, source_target_pairs={{0,1},{1,0},{2,3},{3,2},{4,5},{5,4},{6,7},{7,6},{8,9},{9,8},{10,11... | collective-permute-start | bytes 1966088 | tf_op jit(solution)/shard_map/ppermute | solution.py:35
  79.8 18.8 %collective-permute-start.1 = (bf16[512,640]{1,0:T(8,128)(2,1)}, bf16[512,640]{1,0:T(8,128)(2,1)}, u32[]{:S(2)}, u32[]{:S(2)}) collective-permute-start(bf16[512,640]{1,0:T(8,128)(2,1)} %refs_0_.5), channel_id=1, source_target_pairs={{0,2},{2,0},{4,6},{6,4},{1,3},{3,1},{5,7},{7,5},{8,10},{10,8},{12,... | collective-permute-start | bytes 1966088 | tf_op jit(solution)/shard_map/ppermute | solution.py:35
  83.6 33.2 %collective-permute-start.3 = (bf16[512,640]{1,0:T(8,128)(2,1)}, bf16[512,640]{1,0:T(8,128)(2,1)}, u32[]{:S(2)}, u32[]{:S(2)}) collective-permute-start(bf16[512,640]{1,0:T(8,128)(2,1)} %collective-permute-done.2.refs_2_), channel_id=1, source_target_pairs={{0,2},{2,0},{4,6},{6,4},{1,3},{3,1},{5,7},{7,5},{8,10},{10,8},{12,... | collective-permute-start | bytes 1966088 | tf_op jit(solution)/shard_map/ppermute | solution.py:35
  85.5 0.8 copy-start.4
  86.3 42.2 %collective-permute-start.13 = (bf16[512,640]{1,0:T(8,128)(2,1)}, bf16[512,640]{1,0:T(8,128)(2,1)}, u32[]{:S(2)}, u32[]{:S(2)}) collective-permute-start(bf16[512,640]{1,0:T(8,128)(2,1)} %collective-permute-done.2.refs_2_), channel_id=1, source_target_pairs={{0,1},{1,0},{2,3},{3,2},{4,5},{5,4},{6,7},{7,6},{8,9},{9,8},{10,11... | collective-permute-start | bytes 1966088 | tf_op jit(solution)/shard_map/ppermute | solution.py:35
  90.7 11.6 %collective-permute-start.9 = (bf16[512,640]{1,0:T(8,128)(2,1)S(1)}, bf16[512,640]{1,0:T(8,128)(2,1)S(1)}, u32[]{:S(2)}, u32[]{:S(2)}) collective-permute-start(bf16[512,640]{1,0:T(8,128)(2,1)S(1)} %collective-permute-done.5.refs_3_), channel_id=1, source_target_pairs={{0,1},{1,0},{2,3},{3,2},{4,5},{5,4},{6,7},{7,6},{8,9},{9,8},{10,11... | collective-permute-start | bytes 1966088 | tf_op jit(solution)/shard_map/ppermute | solution.py:35
  92.6 1.1 copy-start.2
  93.7 15.5 %copy-start.3 = (bf16[512,640]{1,0:T(8,128)(2,1)S(1)}, bf16[512,640]{1,0:T(8,128)(2,1)}, u32[]{:S(2)}) copy-start(bf16[512,640]{1,0:T(8,128)(2,1)} %refs_0_.4) | copy-start | bytes 1966084
  98.7 34.4 %collective-permute-start.12 = (bf16[512,640]{1,0:T(8,128)(2,1)}, bf16[512,640]{1,0:T(8,128)(2,1)}, u32[]{:S(2)}, u32[]{:S(2)}) collective-permute-start(bf16[512,640]{1,0:T(8,128)(2,1)} %collective-permute-done.1.refs_1_), channel_id=1, source_target_pairs={{0,1},{1,0},{2,3},{3,2},{4,5},{5,4},{6,7},{7,6},{8,9},{9,8},{10,11... | collective-permute-start | bytes 1966088 | tf_op jit(solution)/shard_map/ppermute | solution.py:35
  102.2 0.8 copy-start.6
  109.2 2.5 %copy-start = (bf16[32,2,160,256]{3,2,1,0:T(8,128)(2,1)S(1)}, bf16[32,2,160,256]{3,2,1,0:T(8,128)(2,1)}, u32[]{:S(2)}) copy-start(bf16[32,2,160,256]{3,2,1,0:T(8,128)(2,1)} %all-gather.4.cloned.1.call-done) | copy-start | bytes 15728644
  111.7 1.1 copy-start.5
  112.8 1.1 copy-start.7
  113.9 19.1 %copy-start.1 = (bf16[32,2,160,256]{3,2,1,0:T(8,128)(2,1)S(1)}, bf16[32,2,160,256]{3,2,1,0:T(8,128)(2,1)}, u32[]{:S(2)}) copy-start(bf16[32,2,160,256]{3,2,1,0:T(8,128)(2,1)} %all-gather.4.cloned.1.call-done) | copy-start | bytes 15728644
  113.9 19.2 %copy-start.8 = (bf16[512,640]{1,0:T(8,128)(2,1)S(1)}, bf16[512,640]{1,0:T(8,128)(2,1)}, u32[]{:S(2)}) copy-start(bf16[512,640]{1,0:T(8,128)(2,1)} %refs_0_.5) | copy-start | bytes 1966084
  113.9 19.2 %copy-start.10 = (f32[128]{0:T(128)S(1)}, f32[128]{0:T(128)}, u32[]{:S(2)}) copy-start(f32[128]{0:T(128)} %param.17) | copy-start | bytes 1540
  116.8 16.2 %collective-permute-start.14 = (bf16[512,640]{1,0:T(8,128)(2,1)}, bf16[512,640]{1,0:T(8,128)(2,1)S(1)}, u32[]{:S(2)}, u32[]{:S(2)}) collective-permute-start(bf16[512,640]{1,0:T(8,128)(2,1)} %collective-permute-done.3.refs_3_), channel_id=1, source_target_pairs={{0,1},{1,0},{2,3},{3,2},{4,5},{5,4},{6,7},{7,6},{8,9},{9,8},{10,11... | collective-permute-start | bytes 1966088 | tf_op jit(solution)/shard_map/ppermute | solution.py:35
  119.4 18.2 %collective-permute-start.15 = (bf16[512,256]{1,0:T(8,128)(2,1)S(1)}, bf16[512,256]{1,0:T(8,128)(2,1)S(1)}, u32[]{:S(2)}, u32[]{:S(2)}) collective-permute-start(bf16[512,256]{1,0:T(8,128)(2,1)S(1)} %layer_two.1.own_ref), channel_id=1, source_target_pairs={{0,8},{8,0},{1,9},{9,1},{2,10},{10,2},{3,11},{11,3},{4,12},{12,4},... | collective-permute-start | bytes 786440 | tf_op jit(solution)/shard_map/ppermute | solution.py:35
  126.5 16.6 %collective-permute-start.16 = (bf16[512,256]{1,0:T(8,128)(2,1)S(1)}, bf16[512,256]{1,0:T(8,128)(2,1)S(1)}, u32[]{:S(2)}, u32[]{:S(2)}) collective-permute-start(bf16[512,256]{1,0:T(8,128)(2,1)S(1)} %layer_two.1.own_ref), channel_id=1, source_target_pairs={{0,32},{16,48},{32,0},{48,16},{64,96},{80,112},{96,64},{112,80},{1... | collective-permute-start | bytes 786440 | tf_op jit(solution)/shard_map/ppermute | solution.py:35
  128.5 16.1 %collective-permute-start.17 = (bf16[512,256]{1,0:T(8,128)(2,1)S(1)}, bf16[512,256]{1,0:T(8,128)(2,1)S(1)}, u32[]{:S(2)}, u32[]{:S(2)}) collective-permute-start(bf16[512,256]{1,0:T(8,128)(2,1)S(1)} %layer_two.1.own_ref), channel_id=1, source_target_pairs={{0,16},{16,0},{32,48},{48,32},{64,80},{80,64},{96,112},{112,96},{1... | collective-permute-start | bytes 786440 | tf_op jit(solution)/shard_map/ppermute | solution.py:35
Sparse Core Ops, SparseCore 0:
  34.6 74.5 all-gather.3

commit v6 on v5

--- a/solution.py
+++ b/solution.py
@@ -88,7 +88,7 @@
     rows = own_ref.shape[0]
     pair_bit, is_old = place[3], place[4] == 1
     own = own_ref[...]
-    received = jnp.where(pair_bit == 1, swap_refs[0][...], swap_refs[1][...])
+    received = jnp.where(pair_bit == 1, swap_refs[1][...], swap_refs[0][...])
     received = jnp.where(pair_bit == 2, swap_refs[2][...], received)
     for first, part in ((0, own), (rows, received)):
         part = jnp.where(is_old, part, jnp.zeros_like(part))
@@ -172,8 +172,8 @@
         name="layer_two",
     )(place, *two_blocks, weights, key_gain_two.reshape(1, HD), squares_two)
     swaps = [
+        move(both_two, ("z",), lambda z: (z ^ 2,)),
         move(both_two, ("h",), lambda h: (h ^ 1,)),
-        move(both_two, ("z",), lambda z: (z ^ 2,)),
         move(both_two, ("z",), lambda z: (z ^ 1,)),
     ]
 

time: 154 us -> 151 us (0.981)
  waiting for transfers between devices: 41.9 us -> 38.9 us
    ppermute x18, waiting for transfers between devices: 35.7 us -> 32.8 us  [move(): return lax.ppermute(value, axes, pairs)]
  transfers between devices with their start and end apart: 19 -> 19, of which waited for: 7 -> 6; matrix products, arithmetic and copies ran while one was open for 0% -> 0% of each run, Pallas kernels for 5% -> 5%
where the time goes in v6:
time: 151 us; the launch traced here: 150 us
  starting transfers between devices  63.7 us (42%)
  waiting for transfers between devices  38.9 us (26%)
  between operations  16.3 us (11%)
  blocking collectives  11.7 us (8%)
  Pallas kernels  9.27 us (6%)
  local copies, waits for them, and re-layouts  9.05 us (6%)
    ppermute x18, starting transfers between devices, move(): return lax.ppermute(value, axes, pairs)  63.7 us
    ppermute x18, waiting for transfers between devices, move(): return lax.ppermute(value, axes, pairs)  32.8 us
    all_gather x1, blocking collectives, on_device(): weights = lax.all_gather(lax.all_gather(weights, 'x'), 'z')  11.7 us
    unnamed x22, local copies, waits for them, and re-layouts  7.42 us
    all_gather x1, waiting for transfers between devices, on_device(): weights = lax.all_gather(lax.all_gather(weights, 'x'), 'z')  6.14 us
    pallas_call x1, Pallas kernels, on_device(): pl.pallas_call(one_kernel, out_shape=(jax.ShapeDtypeStruct((rows, HD), jn...  4.46 us
  transfers between devices with their start and end apart: 19, of which 6 were waited for; matrix products, arithmetic and copies ran while one was open for 0% of the time, Pallas kernels for 5%

profile of v6, /device:TPU:1, one launch (start us, length us, event | category | flops | bytes accessed | tf_op | source)
XLA Modules:
  0.0 149.9 jit_solution(9791811465103032235)
XLA Ops:
  9.7 8.3 %collective-permute-start.10 = (bf16[2,80,256]{2,1,0:T(8,128)(2,1)S(1)}, bf16[2,80,256]{2,1,0:T(8,128)(2,1)S(1)}, u32[]{:S(2)}, u32[]{:S(2)}) collective-permute-start(bf16[2,80,256]{2,1,0:T(8,128)(2,1)S(1)} %pad_maximum_fusion.1), channel_id=1, source_target_pairs={{0,8},{8,0},{1,9},{9,1},{2,10},{10,2},{3,11},{11,3},{4,12},{12,4},... | collective-permute-start | bytes 245768 | tf_op jit(solution)/shard_map/ppermute | solution.py:35
  18.0 2.4 %collective-permute-start.4 = (bf16[512,640]{1,0:T(8,128)(2,1)}, bf16[512,640]{1,0:T(8,128)(2,1)S(1)}, u32[]{:S(2)}, u32[]{:S(2)}) collective-permute-start(bf16[512,640]{1,0:T(8,128)(2,1)} %refs_0_.4), channel_id=1, source_target_pairs={{0,4},{2,6},{4,0},{6,2},{1,5},{3,7},{5,1},{7,3},{8,12},{10,14},{12... | collective-permute-start | bytes 1966088 | tf_op jit(solution)/shard_map/ppermute | solution.py:35
  20.4 2.3 %collective-permute-start = (bf16[512,640]{1,0:T(8,128)(2,1)}, bf16[512,640]{1,0:T(8,128)(2,1)S(1)}, u32[]{:S(2)}, u32[]{:S(2)}) collective-permute-start(bf16[512,640]{1,0:T(8,128)(2,1)} %refs_0_.4), channel_id=1, source_target_pairs={{0,2},{2,0},{4,6},{6,4},{1,3},{3,1},{5,7},{7,5},{8,10},{10,8},{12,... | collective-permute-start | bytes 1966088 | tf_op jit(solution)/shard_map/ppermute | solution.py:35
  22.8 11.7 %all-gather = bf16[8,160,256]{2,1,0:T(8,128)(2,1)} all-gather(bf16[2,160,256]{2,1,0:T(8,128)(2,1)S(1)} %pad_maximum_fusion), channel_id=2, replica_groups=mesh['x'=4,'z'=8,'h'=2,'l'=4,'c'=2] {'x'}, dimensions={0}, use_global_device_ids=true | all-gather | bytes 819200 | tf_op jit(solution)/shard_map/all_gather | solution.py:135
  34.5 9.7 %collective-permute-start.6 = (bf16[512,640]{1,0:T(8,128)(2,1)}, bf16[512,640]{1,0:T(8,128)(2,1)S(1)}, u32[]{:S(2)}, u32[]{:S(2)}) collective-permute-start(bf16[512,640]{1,0:T(8,128)(2,1)} %refs_0_.4), channel_id=1, source_target_pairs={{0,1},{1,0},{2,3},{3,2},{4,5},{5,4},{6,7},{7,6},{8,9},{9,8},{10,11... | collective-permute-start | bytes 1966088 | tf_op jit(solution)/shard_map/ppermute | solution.py:35
  44.2 1.9 %collective-permute-start.2 = (bf16[512,640]{1,0:T(8,128)(2,1)}, bf16[512,640]{1,0:T(8,128)(2,1)}, u32[]{:S(2)}, u32[]{:S(2)}) collective-permute-start(bf16[512,640]{1,0:T(8,128)(2,1)} %refs_0_.5), channel_id=1, source_target_pairs={{0,4},{2,6},{4,0},{6,2},{1,5},{3,7},{5,1},{7,3},{8,12},{10,14},{12... | collective-permute-start | bytes 1966088 | tf_op jit(solution)/shard_map/ppermute | solution.py:35
  46.1 6.6 %collective-permute-done.4.refs_2_ = bf16[512,640]{1,0:T(8,128)(2,1)S(1)} collective-permute-done((bf16[512,640]{1,0:T(8,128)(2,1)}, bf16[512,640]{1,0:T(8,128)(2,1)S(1)}, u32[]{:S(2)}, u32[]{:S(2)}) %collective-permute-start.4) | collective-permute-done | bytes 655392 | tf_op jit(solution)/shard_map/ppermute | solution.py:35
  52.7 1.9 %collective-permute-start.5 = (bf16[512,640]{1,0:T(8,128)(2,1)S(1)}, bf16[512,640]{1,0:T(8,128)(2,1)S(1)}, u32[]{:S(2)}, u32[]{:S(2)}) collective-permute-start(bf16[512,640]{1,0:T(8,128)(2,1)S(1)} %collective-permute-done.4.refs_2_), channel_id=1, source_target_pairs={{0,2},{2,0},{4,6},{6,4},{1,3},{3,1},{5,7},{7,5},{8,10},{10,8},{12,... | collective-permute-start | bytes 1966088 | tf_op jit(solution)/shard_map/ppermute | solution.py:35
  54.6 3.1 %collective-permute-start.7 = (bf16[512,640]{1,0:T(8,128)(2,1)S(1)}, bf16[512,640]{1,0:T(8,128)(2,1)S(1)}, u32[]{:S(2)}, u32[]{:S(2)}) collective-permute-start(bf16[512,640]{1,0:T(8,128)(2,1)S(1)} %collective-permute-done.refs_1_), channel_id=1, source_target_pairs={{0,1},{1,0},{2,3},{3,2},{4,5},{5,4},{6,7},{7,6},{8,9},{9,8},{10,11... | collective-permute-start | bytes 1966088 | tf_op jit(solution)/shard_map/ppermute | solution.py:35
  57.7 1.9 %collective-permute-start.8 = (bf16[512,640]{1,0:T(8,128)(2,1)S(1)}, bf16[512,640]{1,0:T(8,128)(2,1)}, u32[]{:S(2)}, u32[]{:S(2)}) collective-permute-start(bf16[512,640]{1,0:T(8,128)(2,1)S(1)} %collective-permute-done.4.refs_2_), channel_id=1, source_target_pairs={{0,1},{1,0},{2,3},{3,2},{4,5},{5,4},{6,7},{7,6},{8,9},{9,8},{10,11... | collective-permute-start | bytes 1966088 | tf_op jit(solution)/shard_map/ppermute | solution.py:35
  61.7 2.4 %collective-permute-start.11 = (bf16[512,640]{1,0:T(8,128)(2,1)}, bf16[512,640]{1,0:T(8,128)(2,1)}, u32[]{:S(2)}, u32[]{:S(2)}) collective-permute-start(bf16[512,640]{1,0:T(8,128)(2,1)} %refs_0_.5), channel_id=1, source_target_pairs={{0,1},{1,0},{2,3},{3,2},{4,5},{5,4},{6,7},{7,6},{8,9},{9,8},{10,11... | collective-permute-start | bytes 1966088 | tf_op jit(solution)/shard_map/ppermute | solution.py:35
  64.1 15.8 %collective-permute-done.2.refs_2_ = bf16[512,640]{1,0:T(8,128)(2,1)} collective-permute-done((bf16[512,640]{1,0:T(8,128)(2,1)}, bf16[512,640]{1,0:T(8,128)(2,1)}, u32[]{:S(2)}, u32[]{:S(2)}) %collective-permute-start.2) | collective-permute-done | bytes 655392 | tf_op jit(solution)/shard_map/ppermute | solution.py:35
  79.8 1.9 %collective-permute-start.1 = (bf16[512,640]{1,0:T(8,128)(2,1)}, bf16[512,640]{1,0:T(8,128)(2,1)}, u32[]{:S(2)}, u32[]{:S(2)}) collective-permute-start(bf16[512,640]{1,0:T(8,128)(2,1)} %refs_0_.5), channel_id=1, source_target_pairs={{0,2},{2,0},{4,6},{6,4},{1,3},{3,1},{5,7},{7,5},{8,10},{10,8},{12,... | collective-permute-start | bytes 1966088 | tf_op jit(solution)/shard_map/ppermute | solution.py:35
  81.8 1.8 %collective-permute-done.5.refs_3_ = bf16[512,640]{1,0:T(8,128)(2,1)S(1)} collective-permute-done((bf16[512,640]{1,0:T(8,128)(2,1)S(1)}, bf16[512,640]{1,0:T(8,128)(2,1)S(1)}, u32[]{:S(2)}, u32[]{:S(2)}) %collective-permute-start.5) | collective-permute-done | bytes 655392 | tf_op jit(solution)/shard_map/ppermute | solution.py:35
  83.6 1.9 %collective-permute-start.3 = (bf16[512,640]{1,0:T(8,128)(2,1)}, bf16[512,640]{1,0:T(8,128)(2,1)}, u32[]{:S(2)}, u32[]{:S(2)}) collective-permute-start(bf16[512,640]{1,0:T(8,128)(2,1)} %collective-permute-done.2.refs_2_), channel_id=1, source_target_pairs={{0,2},{2,0},{4,6},{6,4},{1,3},{3,1},{5,7},{7,5},{8,10},{10,8},{12,... | collective-permute-start | bytes 1966088 | tf_op jit(solution)/shard_map/ppermute | solution.py:35
  86.3 4.3 %collective-permute-start.13 = (bf16[512,640]{1,0:T(8,128)(2,1)}, bf16[512,640]{1,0:T(8,128)(2,1)}, u32[]{:S(2)}, u32[]{:S(2)}) collective-permute-start(bf16[512,640]{1,0:T(8,128)(2,1)} %collective-permute-done.2.refs_2_), channel_id=1, source_target_pairs={{0,1},{1,0},{2,3},{3,2},{4,5},{5,4},{6,7},{7,6},{8,9},{9,8},{10,11... | collective-permute-start | bytes 1966088 | tf_op jit(solution)/shard_map/ppermute | solution.py:35
  90.7 1.9 %collective-permute-start.9 = (bf16[512,640]{1,0:T(8,128)(2,1)S(1)}, bf16[512,640]{1,0:T(8,128)(2,1)S(1)}, u32[]{:S(2)}, u32[]{:S(2)}) collective-permute-start(bf16[512,640]{1,0:T(8,128)(2,1)S(1)} %collective-permute-done.5.refs_3_), channel_id=1, source_target_pairs={{0,1},{1,0},{2,3},{3,2},{4,5},{5,4},{6,7},{7,6},{8,9},{9,8},{10,11... | collective-permute-start | bytes 1966088 | tf_op jit(solution)/shard_map/ppermute | solution.py:35
  92.6 1.1 copy-done.2
  94.2 4.5 %collective-permute-done.1.refs_1_ = bf16[512,640]{1,0:T(8,128)(2,1)} collective-permute-done((bf16[512,640]{1,0:T(8,128)(2,1)}, bf16[512,640]{1,0:T(8,128)(2,1)}, u32[]{:S(2)}, u32[]{:S(2)}) %collective-permute-start.1) | collective-permute-done | bytes 655392 | tf_op jit(solution)/shard_map/ppermute | solution.py:35
  98.7 3.6 %collective-permute-start.12 = (bf16[512,640]{1,0:T(8,128)(2,1)}, bf16[512,640]{1,0:T(8,128)(2,1)}, u32[]{:S(2)}, u32[]{:S(2)}) collective-permute-start(bf16[512,640]{1,0:T(8,128)(2,1)} %collective-permute-done.1.refs_1_), channel_id=1, source_target_pairs={{0,1},{1,0},{2,3},{3,2},{4,5},{5,4},{6,7},{7,6},{8,9},{9,8},{10,11... | collective-permute-start | bytes 1966088 | tf_op jit(solution)/shard_map/ppermute | solution.py:35
  103.1 6.1 %all-gather.4.cloned.1.call-done = bf16[32,2,160,256]{3,2,1,0:T(8,128)(2,1)} async-done(((bf16[4,2,160,256]{3,2,1,0:T(8,128)(2,1)}), bf16[32,2,160,256]{3,2,1,0:T(8,128)(2,1)}) %all-gather.4.cloned.1.call-update) | async-done | bytes 5242896 | tf_op jit(solution)/shard_map/all_gather | solution.py:135
  109.2 2.5 %copy-done = bf16[32,2,160,256]{3,2,1,0:T(8,128)(2,1)S(1)} copy-done((bf16[32,2,160,256]{3,2,1,0:T(8,128)(2,1)S(1)}, bf16[32,2,160,256]{3,2,1,0:T(8,128)(2,1)}, u32[]{:S(2)}) %copy-start) | copy-done | bytes 5242904
  111.7 1.1 copy-done.5
  112.8 1.1 copy-done.7
  113.9 2.9 %layer_two.1.own_ref = bf16[512,256]{1,0:T(8,128)(2,1)S(1)} custom-call(s32[5]{0:T(128)S(1)} %stack.21.place, bf16[512,640]{1,0:T(8,128)(2,1)S(1)} %copy-done.3, bf16[512,640]{1,0:T(8,128)(2,1)S(1)} %collective-permute-done.refs_1_, bf16[512,640]{1,0:T(8,128)(2,1)S(1)} %collective-permute-done.4.refs_2_, ...), custom_call_target="tpu_custom_call" | custom-call | flops 1342177280 | bytes 7864320 | tf_op jit(solution)/shard_map/layer_two/pallas_call | solution.py:165
  116.8 2.6 %collective-permute-start.14 = (bf16[512,640]{1,0:T(8,128)(2,1)}, bf16[512,640]{1,0:T(8,128)(2,1)S(1)}, u32[]{:S(2)}, u32[]{:S(2)}) collective-permute-start(bf16[512,640]{1,0:T(8,128)(2,1)} %collective-permute-done.3.refs_3_), channel_id=1, source_target_pairs={{0,1},{1,0},{2,3},{3,2},{4,5},{5,4},{6,7},{7,6},{8,9},{9,8},{10,11... | collective-permute-start | bytes 1966088 | tf_op jit(solution)/shard_map/ppermute | solution.py:35
  119.4 2.1 %collective-permute-start.15 = (bf16[512,256]{1,0:T(8,128)(2,1)S(1)}, bf16[512,256]{1,0:T(8,128)(2,1)S(1)}, u32[]{:S(2)}, u32[]{:S(2)}) collective-permute-start(bf16[512,256]{1,0:T(8,128)(2,1)S(1)} %layer_two.1.own_ref), channel_id=1, source_target_pairs={{0,32},{16,48},{32,0},{48,16},{64,96},{80,112},{96,64},{112,80},{1... | collective-permute-start | bytes 786440 | tf_op jit(solution)/shard_map/ppermute | solution.py:35
  121.5 7.0 %collective-permute-start.16 = (bf16[512,256]{1,0:T(8,128)(2,1)S(1)}, bf16[512,256]{1,0:T(8,128)(2,1)S(1)}, u32[]{:S(2)}, u32[]{:S(2)}) collective-permute-start(bf16[512,256]{1,0:T(8,128)(2,1)S(1)} %layer_two.1.own_ref), channel_id=1, source_target_pairs={{0,8},{8,0},{1,9},{9,1},{2,10},{10,2},{3,11},{11,3},{4,12},{12,4},... | collective-permute-start | bytes 786440 | tf_op jit(solution)/shard_map/ppermute | solution.py:35
  128.5 4.5 %collective-permute-start.17 = (bf16[512,256]{1,0:T(8,128)(2,1)S(1)}, bf16[512,256]{1,0:T(8,128)(2,1)S(1)}, u32[]{:S(2)}, u32[]{:S(2)}) collective-permute-start(bf16[512,256]{1,0:T(8,128)(2,1)S(1)} %layer_two.1.own_ref), channel_id=1, source_target_pairs={{0,16},{16,0},{32,48},{48,32},{64,80},{80,64},{96,112},{112,96},{1... | collective-permute-start | bytes 786440 | tf_op jit(solution)/shard_map/ppermute | solution.py:35
  133.1 4.5 %layer_one.1 = (bf16[512,128]{1,0:T(8,128)(2,1)}, bf16[512,128]{1,0:T(8,128)(2,1)}) custom-call(s32[5]{0:T(128)S(1)} %stack.21.place, bf16[512,640]{1,0:T(8,128)(2,1)S(1)} %copy-done.8, bf16[512,640]{1,0:T(8,128)(2,1)} %collective-permute-done.1.refs_1_, bf16[512,640]{1,0:T(8,128)(2,1)} %collective-permute-done.2.refs_2_, ...), custom_call_target="tpu_custom_call" | custom-call | flops 1342177280 | bytes 7864320 | tf_op jit(solution)/shard_map/layer_one/pallas_call | solution.py:183
  137.5 4.1 %collective-permute-done.17.refs_2_ = bf16[512,256]{1,0:T(8,128)(2,1)S(1)} collective-permute-done((bf16[512,256]{1,0:T(8,128)(2,1)S(1)}, bf16[512,256]{1,0:T(8,128)(2,1)S(1)}, u32[]{:S(2)}, u32[]{:S(2)}) %collective-permute-start.17) | collective-permute-done | bytes 262176 | tf_op jit(solution)/shard_map/ppermute | solution.py:35
  141.6 1.4 finish_two.1
  (41 shorter events, 4.8 us)
Async XLA Ops:
  7.2 102.1 %all-gather.4.cloned.1.call-start = ((), (), s32[]{:S(2)}) async-start(), calls=%async_computation | async-start | bytes 5898240 | tf_op jit(solution)/shard_map/all_gather | solution.py:135
  9.7 13.0 %collective-permute-start.10 = (bf16[2,80,256]{2,1,0:T(8,128)(2,1)S(1)}, bf16[2,80,256]{2,1,0:T(8,128)(2,1)S(1)}, u32[]{:S(2)}, u32[]{:S(2)}) collective-permute-start(bf16[2,80,256]{2,1,0:T(8,128)(2,1)S(1)} %pad_maximum_fusion.1), channel_id=1, source_target_pairs={{0,8},{8,0},{1,9},{9,1},{2,10},{10,2},{3,11},{11,3},{4,12},{12,4},... | collective-permute-start | bytes 245768 | tf_op jit(solution)/shard_map/ppermute | solution.py:35
  18.0 34.7 %collective-permute-start.4 = (bf16[512,640]{1,0:T(8,128)(2,1)}, bf16[512,640]{1,0:T(8,128)(2,1)S(1)}, u32[]{:S(2)}, u32[]{:S(2)}) collective-permute-start(bf16[512,640]{1,0:T(8,128)(2,1)} %refs_0_.4), channel_id=1, source_target_pairs={{0,4},{2,6},{4,0},{6,2},{1,5},{3,7},{5,1},{7,3},{8,12},{10,14},{12... | collective-permute-start | bytes 1966088 | tf_op jit(solution)/shard_map/ppermute | solution.py:35
  20.4 34.2 %collective-permute-start = (bf16[512,640]{1,0:T(8,128)(2,1)}, bf16[512,640]{1,0:T(8,128)(2,1)S(1)}, u32[]{:S(2)}, u32[]{:S(2)}) collective-permute-start(bf16[512,640]{1,0:T(8,128)(2,1)} %refs_0_.4), channel_id=1, source_target_pairs={{0,2},{2,0},{4,6},{6,4},{1,3},{3,1},{5,7},{7,5},{8,10},{10,8},{12,... | collective-permute-start | bytes 1966088 | tf_op jit(solution)/shard_map/ppermute | solution.py:35
  34.5 27.2 %collective-permute-start.6 = (bf16[512,640]{1,0:T(8,128)(2,1)}, bf16[512,640]{1,0:T(8,128)(2,1)S(1)}, u32[]{:S(2)}, u32[]{:S(2)}) collective-permute-start(bf16[512,640]{1,0:T(8,128)(2,1)} %refs_0_.4), channel_id=1, source_target_pairs={{0,1},{1,0},{2,3},{3,2},{4,5},{5,4},{6,7},{7,6},{8,9},{9,8},{10,11... | collective-permute-start | bytes 1966088 | tf_op jit(solution)/shard_map/ppermute | solution.py:35
  44.2 35.7 %collective-permute-start.2 = (bf16[512,640]{1,0:T(8,128)(2,1)}, bf16[512,640]{1,0:T(8,128)(2,1)}, u32[]{:S(2)}, u32[]{:S(2)}) collective-permute-start(bf16[512,640]{1,0:T(8,128)(2,1)} %refs_0_.5), channel_id=1, source_target_pairs={{0,4},{2,6},{4,0},{6,2},{1,5},{3,7},{5,1},{7,3},{8,12},{10,14},{12... | collective-permute-start | bytes 1966088 | tf_op jit(solution)/shard_map/ppermute | solution.py:35
  52.7 30.9 %collective-permute-start.5 = (bf16[512,640]{1,0:T(8,128)(2,1)S(1)}, bf16[512,640]{1,0:T(8,128)(2,1)S(1)}, u32[]{:S(2)}, u32[]{:S(2)}) collective-permute-start(bf16[512,640]{1,0:T(8,128)(2,1)S(1)} %collective-permute-done.4.refs_2_), channel_id=1, source_target_pairs={{0,2},{2,0},{4,6},{6,4},{1,3},{3,1},{5,7},{7,5},{8,10},{10,8},{12,... | collective-permute-start | bytes 1966088 | tf_op jit(solution)/shard_map/ppermute | solution.py:35
  54.6 30.9 %collective-permute-start.7 = (bf16[512,640]{1,0:T(8,128)(2,1)S(1)}, bf16[512,640]{1,0:T(8,128)(2,1)S(1)}, u32[]{:S(2)}, u32[]{:S(2)}) collective-permute-start(bf16[512,640]{1,0:T(8,128)(2,1)S(1)} %collective-permute-done.refs_1_), channel_id=1, source_target_pairs={{0,1},{1,0},{2,3},{3,2},{4,5},{5,4},{6,7},{7,6},{8,9},{9,8},{10,11... | collective-permute-start | bytes 1966088 | tf_op jit(solution)/shard_map/ppermute | solution.py:35
  57.7 33.0 %collective-permute-start.8 = (bf16[512,640]{1,0:T(8,128)(2,1)S(1)}, bf16[512,640]{1,0:T(8,128)(2,1)}, u32[]{:S(2)}, u32[]{:S(2)}) collective-permute-start(bf16[512,640]{1,0:T(8,128)(2,1)S(1)} %collective-permute-done.4.refs_2_), channel_id=1, source_target_pairs={{0,1},{1,0},{2,3},{3,2},{4,5},{5,4},{6,7},{7,6},{8,9},{9,8},{10,11... | collective-permute-start | bytes 1966088 | tf_op jit(solution)/shard_map/ppermute | solution.py:35
  61.6 47.7 %copy-start.9 = (f32[128]{0:T(128)S(1)}, f32[128]{0:T(128)}, u32[]{:S(2)}) copy-start(f32[128]{0:T(128)} %param.18) | copy-start | bytes 1540
  61.7 59.8 %collective-permute-start.11 = (bf16[512,640]{1,0:T(8,128)(2,1)}, bf16[512,640]{1,0:T(8,128)(2,1)}, u32[]{:S(2)}, u32[]{:S(2)}) collective-permute-start(bf16[512,640]{1,0:T(8,128)(2,1)} %refs_0_.5), channel_id=1, source_target_pairs={{0,1},{1,0},{2,3},{3,2},{4,5},{5,4},{6,7},{7,6},{8,9},{9,8},{10,11... | collective-permute-start | bytes 1966088 | tf_op jit(solution)/shard_map/ppermute | solution.py:35
  79.8 18.8 %collective-permute-start.1 = (bf16[512,640]{1,0:T(8,128)(2,1)}, bf16[512,640]{1,0:T(8,128)(2,1)}, u32[]{:S(2)}, u32[]{:S(2)}) collective-permute-start(bf16[512,640]{1,0:T(8,128)(2,1)} %refs_0_.5), channel_id=1, source_target_pairs={{0,2},{2,0},{4,6},{6,4},{1,3},{3,1},{5,7},{7,5},{8,10},{10,8},{12,... | collective-permute-start | bytes 1966088 | tf_op jit(solution)/shard_map/ppermute | solution.py:35
  83.6 33.2 %collective-permute-start.3 = (bf16[512,640]{1,0:T(8,128)(2,1)}, bf16[512,640]{1,0:T(8,128)(2,1)}, u32[]{:S(2)}, u32[]{:S(2)}) collective-permute-start(bf16[512,640]{1,0:T(8,128)(2,1)} %collective-permute-done.2.refs_2_), channel_id=1, source_target_pairs={{0,2},{2,0},{4,6},{6,4},{1,3},{3,1},{5,7},{7,5},{8,10},{10,8},{12,... | collective-permute-start | bytes 1966088 | tf_op jit(solution)/shard_map/ppermute | solution.py:35
  85.5 0.8 copy-start.4
  86.3 42.2 %collective-permute-start.13 = (bf16[512,640]{1,0:T(8,128)(2,1)}, bf16[512,640]{1,0:T(8,128)(2,1)}, u32[]{:S(2)}, u32[]{:S(2)}) collective-permute-start(bf16[512,640]{1,0:T(8,128)(2,1)} %collective-permute-done.2.refs_2_), channel_id=1, source_target_pairs={{0,1},{1,0},{2,3},{3,2},{4,5},{5,4},{6,7},{7,6},{8,9},{9,8},{10,11... | collective-permute-start | bytes 1966088 | tf_op jit(solution)/shard_map/ppermute | solution.py:35
  90.7 11.6 %collective-permute-start.9 = (bf16[512,640]{1,0:T(8,128)(2,1)S(1)}, bf16[512,640]{1,0:T(8,128)(2,1)S(1)}, u32[]{:S(2)}, u32[]{:S(2)}) collective-permute-start(bf16[512,640]{1,0:T(8,128)(2,1)S(1)} %collective-permute-done.5.refs_3_), channel_id=1, source_target_pairs={{0,1},{1,0},{2,3},{3,2},{4,5},{5,4},{6,7},{7,6},{8,9},{9,8},{10,11... | collective-permute-start | bytes 1966088 | tf_op jit(solution)/shard_map/ppermute | solution.py:35
  92.6 1.1 copy-start.2
  93.7 15.5 %copy-start.3 = (bf16[512,640]{1,0:T(8,128)(2,1)S(1)}, bf16[512,640]{1,0:T(8,128)(2,1)}, u32[]{:S(2)}) copy-start(bf16[512,640]{1,0:T(8,128)(2,1)} %refs_0_.4) | copy-start | bytes 1966084
  98.7 34.4 %collective-permute-start.12 = (bf16[512,640]{1,0:T(8,128)(2,1)}, bf16[512,640]{1,0:T(8,128)(2,1)}, u32[]{:S(2)}, u32[]{:S(2)}) collective-permute-start(bf16[512,640]{1,0:T(8,128)(2,1)} %collective-permute-done.1.refs_1_), channel_id=1, source_target_pairs={{0,1},{1,0},{2,3},{3,2},{4,5},{5,4},{6,7},{7,6},{8,9},{9,8},{10,11... | collective-permute-start | bytes 1966088 | tf_op jit(solution)/shard_map/ppermute | solution.py:35
  102.2 0.8 copy-start.6
  109.2 2.5 %copy-start = (bf16[32,2,160,256]{3,2,1,0:T(8,128)(2,1)S(1)}, bf16[32,2,160,256]{3,2,1,0:T(8,128)(2,1)}, u32[]{:S(2)}) copy-start(bf16[32,2,160,256]{3,2,1,0:T(8,128)(2,1)} %all-gather.4.cloned.1.call-done) | copy-start | bytes 15728644
  111.7 1.1 copy-start.5
  112.8 1.1 copy-start.7
  113.9 19.1 %copy-start.1 = (bf16[32,2,160,256]{3,2,1,0:T(8,128)(2,1)S(1)}, bf16[32,2,160,256]{3,2,1,0:T(8,128)(2,1)}, u32[]{:S(2)}) copy-start(bf16[32,2,160,256]{3,2,1,0:T(8,128)(2,1)} %all-gather.4.cloned.1.call-done) | copy-start | bytes 15728644
  113.9 19.2 %copy-start.8 = (bf16[512,640]{1,0:T(8,128)(2,1)S(1)}, bf16[512,640]{1,0:T(8,128)(2,1)}, u32[]{:S(2)}) copy-start(bf16[512,640]{1,0:T(8,128)(2,1)} %refs_0_.5) | copy-start | bytes 1966084
  113.9 19.2 %copy-start.10 = (f32[128]{0:T(128)S(1)}, f32[128]{0:T(128)}, u32[]{:S(2)}) copy-start(f32[128]{0:T(128)} %param.17) | copy-start | bytes 1540
  116.8 16.2 %collective-permute-start.14 = (bf16[512,640]{1,0:T(8,128)(2,1)}, bf16[512,640]{1,0:T(8,128)(2,1)S(1)}, u32[]{:S(2)}, u32[]{:S(2)}) collective-permute-start(bf16[512,640]{1,0:T(8,128)(2,1)} %collective-permute-done.3.refs_3_), channel_id=1, source_target_pairs={{0,1},{1,0},{2,3},{3,2},{4,5},{5,4},{6,7},{7,6},{8,9},{9,8},{10,11... | collective-permute-start | bytes 1966088 | tf_op jit(solution)/shard_map/ppermute | solution.py:35
  119.4 18.2 %collective-permute-start.15 = (bf16[512,256]{1,0:T(8,128)(2,1)S(1)}, bf16[512,256]{1,0:T(8,128)(2,1)S(1)}, u32[]{:S(2)}, u32[]{:S(2)}) collective-permute-start(bf16[512,256]{1,0:T(8,128)(2,1)S(1)} %layer_two.1.own_ref), channel_id=1, source_target_pairs={{0,32},{16,48},{32,0},{48,16},{64,96},{80,112},{96,64},{112,80},{1... | collective-permute-start | bytes 786440 | tf_op jit(solution)/shard_map/ppermute | solution.py:35
  121.5 16.1 %collective-permute-start.16 = (bf16[512,256]{1,0:T(8,128)(2,1)S(1)}, bf16[512,256]{1,0:T(8,128)(2,1)S(1)}, u32[]{:S(2)}, u32[]{:S(2)}) collective-permute-start(bf16[512,256]{1,0:T(8,128)(2,1)S(1)} %layer_two.1.own_ref), channel_id=1, source_target_pairs={{0,8},{8,0},{1,9},{9,1},{2,10},{10,2},{3,11},{11,3},{4,12},{12,4},... | collective-permute-start | bytes 786440 | tf_op jit(solution)/shard_map/ppermute | solution.py:35
  128.5 13.1 %collective-permute-start.17 = (bf16[512,256]{1,0:T(8,128)(2,1)S(1)}, bf16[512,256]{1,0:T(8,128)(2,1)S(1)}, u32[]{:S(2)}, u32[]{:S(2)}) collective-permute-start(bf16[512,256]{1,0:T(8,128)(2,1)S(1)} %layer_two.1.own_ref), channel_id=1, source_target_pairs={{0,16},{16,0},{32,48},{48,32},{64,80},{80,64},{96,112},{112,96},{1... | collective-permute-start | bytes 786440 | tf_op jit(solution)/shard_map/ppermute | solution.py:35
Sparse Core Ops, SparseCore 0:
  34.6 74.5 all-gather.3

commit v7 on v6

--- a/solution.py
+++ b/solution.py
@@ -154,8 +154,7 @@
     )(*two_blocks)
     two_blocks += [from_core(block) for block in two_blocks]
     one_far = from_line(x_one, 2)
-    x_first, two_near = lax.optimization_barrier((x_one, two_near))
-    one_near = from_line(x_first, 1)
+    one_near = from_line(x_one, 1)
     one_last = from_line(one_far, 1)
     place = jnp.stack([l, c, lengths[0], pair_bit, is_old]).astype(jnp.int32)
 

time: 151 us -> 151 us (level)
  local copies, waits for them, and re-layouts: 9.05 us -> 11 us
    ppermute x18, waiting for transfers between devices: 32.8 us -> 36.7 us  [move(): return lax.ppermute(value, axes, pairs)]
    all_gather x1, waiting for transfers between devices: 6.14 us -> 2.23 us  [on_device(): weights = lax.all_gather(lax.all_gather(weights, 'x'), 'z')]
    unnamed x22 -> x26, local copies, waits for them, and re-layouts: 7.42 us -> 9.37 us
where the time goes in v7:
time: 151 us; the launch traced here: 150 us
  starting transfers between devices  62.8 us (42%)
  waiting for transfers between devices  39 us (26%)
  between operations  16.3 us (11%)
  blocking collectives  11.7 us (8%)
  local copies, waits for them, and re-layouts  11 us (7%)
  Pallas kernels  8.57 us (6%)
    ppermute x18, starting transfers between devices, move(): return lax.ppermute(value, axes, pairs)  62.7 us
    ppermute x18, waiting for transfers between devices, move(): return lax.ppermute(value, axes, pairs)  36.7 us
    all_gather x1, blocking collectives, on_device(): weights = lax.all_gather(lax.all_gather(weights, 'x'), 'z')  11.7 us
    unnamed x26, local copies, waits for them, and re-layouts  9.37 us
    pallas_call x1, Pallas kernels, on_device(): pl.pallas_call(one_kernel, out_shape=(jax.ShapeDtypeStruct((rows, HD), jn...  4.46 us
  transfers between devices with their start and end apart: 19, of which 6 were waited for; matrix products, arithmetic and copies ran while one was open for 0% of the time, Pallas kernels for 5%

profile of v7, /device:TPU:1, one launch (start us, length us, event | category | flops | bytes accessed | tf_op | source)
XLA Modules:
  0.0 150.3 jit_solution(11239760722494829799)
XLA Ops:
  9.7 8.3 %collective-permute-start.10 = (bf16[2,80,256]{2,1,0:T(8,128)(2,1)S(1)}, bf16[2,80,256]{2,1,0:T(8,128)(2,1)S(1)}, u32[]{:S(2)}, u32[]{:S(2)}) collective-permute-start(bf16[2,80,256]{2,1,0:T(8,128)(2,1)S(1)} %pad_maximum_fusion.1), channel_id=1, source_target_pairs={{0,8},{8,0},{1,9},{9,1},{2,10},{10,2},{3,11},{11,3},{4,12},{12,4},... | collective-permute-start | bytes 245768 | tf_op jit(solution)/shard_map/ppermute | solution.py:35
  18.0 2.4 %collective-permute-start.4 = (bf16[512,640]{1,0:T(8,128)(2,1)}, bf16[512,640]{1,0:T(8,128)(2,1)S(1)}, u32[]{:S(2)}, u32[]{:S(2)}) collective-permute-start(bf16[512,640]{1,0:T(8,128)(2,1)} %refs_0_.4), channel_id=1, source_target_pairs={{0,4},{2,6},{4,0},{6,2},{1,5},{3,7},{5,1},{7,3},{8,12},{10,14},{12... | collective-permute-start | bytes 1966088 | tf_op jit(solution)/shard_map/ppermute | solution.py:35
  20.4 2.3 %collective-permute-start.3 = (bf16[512,640]{1,0:T(8,128)(2,1)}, bf16[512,640]{1,0:T(8,128)(2,1)S(1)}, u32[]{:S(2)}, u32[]{:S(2)}) collective-permute-start(bf16[512,640]{1,0:T(8,128)(2,1)} %refs_0_.4), channel_id=1, source_target_pairs={{0,2},{2,0},{4,6},{6,4},{1,3},{3,1},{5,7},{7,5},{8,10},{10,8},{12,... | collective-permute-start | bytes 1966088 | tf_op jit(solution)/shard_map/ppermute | solution.py:35
  22.8 11.7 %all-gather = bf16[8,160,256]{2,1,0:T(8,128)(2,1)} all-gather(bf16[2,160,256]{2,1,0:T(8,128)(2,1)S(1)} %pad_maximum_fusion), channel_id=2, replica_groups=mesh['x'=4,'z'=8,'h'=2,'l'=4,'c'=2] {'x'}, dimensions={0}, use_global_device_ids=true | all-gather | bytes 819200 | tf_op jit(solution)/shard_map/all_gather | solution.py:135
  34.5 9.7 %collective-permute-start.6 = (bf16[512,640]{1,0:T(8,128)(2,1)}, bf16[512,640]{1,0:T(8,128)(2,1)S(1)}, u32[]{:S(2)}, u32[]{:S(2)}) collective-permute-start(bf16[512,640]{1,0:T(8,128)(2,1)} %refs_0_.4), channel_id=1, source_target_pairs={{0,1},{1,0},{2,3},{3,2},{4,5},{5,4},{6,7},{7,6},{8,9},{9,8},{10,11... | collective-permute-start | bytes 1966088 | tf_op jit(solution)/shard_map/ppermute | solution.py:35
  44.2 1.9 %collective-permute-start.1 = (bf16[512,640]{1,0:T(8,128)(2,1)}, bf16[512,640]{1,0:T(8,128)(2,1)}, u32[]{:S(2)}, u32[]{:S(2)}) collective-permute-start(bf16[512,640]{1,0:T(8,128)(2,1)} %refs_0_.5), channel_id=1, source_target_pairs={{0,4},{2,6},{4,0},{6,2},{1,5},{3,7},{5,1},{7,3},{8,12},{10,14},{12... | collective-permute-start | bytes 1966088 | tf_op jit(solution)/shard_map/ppermute | solution.py:35
  46.1 1.9 %collective-permute-start = (bf16[512,640]{1,0:T(8,128)(2,1)}, bf16[512,640]{1,0:T(8,128)(2,1)}, u32[]{:S(2)}, u32[]{:S(2)}) collective-permute-start(bf16[512,640]{1,0:T(8,128)(2,1)} %refs_0_.5), channel_id=1, source_target_pairs={{0,2},{2,0},{4,6},{6,4},{1,3},{3,1},{5,7},{7,5},{8,10},{10,8},{12,... | collective-permute-start | bytes 1966088 | tf_op jit(solution)/shard_map/ppermute | solution.py:35
  48.0 4.6 %collective-permute-done.4.refs_2_ = bf16[512,640]{1,0:T(8,128)(2,1)S(1)} collective-permute-done((bf16[512,640]{1,0:T(8,128)(2,1)}, bf16[512,640]{1,0:T(8,128)(2,1)S(1)}, u32[]{:S(2)}, u32[]{:S(2)}) %collective-permute-start.4) | collective-permute-done | bytes 655392 | tf_op jit(solution)/shard_map/ppermute | solution.py:35
  52.7 1.9 %collective-permute-start.5 = (bf16[512,640]{1,0:T(8,128)(2,1)S(1)}, bf16[512,640]{1,0:T(8,128)(2,1)S(1)}, u32[]{:S(2)}, u32[]{:S(2)}) collective-permute-start(bf16[512,640]{1,0:T(8,128)(2,1)S(1)} %collective-permute-done.4.refs_2_), channel_id=1, source_target_pairs={{0,2},{2,0},{4,6},{6,4},{1,3},{3,1},{5,7},{7,5},{8,10},{10,8},{12,... | collective-permute-start | bytes 1966088 | tf_op jit(solution)/shard_map/ppermute | solution.py:35
  54.6 3.1 %collective-permute-start.8 = (bf16[512,640]{1,0:T(8,128)(2,1)S(1)}, bf16[512,640]{1,0:T(8,128)(2,1)S(1)}, u32[]{:S(2)}, u32[]{:S(2)}) collective-permute-start(bf16[512,640]{1,0:T(8,128)(2,1)S(1)} %collective-permute-done.4.refs_2_), channel_id=1, source_target_pairs={{0,1},{1,0},{2,3},{3,2},{4,5},{5,4},{6,7},{7,6},{8,9},{9,8},{10,11... | collective-permute-start | bytes 1966088 | tf_op jit(solution)/shard_map/ppermute | solution.py:35
  59.7 1.9 %collective-permute-start.11 = (bf16[512,640]{1,0:T(8,128)(2,1)}, bf16[512,640]{1,0:T(8,128)(2,1)}, u32[]{:S(2)}, u32[]{:S(2)}) collective-permute-start(bf16[512,640]{1,0:T(8,128)(2,1)} %refs_0_.5), channel_id=1, source_target_pairs={{0,1},{1,0},{2,3},{3,2},{4,5},{5,4},{6,7},{7,6},{8,9},{9,8},{10,11... | collective-permute-start | bytes 1966088 | tf_op jit(solution)/shard_map/ppermute | solution.py:35
  61.7 18.2 %collective-permute-done.1.refs_2_ = bf16[512,640]{1,0:T(8,128)(2,1)} collective-permute-done((bf16[512,640]{1,0:T(8,128)(2,1)}, bf16[512,640]{1,0:T(8,128)(2,1)}, u32[]{:S(2)}, u32[]{:S(2)}) %collective-permute-start.1) | collective-permute-done | bytes 655392 | tf_op jit(solution)/shard_map/ppermute | solution.py:35
  79.8 1.9 %collective-permute-start.2 = (bf16[512,640]{1,0:T(8,128)(2,1)}, bf16[512,640]{1,0:T(8,128)(2,1)}, u32[]{:S(2)}, u32[]{:S(2)}) collective-permute-start(bf16[512,640]{1,0:T(8,128)(2,1)} %collective-permute-done.1.refs_2_), channel_id=1, source_target_pairs={{0,2},{2,0},{4,6},{6,4},{1,3},{3,1},{5,7},{7,5},{8,10},{10,8},{12,... | collective-permute-start | bytes 1966088 | tf_op jit(solution)/shard_map/ppermute | solution.py:35
  81.8 2.8 %collective-permute-start.13 = (bf16[512,640]{1,0:T(8,128)(2,1)}, bf16[512,640]{1,0:T(8,128)(2,1)}, u32[]{:S(2)}, u32[]{:S(2)}) collective-permute-start(bf16[512,640]{1,0:T(8,128)(2,1)} %collective-permute-done.1.refs_2_), channel_id=1, source_target_pairs={{0,1},{1,0},{2,3},{3,2},{4,5},{5,4},{6,7},{7,6},{8,9},{9,8},{10,11... | collective-permute-start | bytes 1966088 | tf_op jit(solution)/shard_map/ppermute | solution.py:35
  84.5 9.8 %collective-permute-done.5.refs_3_ = bf16[512,640]{1,0:T(8,128)(2,1)S(1)} collective-permute-done((bf16[512,640]{1,0:T(8,128)(2,1)S(1)}, bf16[512,640]{1,0:T(8,128)(2,1)S(1)}, u32[]{:S(2)}, u32[]{:S(2)}) %collective-permute-start.5) | collective-permute-done | bytes 655392 | tf_op jit(solution)/shard_map/ppermute | solution.py:35
  94.3 4.2 %collective-permute-start.7 = (bf16[512,640]{1,0:T(8,128)(2,1)S(1)}, bf16[512,640]{1,0:T(8,128)(2,1)S(1)}, u32[]{:S(2)}, u32[]{:S(2)}) collective-permute-start(bf16[512,640]{1,0:T(8,128)(2,1)S(1)} %collective-permute-done.3.refs_1_), channel_id=1, source_target_pairs={{0,1},{1,0},{2,3},{3,2},{4,5},{5,4},{6,7},{7,6},{8,9},{9,8},{10,11... | collective-permute-start | bytes 1966088 | tf_op jit(solution)/shard_map/ppermute | solution.py:35
  99.3 1.9 %collective-permute-start.9 = (bf16[512,640]{1,0:T(8,128)(2,1)S(1)}, bf16[512,640]{1,0:T(8,128)(2,1)S(1)}, u32[]{:S(2)}, u32[]{:S(2)}) collective-permute-start(bf16[512,640]{1,0:T(8,128)(2,1)S(1)} %collective-permute-done.5.refs_3_), channel_id=1, source_target_pairs={{0,1},{1,0},{2,3},{3,2},{4,5},{5,4},{6,7},{7,6},{8,9},{9,8},{10,11... | collective-permute-start | bytes 1966088 | tf_op jit(solution)/shard_map/ppermute | solution.py:35
  103.7 2.4 %collective-permute-start.12 = (bf16[512,640]{1,0:T(8,128)(2,1)}, bf16[512,640]{1,0:T(8,128)(2,1)}, u32[]{:S(2)}, u32[]{:S(2)}) collective-permute-start(bf16[512,640]{1,0:T(8,128)(2,1)} %collective-permute-done.refs_1_), channel_id=1, source_target_pairs={{0,1},{1,0},{2,3},{3,2},{4,5},{5,4},{6,7},{7,6},{8,9},{9,8},{10,11... | collective-permute-start | bytes 1966088 | tf_op jit(solution)/shard_map/ppermute | solution.py:35
  107.0 2.2 %all-gather.4.cloned.1.call-done = bf16[32,2,160,256]{3,2,1,0:T(8,128)(2,1)} async-done(((bf16[4,2,160,256]{3,2,1,0:T(8,128)(2,1)}), bf16[32,2,160,256]{3,2,1,0:T(8,128)(2,1)}) %all-gather.4.cloned.1.call-update) | async-done | bytes 5242896 | tf_op jit(solution)/shard_map/all_gather | solution.py:135
  109.2 2.5 %copy-done = bf16[32,2,160,256]{3,2,1,0:T(8,128)(2,1)S(1)} copy-done((bf16[32,2,160,256]{3,2,1,0:T(8,128)(2,1)S(1)}, bf16[32,2,160,256]{3,2,1,0:T(8,128)(2,1)}, u32[]{:S(2)}) %copy-start) | copy-done | bytes 5242904
  111.7 1.1 copy-done.5
  112.8 1.1 copy-done.7
  113.9 1.1 copy-done.9
  115.0 2.2 %layer_two.1.own_ref = bf16[512,256]{1,0:T(8,128)(2,1)S(1)} custom-call(s32[5]{0:T(128)S(1)} %stack.21.place, bf16[512,640]{1,0:T(8,128)(2,1)S(1)} %copy-done.3, bf16[512,640]{1,0:T(8,128)(2,1)S(1)} %collective-permute-done.3.refs_1_, bf16[512,640]{1,0:T(8,128)(2,1)S(1)} %collective-permute-done.4.refs_2_, ...), custom_call_target="tpu_custom_call" | custom-call | flops 1342177280 | bytes 7864320 | tf_op jit(solution)/shard_map/layer_two/pallas_call | solution.py:164
  117.2 2.6 %collective-permute-start.14 = (bf16[512,640]{1,0:T(8,128)(2,1)}, bf16[512,640]{1,0:T(8,128)(2,1)S(1)}, u32[]{:S(2)}, u32[]{:S(2)}) collective-permute-start(bf16[512,640]{1,0:T(8,128)(2,1)} %collective-permute-done.2.refs_3_), channel_id=1, source_target_pairs={{0,1},{1,0},{2,3},{3,2},{4,5},{5,4},{6,7},{7,6},{8,9},{9,8},{10,11... | collective-permute-start | bytes 1966088 | tf_op jit(solution)/shard_map/ppermute | solution.py:35
  119.8 3.1 %collective-permute-start.15 = (bf16[512,256]{1,0:T(8,128)(2,1)S(1)}, bf16[512,256]{1,0:T(8,128)(2,1)S(1)}, u32[]{:S(2)}, u32[]{:S(2)}) collective-permute-start(bf16[512,256]{1,0:T(8,128)(2,1)S(1)} %layer_two.1.own_ref), channel_id=1, source_target_pairs={{0,32},{16,48},{32,0},{48,16},{64,96},{80,112},{96,64},{112,80},{1... | collective-permute-start | bytes 786440 | tf_op jit(solution)/shard_map/ppermute | solution.py:35
  122.8 6.0 %collective-permute-start.16 = (bf16[512,256]{1,0:T(8,128)(2,1)S(1)}, bf16[512,256]{1,0:T(8,128)(2,1)S(1)}, u32[]{:S(2)}, u32[]{:S(2)}) collective-permute-start(bf16[512,256]{1,0:T(8,128)(2,1)S(1)} %layer_two.1.own_ref), channel_id=1, source_target_pairs={{0,8},{8,0},{1,9},{9,1},{2,10},{10,2},{3,11},{11,3},{4,12},{12,4},... | collective-permute-start | bytes 786440 | tf_op jit(solution)/shard_map/ppermute | solution.py:35
  128.9 4.5 %collective-permute-start.17 = (bf16[512,256]{1,0:T(8,128)(2,1)S(1)}, bf16[512,256]{1,0:T(8,128)(2,1)S(1)}, u32[]{:S(2)}, u32[]{:S(2)}) collective-permute-start(bf16[512,256]{1,0:T(8,128)(2,1)S(1)} %layer_two.1.own_ref), channel_id=1, source_target_pairs={{0,16},{16,0},{32,48},{48,32},{64,80},{80,64},{96,112},{112,96},{1... | collective-permute-start | bytes 786440 | tf_op jit(solution)/shard_map/ppermute | solution.py:35
  133.4 4.5 %layer_one.1 = (bf16[512,128]{1,0:T(8,128)(2,1)}, bf16[512,128]{1,0:T(8,128)(2,1)}) custom-call(s32[5]{0:T(128)S(1)} %stack.21.place, bf16[512,640]{1,0:T(8,128)(2,1)S(1)} %copy-done.10, bf16[512,640]{1,0:T(8,128)(2,1)} %collective-permute-done.refs_1_, bf16[512,640]{1,0:T(8,128)(2,1)} %collective-permute-done.1.refs_2_, ...), custom_call_target="tpu_custom_call" | custom-call | flops 1342177280 | bytes 7864320 | tf_op jit(solution)/shard_map/layer_one/pallas_call | solution.py:182
  137.9 2.6 %collective-permute-done.16.refs_1_ = bf16[512,256]{1,0:T(8,128)(2,1)S(1)} collective-permute-done((bf16[512,256]{1,0:T(8,128)(2,1)S(1)}, bf16[512,256]{1,0:T(8,128)(2,1)S(1)}, u32[]{:S(2)}, u32[]{:S(2)}) %collective-permute-start.16) | collective-permute-done | bytes 262176 | tf_op jit(solution)/shard_map/ppermute | solution.py:35
  140.5 1.6 %collective-permute-done.17.refs_2_ = bf16[512,256]{1,0:T(8,128)(2,1)S(1)} collective-permute-done((bf16[512,256]{1,0:T(8,128)(2,1)S(1)}, bf16[512,256]{1,0:T(8,128)(2,1)S(1)}, u32[]{:S(2)}, u32[]{:S(2)}) %collective-permute-start.17) | collective-permute-done | bytes 262176 | tf_op jit(solution)/shard_map/ppermute | solution.py:35
  142.0 1.4 finish_two.1
  (45 shorter events, 6.8 us)
Async XLA Ops:
  7.2 102.1 %all-gather.4.cloned.1.call-start = ((), (), s32[]{:S(2)}) async-start(), calls=%async_computation | async-start | bytes 5898240 | tf_op jit(solution)/shard_map/all_gather | solution.py:135
  9.7 13.0 %collective-permute-start.10 = (bf16[2,80,256]{2,1,0:T(8,128)(2,1)S(1)}, bf16[2,80,256]{2,1,0:T(8,128)(2,1)S(1)}, u32[]{:S(2)}, u32[]{:S(2)}) collective-permute-start(bf16[2,80,256]{2,1,0:T(8,128)(2,1)S(1)} %pad_maximum_fusion.1), channel_id=1, source_target_pairs={{0,8},{8,0},{1,9},{9,1},{2,10},{10,2},{3,11},{11,3},{4,12},{12,4},... | collective-permute-start | bytes 245768 | tf_op jit(solution)/shard_map/ppermute | solution.py:35
  18.0 34.7 %collective-permute-start.4 = (bf16[512,640]{1,0:T(8,128)(2,1)}, bf16[512,640]{1,0:T(8,128)(2,1)S(1)}, u32[]{:S(2)}, u32[]{:S(2)}) collective-permute-start(bf16[512,640]{1,0:T(8,128)(2,1)} %refs_0_.4), channel_id=1, source_target_pairs={{0,4},{2,6},{4,0},{6,2},{1,5},{3,7},{5,1},{7,3},{8,12},{10,14},{12... | collective-permute-start | bytes 1966088 | tf_op jit(solution)/shard_map/ppermute | solution.py:35
  20.4 34.2 %collective-permute-start.3 = (bf16[512,640]{1,0:T(8,128)(2,1)}, bf16[512,640]{1,0:T(8,128)(2,1)S(1)}, u32[]{:S(2)}, u32[]{:S(2)}) collective-permute-start(bf16[512,640]{1,0:T(8,128)(2,1)} %refs_0_.4), channel_id=1, source_target_pairs={{0,2},{2,0},{4,6},{6,4},{1,3},{3,1},{5,7},{7,5},{8,10},{10,8},{12,... | collective-permute-start | bytes 1966088 | tf_op jit(solution)/shard_map/ppermute | solution.py:35
  34.5 25.2 %collective-permute-start.6 = (bf16[512,640]{1,0:T(8,128)(2,1)}, bf16[512,640]{1,0:T(8,128)(2,1)S(1)}, u32[]{:S(2)}, u32[]{:S(2)}) collective-permute-start(bf16[512,640]{1,0:T(8,128)(2,1)} %refs_0_.4), channel_id=1, source_target_pairs={{0,1},{1,0},{2,3},{3,2},{4,5},{5,4},{6,7},{7,6},{8,9},{9,8},{10,11... | collective-permute-start | bytes 1966088 | tf_op jit(solution)/shard_map/ppermute | solution.py:35
  44.2 35.6 %collective-permute-start.1 = (bf16[512,640]{1,0:T(8,128)(2,1)}, bf16[512,640]{1,0:T(8,128)(2,1)}, u32[]{:S(2)}, u32[]{:S(2)}) collective-permute-start(bf16[512,640]{1,0:T(8,128)(2,1)} %refs_0_.5), channel_id=1, source_target_pairs={{0,4},{2,6},{4,0},{6,2},{1,5},{3,7},{5,1},{7,3},{8,12},{10,14},{12... | collective-permute-start | bytes 1966088 | tf_op jit(solution)/shard_map/ppermute | solution.py:35
  46.1 35.6 %collective-permute-start = (bf16[512,640]{1,0:T(8,128)(2,1)}, bf16[512,640]{1,0:T(8,128)(2,1)}, u32[]{:S(2)}, u32[]{:S(2)}) collective-permute-start(bf16[512,640]{1,0:T(8,128)(2,1)} %refs_0_.5), channel_id=1, source_target_pairs={{0,2},{2,0},{4,6},{6,4},{1,3},{3,1},{5,7},{7,5},{8,10},{10,8},{12,... | collective-permute-start | bytes 1966088 | tf_op jit(solution)/shard_map/ppermute | solution.py:35
  52.7 41.6 %collective-permute-start.5 = (bf16[512,640]{1,0:T(8,128)(2,1)S(1)}, bf16[512,640]{1,0:T(8,128)(2,1)S(1)}, u32[]{:S(2)}, u32[]{:S(2)}) collective-permute-start(bf16[512,640]{1,0:T(8,128)(2,1)S(1)} %collective-permute-done.4.refs_2_), channel_id=1, source_target_pairs={{0,2},{2,0},{4,6},{6,4},{1,3},{3,1},{5,7},{7,5},{8,10},{10,8},{12,... | collective-permute-start | bytes 1966088 | tf_op jit(solution)/shard_map/ppermute | solution.py:35
  54.6 43.9 %collective-permute-start.8 = (bf16[512,640]{1,0:T(8,128)(2,1)S(1)}, bf16[512,640]{1,0:T(8,128)(2,1)S(1)}, u32[]{:S(2)}, u32[]{:S(2)}) collective-permute-start(bf16[512,640]{1,0:T(8,128)(2,1)S(1)} %collective-permute-done.4.refs_2_), channel_id=1, source_target_pairs={{0,1},{1,0},{2,3},{3,2},{4,5},{5,4},{6,7},{7,6},{8,9},{9,8},{10,11... | collective-permute-start | bytes 1966088 | tf_op jit(solution)/shard_map/ppermute | solution.py:35
  59.6 49.6 %copy-start.11 = (f32[128]{0:T(128)S(1)}, f32[128]{0:T(128)}, u32[]{:S(2)}) copy-start(f32[128]{0:T(128)} %param.18) | copy-start | bytes 1540
  59.7 63.1 %collective-permute-start.11 = (bf16[512,640]{1,0:T(8,128)(2,1)}, bf16[512,640]{1,0:T(8,128)(2,1)}, u32[]{:S(2)}, u32[]{:S(2)}) collective-permute-start(bf16[512,640]{1,0:T(8,128)(2,1)} %refs_0_.5), channel_id=1, source_target_pairs={{0,1},{1,0},{2,3},{3,2},{4,5},{5,4},{6,7},{7,6},{8,9},{9,8},{10,11... | collective-permute-start | bytes 1966088 | tf_op jit(solution)/shard_map/ppermute | solution.py:35
  79.8 37.3 %collective-permute-start.2 = (bf16[512,640]{1,0:T(8,128)(2,1)}, bf16[512,640]{1,0:T(8,128)(2,1)}, u32[]{:S(2)}, u32[]{:S(2)}) collective-permute-start(bf16[512,640]{1,0:T(8,128)(2,1)} %collective-permute-done.1.refs_2_), channel_id=1, source_target_pairs={{0,2},{2,0},{4,6},{6,4},{1,3},{3,1},{5,7},{7,5},{8,10},{10,8},{12,... | collective-permute-start | bytes 1966088 | tf_op jit(solution)/shard_map/ppermute | solution.py:35
  81.8 47.1 %collective-permute-start.13 = (bf16[512,640]{1,0:T(8,128)(2,1)}, bf16[512,640]{1,0:T(8,128)(2,1)}, u32[]{:S(2)}, u32[]{:S(2)}) collective-permute-start(bf16[512,640]{1,0:T(8,128)(2,1)} %collective-permute-done.1.refs_2_), channel_id=1, source_target_pairs={{0,1},{1,0},{2,3},{3,2},{4,5},{5,4},{6,7},{7,6},{8,9},{9,8},{10,11... | collective-permute-start | bytes 1966088 | tf_op jit(solution)/shard_map/ppermute | solution.py:35
  94.3 8.5 %collective-permute-start.7 = (bf16[512,640]{1,0:T(8,128)(2,1)S(1)}, bf16[512,640]{1,0:T(8,128)(2,1)S(1)}, u32[]{:S(2)}, u32[]{:S(2)}) collective-permute-start(bf16[512,640]{1,0:T(8,128)(2,1)S(1)} %collective-permute-done.3.refs_1_), channel_id=1, source_target_pairs={{0,1},{1,0},{2,3},{3,2},{4,5},{5,4},{6,7},{7,6},{8,9},{9,8},{10,11... | collective-permute-start | bytes 1966088 | tf_op jit(solution)/shard_map/ppermute | solution.py:35
  98.5 0.8 copy-start.4
  99.3 6.8 %collective-permute-start.9 = (bf16[512,640]{1,0:T(8,128)(2,1)S(1)}, bf16[512,640]{1,0:T(8,128)(2,1)S(1)}, u32[]{:S(2)}, u32[]{:S(2)}) collective-permute-start(bf16[512,640]{1,0:T(8,128)(2,1)S(1)} %collective-permute-done.5.refs_3_), channel_id=1, source_target_pairs={{0,1},{1,0},{2,3},{3,2},{4,5},{5,4},{6,7},{7,6},{8,9},{9,8},{10,11... | collective-permute-start | bytes 1966088 | tf_op jit(solution)/shard_map/ppermute | solution.py:35
  101.3 1.1 copy-start.2
  102.4 6.9 %copy-start.3 = (bf16[512,640]{1,0:T(8,128)(2,1)S(1)}, bf16[512,640]{1,0:T(8,128)(2,1)}, u32[]{:S(2)}) copy-start(bf16[512,640]{1,0:T(8,128)(2,1)} %refs_0_.4) | copy-start | bytes 1966084
  102.9 0.9 copy-start.6
  103.7 29.7 %collective-permute-start.12 = (bf16[512,640]{1,0:T(8,128)(2,1)}, bf16[512,640]{1,0:T(8,128)(2,1)}, u32[]{:S(2)}, u32[]{:S(2)}) collective-permute-start(bf16[512,640]{1,0:T(8,128)(2,1)} %collective-permute-done.refs_1_), channel_id=1, source_target_pairs={{0,1},{1,0},{2,3},{3,2},{4,5},{5,4},{6,7},{7,6},{8,9},{9,8},{10,11... | collective-permute-start | bytes 1966088 | tf_op jit(solution)/shard_map/ppermute | solution.py:35
  106.2 0.8 copy-start.8
  109.2 2.5 %copy-start = (bf16[32,2,160,256]{3,2,1,0:T(8,128)(2,1)S(1)}, bf16[32,2,160,256]{3,2,1,0:T(8,128)(2,1)}, u32[]{:S(2)}) copy-start(bf16[32,2,160,256]{3,2,1,0:T(8,128)(2,1)} %all-gather.4.cloned.1.call-done) | copy-start | bytes 15728644
  111.7 1.1 copy-start.5
  112.8 1.1 copy-start.7
  113.9 1.1 copy-start.9
  115.0 18.4 %copy-start.1 = (bf16[32,2,160,256]{3,2,1,0:T(8,128)(2,1)S(1)}, bf16[32,2,160,256]{3,2,1,0:T(8,128)(2,1)}, u32[]{:S(2)}) copy-start(bf16[32,2,160,256]{3,2,1,0:T(8,128)(2,1)} %all-gather.4.cloned.1.call-done) | copy-start | bytes 15728644
  115.0 18.4 %copy-start.10 = (bf16[512,640]{1,0:T(8,128)(2,1)S(1)}, bf16[512,640]{1,0:T(8,128)(2,1)}, u32[]{:S(2)}) copy-start(bf16[512,640]{1,0:T(8,128)(2,1)} %refs_0_.5) | copy-start | bytes 1966084
  115.0 18.4 %copy-start.12 = (f32[128]{0:T(128)S(1)}, f32[128]{0:T(128)}, u32[]{:S(2)}) copy-start(f32[128]{0:T(128)} %param.17) | copy-start | bytes 1540
  117.2 16.2 %collective-permute-start.14 = (bf16[512,640]{1,0:T(8,128)(2,1)}, bf16[512,640]{1,0:T(8,128)(2,1)S(1)}, u32[]{:S(2)}, u32[]{:S(2)}) collective-permute-start(bf16[512,640]{1,0:T(8,128)(2,1)} %collective-permute-done.2.refs_3_), channel_id=1, source_target_pairs={{0,1},{1,0},{2,3},{3,2},{4,5},{5,4},{6,7},{7,6},{8,9},{9,8},{10,11... | collective-permute-start | bytes 1966088 | tf_op jit(solution)/shard_map/ppermute | solution.py:35
  119.8 18.1 %collective-permute-start.15 = (bf16[512,256]{1,0:T(8,128)(2,1)S(1)}, bf16[512,256]{1,0:T(8,128)(2,1)S(1)}, u32[]{:S(2)}, u32[]{:S(2)}) collective-permute-start(bf16[512,256]{1,0:T(8,128)(2,1)S(1)} %layer_two.1.own_ref), channel_id=1, source_target_pairs={{0,32},{16,48},{32,0},{48,16},{64,96},{80,112},{96,64},{112,80},{1... | collective-permute-start | bytes 786440 | tf_op jit(solution)/shard_map/ppermute | solution.py:35
  122.8 17.6 %collective-permute-start.16 = (bf16[512,256]{1,0:T(8,128)(2,1)S(1)}, bf16[512,256]{1,0:T(8,128)(2,1)S(1)}, u32[]{:S(2)}, u32[]{:S(2)}) collective-permute-start(bf16[512,256]{1,0:T(8,128)(2,1)S(1)} %layer_two.1.own_ref), channel_id=1, source_target_pairs={{0,8},{8,0},{1,9},{9,1},{2,10},{10,2},{3,11},{11,3},{4,12},{12,4},... | collective-permute-start | bytes 786440 | tf_op jit(solution)/shard_map/ppermute | solution.py:35
  128.9 13.1 %collective-permute-start.17 = (bf16[512,256]{1,0:T(8,128)(2,1)S(1)}, bf16[512,256]{1,0:T(8,128)(2,1)S(1)}, u32[]{:S(2)}, u32[]{:S(2)}) collective-permute-start(bf16[512,256]{1,0:T(8,128)(2,1)S(1)} %layer_two.1.own_ref), channel_id=1, source_target_pairs={{0,16},{16,0},{32,48},{48,32},{64,80},{80,64},{96,112},{112,96},{1... | collective-permute-start | bytes 786440 | tf_op jit(solution)/shard_map/ppermute | solution.py:35
Sparse Core Ops, SparseCore 0:
  34.6 74.5 all-gather.3
